TPU v7x, 256 devices: a whole 4x4x8 slice. The times are simulated.
256 devices in a mesh: region: 8 (over x, core), dev: 32 (over z, y).
Axes of the slice: x: 4, y: 4, z: 8, core: 2. Of those that a mesh axis runs over, the one named last changes fastest.
Arguments:
- synthetic: bfloat16 [4096, 3, 4096], P(('region', 'dev')), may hold values from -6 to 6
- observed: bfloat16 [4096, 3, 4096], P(('region', 'dev')), may hold values from -6 to 6
- nearby_receiver_slots: int32 [8192, 4], P(('region', 'dev')), may hold values from 0 to 15
- far_rows: int32 [8192, 4], P(('region', 'dev')), may hold values from 0 to 15
- first_slot: int32 [65536], P(('region', 'dev')), may hold values from 0 to 127
- second_slot: int32 [65536], P(('region', 'dev')), may hold values from 0 to 255
- window_start: int32 [65536], P(('region', 'dev')), may hold values from 0 to 255
- pair_delay_indices: int32 [65536], P(('region', 'dev')), may hold values from 64 to 256
Outputs:
- adjoint: bfloat16 [4096, 3, 4096], P(('region', 'dev'))
- misfit: float32 [65536], P(('region', 'dev'))
All inputs are finite; a program needn't handle non-finite values.
Results may differ from a plain program's by a relative error of at most 0.0084.
Values may be sent and summed in bfloat16 or wider, within the bound.
No kernel may reach another device: no remote copies, remote signals or barrier semaphores. Data moves between devices by JAX's collectives and lax.ppermute only.
A program may use at most 128 MiB of HBM per device.

v0:
```python
import math

import jax
import jax.numpy as jnp
from jax import lax
from jax.sharding import PartitionSpec as P

F = 512
FLOW = 64
LAGS = 512


def from_behind(value, axis, steps):
    count = lax.axis_size(axis)
    first, last = (max(0, -steps), min(count, count - steps))
    return lax.ppermute(value, axis, [(source, source + steps) for source in range(first, last)])


def make_tables(discrete_ticks):
    clock_moments = jnp.arange(discrete_ticks, dtype=jnp.int32)
    angular_rate = FLOW + jnp.arange(F, dtype=jnp.int32)
    oscillation_arguments = clock_moments[:, None] * angular_rate[None, :] % discrete_ticks
    angles = oscillation_arguments.astype(jnp.float32) * (2.0 * math.pi / discrete_ticks)
    forward = (
        jnp.concatenate([jnp.cos(angles), -jnp.sin(angles)], 1) / math.sqrt(discrete_ticks)
    ).astype(jnp.bfloat16)
    shifts = jnp.arange(LAGS, dtype=jnp.int32) - LAGS // 2
    turning = angular_rate[:, None] * shifts[None, :] % discrete_ticks
    delay_rotation_matrix = turning.astype(jnp.float32) * (2.0 * math.pi / discrete_ticks)
    lag_lookup_table = (
        jnp.concatenate([jnp.cos(delay_rotation_matrix), -jnp.sin(delay_rotation_matrix)], 0)
        / math.sqrt(F)
    ).astype(jnp.bfloat16)
    return (forward, lag_lookup_table)


def cross_power_spectrum(left, right):
    left_re, left_im = (left[..., :F], left[..., F:])
    right_re, right_im = (right[..., :F], right[..., F:])
    return jnp.concatenate(
        [left_re * right_re + left_im * right_im, left_im * right_re - left_re * right_im], -1
    )


def pair_terms(first, second, starts, lengths, lag_lookup_table):
    first = first.astype(jnp.float32)
    second = second.astype(jnp.float32)
    change = (
        cross_power_spectrum(first[:, 0], second[:, 0])
        - cross_power_spectrum(first[:, 1], second[:, 1])
    ).astype(jnp.bfloat16)
    count = change.shape[0]
    shifted = jnp.dot(
        change.reshape(count * 3, 2 * F), lag_lookup_table, preferred_element_type=jnp.float32
    ).reshape(count, 3, LAGS)
    position = jnp.arange(LAGS, dtype=jnp.int32)
    inside = (position[None, :] >= starts[:, None]) & (
        position[None, :] < (starts + lengths)[:, None]
    )
    residual = jnp.where(inside[:, None, :], shifted, 0.0)
    misfit = jnp.sum(residual * residual, axis=(1, 2)) / (2.0 * LAGS)
    slope = lax.dot_general(
        residual.astype(jnp.bfloat16).reshape(count * 3, LAGS),
        lag_lookup_table,
        (((1,), (1,)), ((), ())),
        preferred_element_type=jnp.float32,
    ).reshape(count, 3, 2 * F)
    slope_re, slope_im = (slope[..., :F], slope[..., F:])
    first_re, first_im = (first[:, 0, :, :F], first[:, 0, :, F:])
    second_re, second_im = (second[:, 0, :, :F], second[:, 0, :, F:])
    grad_first = jnp.concatenate(
        [slope_re * second_re - slope_im * second_im, slope_re * second_im + slope_im * second_re],
        -1,
    )
    grad_second = jnp.concatenate(
        [slope_re * first_re + slope_im * first_im, slope_re * first_im - slope_im * first_re], -1
    )
    return (misfit, grad_first, grad_second)


def on_device(
    synthetic,
    observed,
    nearby_receiver_slots,
    far_rows,
    first_slot,
    second_slot,
    window_start,
    pair_delay_indices,
):
    local_count = synthetic.shape[0]
    discrete_ticks = synthetic.shape[2]
    peers = nearby_receiver_slots.shape[0]
    capacity = nearby_receiver_slots.shape[1]
    forward, lag_lookup_table = make_tables(discrete_ticks)
    stacked = jnp.stack([synthetic, observed], 1).reshape(local_count * 6, discrete_ticks)
    spectra = (
        jnp.dot(stacked, forward, preferred_element_type=jnp.float32)
        .astype(jnp.bfloat16)
        .reshape(local_count, 2, 3, 2 * F)
    )
    near_out = spectra[nearby_receiver_slots]
    far_index = from_behind(far_rows, "region", 1)
    far_out = spectra[far_index]
    received = lax.all_to_all(
        jnp.stack([near_out, far_out]), "dev", split_axis=1, concat_axis=1, tiled=True
    )
    fetched = jnp.stack([received[0], from_behind(received[1], "region", -1)])
    slot_count = 2 * peers * capacity
    slot_spectra = fetched.reshape(slot_count, 2, 3, 2 * F)
    misfit, grad_first, grad_second = pair_terms(
        slot_spectra[first_slot],
        slot_spectra[second_slot],
        window_start,
        pair_delay_indices,
        lag_lookup_table,
    )
    slot_grad = jax.ops.segment_sum(
        jnp.concatenate([grad_first, grad_second], 0),
        jnp.concatenate([first_slot, second_slot], 0),
        num_segments=slot_count,
    ).reshape(2, peers, capacity, 3, 2 * F)
    outgoing = jnp.stack([slot_grad[0], from_behind(slot_grad[1], "region", 1)])
    returned = lax.all_to_all(outgoing, "dev", split_axis=1, concat_axis=1, tiled=True)
    own_grad = jax.ops.segment_sum(
        returned[0].reshape(peers * capacity, 3, 2 * F),
        nearby_receiver_slots.reshape(-1),
        num_segments=local_count,
    )
    far_grad = jax.ops.segment_sum(
        returned[1].reshape(peers * capacity, 3, 2 * F),
        far_index.reshape(-1),
        num_segments=local_count,
    )
    own_grad = own_grad + far_grad
    adjoint = lax.dot_general(
        own_grad.astype(jnp.bfloat16).reshape(local_count * 3, 2 * F),
        forward,
        (((1,), (1,)), ((), ())),
        preferred_element_type=jnp.float32,
    )
    return (adjoint.astype(jnp.bfloat16).reshape(local_count, 3, discrete_ticks), misfit)


def solution(mesh):
    placed = (
        P(("region", "dev"), None, None),
        P(("region", "dev"), None, None),
        P(("region", "dev"), None),
        P(("region", "dev"), None),
        P(("region", "dev")),
        P(("region", "dev")),
        P(("region", "dev")),
        P(("region", "dev")),
    )
    return jax.shard_map(
        on_device,
        mesh=mesh,
        in_specs=placed,
        out_specs=(P(("region", "dev"), None, None), P(("region", "dev"))),
        check_vma=False,
    )
```

profile of v0, /device:TPU:20, one launch (start us, length us, event | category | flops | bytes accessed | tf_op | source)
XLA Modules:
  0.0 449.8 jit_solution(633323513305541462)
XLA Ops:
  0.6 1.9 collective-permute-start
  2.6 34.6 %fusion.7 = (f32[4096,512]{1,0:T(8,128)}, f32[4096,512]{1,0:T(8,128)}) fusion(s32[512]{0:T(512)S(1)} %get-tuple-element.39), kind=kLoop, calls=%fused_computation.21 | loop fusion | flops 31457280 | bytes 16779264 | tf_op jit(solution)/shard_map/cos | solution.py:25
  38.0 0.7 reshape.89
  38.9 6.9 %convolution_convert_fusion.1 = bf16[96,1024]{1,0:T(8,128)(2,1)S(1)} fusion(bf16[96,4096]{1,0:T(8,128)(2,1)S(1)} %reshape.89, f32[4096,512]{1,0:T(8,128)} %get-tuple-element.35, f32[4096,512]{1,0:T(8,128)} %get-tuple-element.34), kind=kOutput, calls=%fused_computation.57 | convolution fusion | flops 817987584 | bytes 17760256 | tf_op jit(solution)/shard_map/dot_general | solution.py:98
  46.0 2.3 gather_fusion
  48.3 2.7 copy.62
  51.2 2.3 gather_fusion.1
  53.6 1.5 copy.63
  55.1 4.3 pad_maximum_fusion
  59.3 86.5 %all_to_all.10 = bf16[2,32,4,2,3,1024]{5,3,4,2,0,1:T(2,128)(2,1)S(1)} all-to-all(bf16[2,32,4,2,3,1024]{5,3,4,2,0,1:T(2,128)(2,1)S(1)} %pad_maximum_fusion), channel_id=1, replica_groups=mesh['region'=8,'dev'=32] {'dev'}, dimensions={1} | all-to-all | bytes 6291456 | tf_op jit(solution)/shard_map/all_to_all | solution.py:105
  145.8 2.5 slice_bitcast_fusion.9
  148.3 1.9 collective-permute-start.1
  150.5 5.9 %fusion.19 = (f32[512,512]{1,0:T(8,128)}, f32[512,512]{1,0:T(8,128)}) fusion(s32[512]{0:T(512)S(1)} %get-tuple-element.38, s32[512]{0:T(512)S(1)} %get-tuple-element.39), kind=kLoop, calls=%fused_computation.67 | loop fusion | flops 3932160 | bytes 2101248 | tf_op jit(solution)/shard_map/cos | solution.py:31
  156.4 11.7 %collective-permute-done.1 = bf16[32,4,2,3,1024]{4,2,3,1,0:T(2,128)(2,1)S(1)} collective-permute-done((bf16[32,4,2,3,1024]{4,2,3,1,0:T(2,128)(2,1)S(1)}, bf16[32,4,2,3,1024]{4,2,3,1,0:T(2,128)(2,1)S(1)}, u32[]{:S(2)}, u32[]{:S(2)}) %collective-permute-start.1) | collective-permute-done | bytes 1572896 | tf_op jit(solution)/shard_map/ppermute | solution.py:16
  168.1 4.4 pad_maximum_fusion.1
  172.6 13.0 %gather_fusion.2 = bf16[256,2,3,1024]{3,1,2,0:T(2,128)(2,1)} fusion(bf16[256,2,3,1024]{3,1,2,0:T(2,128)(2,1)S(1)} %bitcast.55, s32[1024]{0:T(1024)S(1)} %pad_clamp_fusion.1), kind=kCustom, calls=%fused_computation.2 | custom fusion | bytes 6292480 | tf_op jit(solution)/shard_map/gather | solution.py:112
  185.6 3.0 copy_convert_fusion.1
  188.6 2.6 copy-done
  191.3 3.2 slice_bitcast_fusion.1
  194.4 13.2 %gather_fusion.3 = bf16[256,2,3,1024]{3,1,2,0:T(2,128)(2,1)} fusion(bf16[256,2,3,1024]{3,1,2,0:T(2,128)(2,1)S(1)} %bitcast.56, s32[1024]{0:T(1024)S(1)} %pad_clamp_fusion), kind=kCustom, calls=%fused_computation.3 | custom fusion | bytes 6292480 | tf_op jit(solution)/shard_map/gather | solution.py:113
  207.6 3.0 copy_convert_fusion
  210.7 0.8 slice_bitcast_fusion
  211.5 1.0 copy-done.2
  212.5 0.8 multiply_add_fusion.2
  213.3 1.1 copy-done.1
  214.4 0.8 multiply_add_fusion.3
  216.0 1.2 multiply_reduce_fusion
  217.1 1.0 fusion.16
  218.2 2.8 multiply_subtract_fusion.1
  221.0 2.8 maximum_maximum_fusion
  223.8 7.6 %copy.67 = f32[512,3,1024]{2,1,0:T(4,128)} copy(f32[512,3,1024]{2,0,1:T(8,128)S(1)} %maximum_maximum_fusion) | data formatting | bytes 12582912 | tf_op jit(solution)/shard_map/concatenate | solution.py:119
  231.4 3.2 broadcast_in_dim.39
  234.6 73.0 %scatter_fusion = f32[256,3,1024]{2,1,0:T(4,128)} fusion(f32[256,3,1024]{2,1,0:T(4,128)} %broadcast_in_dim.39, s32[512]{0:T(512)S(1)} %pad_add_fusion, f32[512,3,1024]{2,1,0:T(4,128)} %copy.67), kind=kCustom, calls=%fused_computation.4 | custom fusion | flops 1572864 | bytes 18876416 | tf_op jit(solution)/shard_map/scatter-add | solution.py:118
  307.7 3.2 fusion.34
  310.9 0.9 copy.68
  311.8 3.9 collective-permute-start.2
  315.7 0.9 copy.69
  316.6 17.0 %collective-permute-done.2 = f32[32,4,3,1024]{3,0,2,1:T(8,128)S(1)} collective-permute-done((f32[32,4,3,1024]{3,0,2,1:T(8,128)S(1)}, f32[32,4,3,1024]{3,0,2,1:T(8,128)S(1)}, u32[]{:S(2)}, u32[]{:S(2)}) %collective-permute-start.2) | collective-permute-done | bytes 1572896 | tf_op jit(solution)/shard_map/ppermute | solution.py:16
  333.9 3.7 copy.70
  337.6 5.6 %all-to-all-start.1 = ((f32[2,32,4,3,1024]{4,2,3,0,1:T(4,128)}), f32[2,32,4,3,1024]{4,2,3,0,1:T(4,128)S(1)}, u32[]{:S(2)}, u32[]{:S(2)}) async-start(f32[2,32,4,3,1024]{4,2,3,0,1:T(4,128)} %copy.70), calls=%async_computation.1 | async-start | bytes 6291456 | tf_op jit(solution)/shard_map/all_to_all | solution.py:124
  344.1 71.2 %all-to-all-done.1 = f32[2,32,4,3,1024]{4,2,3,0,1:T(4,128)S(1)} async-done(((f32[2,32,4,3,1024]{4,2,3,0,1:T(4,128)}), f32[2,32,4,3,1024]{4,2,3,0,1:T(4,128)S(1)}, u32[]{:S(2)}, u32[]{:S(2)}) %all-to-all-start.1) | async-done | bytes 3145760 | tf_op jit(solution)/shard_map/all_to_all | solution.py:124
  415.3 0.7 fusion.35
  416.0 2.6 copy.78
  418.6 1.3 copy.77
  419.9 12.9 %scatter_fusion.2 = f32[16,3,1024]{2,1,0:T(4,128)S(1)} fusion(f32[16,3,1024]{2,1,0:T(4,128)S(1)} %broadcast.63.clone.1, s32[128]{0:T(128)S(1)} %reshape.144, f32[128,3,1024]{2,1,0:T(4,128)} %bitcast.60), kind=kCustom, calls=%fused_computation.6 | custom fusion | flops 393216 | bytes 4719104 | tf_op jit(solution)/shard_map/scatter-add | solution.py:130
  433.0 6.7 %scatter_fusion.1 = f32[16,3,1024]{2,1,0:T(4,128)S(1)} fusion(f32[16,3,1024]{2,1,0:T(4,128)S(1)} %broadcast.63.clone, s32[128]{0:T(128)S(1)} %reshape.136, f32[128,3,1024]{2,1,0:T(4,128)S(1)} %bitcast.59), kind=kCustom, calls=%fused_computation.5 | custom fusion | flops 393216 | bytes 4719104 | tf_op jit(solution)/shard_map/scatter-add | solution.py:125
  439.8 8.4 %convolution_convert_fusion = bf16[48,4096]{1,0:T(8,128)(2,1)S(1)} fusion(bf16[48,1024]{1,0:T(8,128)(2,1)S(1)} %reshape.92, f32[4096,512]{1,0:T(8,128)} %get-tuple-element.35, f32[4096,512]{1,0:T(8,128)} %get-tuple-element.34), kind=kOutput, calls=%fused_computation.20 | convolution fusion | flops 415432704 | bytes 17268736 | tf_op jit(solution)/shard_map/dot_general | solution.py:136
  448.5 1.0 copy.76
  (59 shorter events, 4.0 us)
Async XLA Ops:
  0.6 50.4 %collective-permute-start = (s32[32,4]{0,1:T(4,128)}, s32[32,4]{0,1:T(4,128)S(1)}, u32[]{:S(2)}, u32[]{:S(2)}) collective-permute-start(s32[32,4]{0,1:T(4,128)} %param.11), channel_id=1, source_target_pairs={{0,32},{32,64},{64,96},{96,128},{128,160},{160,192},{192,224},{1,3... | collective-permute-start | bytes 1544 | tf_op jit(solution)/shard_map/ppermute | solution.py:16
  2.6 34.7 %copy-start.6 = (bf16[16,3,4096]{2,0,1:T(8,128)(2,1)S(1)}, bf16[16,3,4096]{2,0,1:T(8,128)(2,1)}, u32[]{:S(2)}) copy-start(bf16[16,3,4096]{2,0,1:T(8,128)(2,1)} %param.9) | copy-start | bytes 1179652
  2.6 34.7 %copy-start.7 = (bf16[16,3,4096]{2,0,1:T(8,128)(2,1)S(1)}, bf16[16,3,4096]{2,0,1:T(8,128)(2,1)}, u32[]{:S(2)}) copy-start(bf16[16,3,4096]{2,0,1:T(8,128)(2,1)} %param.8) | copy-start | bytes 1179652
  37.2 1.5 copy-start.8
  53.6 1.5 copy-start.3
  145.8 4.4 copy-start.9
  145.8 4.4 copy-start.12
  145.8 4.4 copy-start.10
  145.8 4.5 copy-start.11
  148.3 19.8 %collective-permute-start.1 = (bf16[32,4,2,3,1024]{4,2,3,1,0:T(2,128)(2,1)S(1)}, bf16[32,4,2,3,1024]{4,2,3,1,0:T(2,128)(2,1)S(1)}, u32[]{:S(2)}, u32[]{:S(2)}) collective-permute-start(bf16[32,4,2,3,1024]{4,2,3,1,0:T(2,128)(2,1)S(1)} %get-tuple-element.31), channel_id=1, source_target_pairs={{32,0},{64,32},{96,64},{128,96},{160,128},{192,160},{224,192},{33,... | collective-permute-start | bytes 4718600 | tf_op jit(solution)/shard_map/ppermute | solution.py:16
  188.6 2.7 copy-start
  210.7 1.9 copy-start.2
  212.5 1.9 copy-start.1
  214.4 1.2 copy-start.4
  214.4 1.5 copy-start.5
  214.4 3.7 slice-start
  216.0 2.2 slice-start.1
  311.8 21.9 %collective-permute-start.2 = (f32[32,4,3,1024]{3,0,2,1:T(8,128)S(1)}, f32[32,4,3,1024]{3,0,2,1:T(8,128)S(1)}, u32[]{:S(2)}, u32[]{:S(2)}) collective-permute-start(f32[32,4,3,1024]{3,0,2,1:T(8,128)S(1)} %copy.68), channel_id=1, source_target_pairs={{0,32},{32,64},{64,96},{96,128},{128,160},{160,192},{192,224},{1,3... | collective-permute-start | bytes 4718600 | tf_op jit(solution)/shard_map/ppermute | solution.py:16
  337.6 77.8 %all-to-all-start.1 = ((f32[2,32,4,3,1024]{4,2,3,0,1:T(4,128)}), f32[2,32,4,3,1024]{4,2,3,0,1:T(4,128)S(1)}, u32[]{:S(2)}, u32[]{:S(2)}) async-start(f32[2,32,4,3,1024]{4,2,3,0,1:T(4,128)} %copy.70), calls=%async_computation.1 | async-start | bytes 6291456 | tf_op jit(solution)/shard_map/all_to_all | solution.py:124
where the time goes:
time: 455 us; the launch traced here: 450 us
  other arithmetic  156 us (34%)
  waiting for transfers between devices  100 us (22%)
  blocking collectives  86.5 us (19%)
  local copies, waits for them, and re-layouts  74.9 us (16%)
  matrix products  17.5 us (4%)
  starting transfers between devices  13.3 us (3%)
    all_to_all x1, blocking collectives, on_device(): lax.all_to_all(jnp.stack([near_out, far_out]), 'dev', split_axis=1, conca...  86.5 us
    scatter-add x1, other arithmetic, on_device(): jax.ops.segment_sum(jnp.concatenate([grad_first, grad_second], 0), jnp.co...  73 us
    all_to_all x1, waiting for transfers between devices, on_device(): lax.all_to_all(outgoing, 'dev', split_axis=1, concat_axis=1, tiled=True)  71.2 us
    cos x1, other arithmetic, make_tables(): jnp.cos(angles)  34.6 us
    ppermute x3, waiting for transfers between devices, from_behind(): lax.ppermute(value, axis, [(source, source + steps) for source in range(f...  28.8 us
    gather x1, local copies, waits for them, and re-layouts, on_device(): slot_spectra[second_slot]  13.2 us
    gather x1, local copies, waits for them, and re-layouts, on_device(): slot_spectra[first_slot]  13 us
    scatter-add x1, other arithmetic, on_device(): jax.ops.segment_sum(returned[1].reshape(peers * capacity, 3, 2 * F), far_...  12.9 us
  transfers between devices with their start and end apart: 4, of which 3 were waited for; matrix products, arithmetic and copies ran while one was open for 13% of the time, Pallas kernels for 0%

commit v1 on v0

v1 whole, which is shorter than its diff:
```python
import functools
import math

import jax
import jax.numpy as jnp
import ml_dtypes
import numpy as np
from jax import lax
from jax.experimental import pallas as pl
from jax.experimental.pallas import tpu as pltpu
from jax.sharding import PartitionSpec as P

F = 512
FLOW = 64
LAGS = 512
ZS = 8
YS = 4
CAP = 4
ROWS = 16
Q = 6
VMEM_BYTES = 40 * 1024 * 1024
BF = jnp.bfloat16
F32 = jnp.float32


def tables(ticks):
    rate = FLOW + np.arange(F, dtype=np.int64)
    turn = (np.arange(ticks, dtype=np.int64)[:, None] * rate[None, :]) % ticks
    angle = (turn.astype(np.float32) * np.float32(2.0 * math.pi / ticks)).astype(np.float64)
    forward = np.concatenate([np.cos(angle), -np.sin(angle)], 1).astype(np.float32)
    forward = (forward / np.float32(math.sqrt(ticks))).astype(ml_dtypes.bfloat16)
    shifts = np.arange(LAGS, dtype=np.int64) - LAGS // 2
    turn = (rate[:, None] * shifts[None, :]) % ticks
    angle = (turn.astype(np.float32) * np.float32(2.0 * math.pi / ticks)).astype(np.float64)
    lag = np.concatenate([np.cos(angle), -np.sin(angle)], 0).astype(np.float32)
    lag = (lag / np.float32(math.sqrt(F))).astype(ml_dtypes.bfloat16)
    return forward, lag


def z_pairs(step):
    return [(z * YS + y, (z + step) % ZS * YS + y) for z in range(ZS) for y in range(YS)]


def y_pairs(step, regions, shift):
    devs = ZS * YS
    return [
        (r * devs + z * YS + y, (r + shift) * devs + z * YS + (y + step) % YS)
        for r in range(max(0, -shift), min(regions, regions - shift))
        for z in range(ZS)
        for y in range(YS)
    ]


def iota(shape, axis):
    return lax.broadcasted_iota(jnp.int32, shape, axis)


def dot(a, b):
    return jnp.dot(a, b, preferred_element_type=F32)


def ring_place(offset):
    offset = lax.rem(offset + 2 * ZS, ZS)
    return jnp.where(offset == 0, 0, jnp.where(offset <= ZS // 2, 2 * offset - 1, 2 * (ZS - offset)))


def select_kernel(place_ref, *refs):
    blocks = refs[: ZS - 1]
    halves = refs[ZS - 1 : ZS + 1]
    near = refs[ZS + 1 : ZS + 1 + YS]
    far = refs[ZS + 1 + YS : ZS + 1 + 2 * YS]
    pick_out = refs[ZS + 1 + 2 * YS]
    z, y = place_ref[0], place_ref[1]
    split = halves[0].shape[0]

    def stacked(q):
        last = halves[0][q] if q < split else halves[1][q - split]
        return jnp.concatenate([block[q] for block in blocks] + [last], 0)

    total = 2 * YS * ZS * CAP
    wide = ZS * ROWS
    row = iota((total, 1), 0)
    cap, ring, step, side = row % CAP, row // CAP % ZS, row // (CAP * ZS) % YS, row // (CAP * ZS * YS)
    expand = (iota((total, wide), 1) == ring * ROWS).astype(BF)
    index = stacked(Q)[:, :total]
    spread = dot(expand, index)
    lane = side * (total // 2) + z * (YS * CAP) + (y + step) % YS * CAP + cap
    chosen = jnp.sum(jnp.where(iota((total, total), 1) == lane, spread, 0.0), 1, keepdims=True)
    target = ring * ROWS + chosen.astype(jnp.int32)
    pick = (iota((total, wide), 1) == target).astype(F32)
    pick_out[...] = pick.T.astype(BF)
    pick = pick.astype(BF)
    count = ZS * CAP
    for q in range(Q):
        got = dot(pick, stacked(q)).astype(BF)
        for k in range(YS):
            near[k][q // 3, q % 3] = got[k * count : (k + 1) * count]
            far[k][q // 3, q % 3] = got[(YS + k) * count : (YS + k + 1) * count]


def pair_kernel(column_ref, row_ref, lag_ref, *refs):
    slots = refs[: 2 * YS]
    misfit_ref = refs[2 * YS]
    outs = refs[2 * YS + 1 :]
    pairs = column_ref.shape[0]
    count = ZS * CAP
    near = YS * count
    lag = lag_ref[...]
    first = (iota((pairs, near), 1) == column_ref[:, 0:1]).astype(BF)
    second = (iota((pairs, 2 * near), 1) == column_ref[:, 1:2]).astype(BF)
    first_back = (iota((near, pairs), 0) == row_ref[0:1, :]).astype(BF)
    second_back = (iota((2 * near, pairs), 0) == row_ref[1:2, :]).astype(BF)

    def both(kind):
        spectra = jnp.concatenate([slot[kind, 0] for slot in slots], 0)
        a = dot(first, spectra[:near])
        b = dot(second, spectra)
        return a[:, :F], a[:, F:], b[:, :F], b[:, F:]

    ar, ai, br, bi = both(0)
    cr, ci, dr, di = both(1)
    real = (ar * br + ai * bi) - (cr * dr + ci * di)
    imag = (ai * br - ar * bi) - (ci * dr - cr * di)
    shifted = dot(real.astype(BF), lag[:F]) + dot(imag.astype(BF), lag[F:])
    position = iota((pairs, LAGS), 1)
    start = column_ref[:, 2:3]
    inside = (position >= start) & (position < start + column_ref[:, 3:4])
    residual = jnp.where(inside, shifted, 0.0)
    part = jnp.sum(residual * residual, axis=1, keepdims=True)

    @pl.when(pl.program_id(0) == 0)
    def _():
        misfit_ref[...] = jnp.zeros_like(misfit_ref)

    misfit_ref[...] += part * (1.0 / (2.0 * LAGS))
    slope = lax.dot_general(
        residual.astype(BF), lag, (((1,), (1,)), ((), ())), preferred_element_type=F32
    )
    gr, gi = slope[:, :F], slope[:, F:]
    grad_first = jnp.concatenate([gr * br - gi * bi, gr * bi + gi * br], 1).astype(BF)
    grad_second = jnp.concatenate([gr * ar + gi * ai, gr * ai - gi * ar], 1).astype(BF)
    total = dot(second_back, grad_second)
    top = total[:near] + dot(first_back, grad_first)
    for k in range(YS):
        outs[k][0] = top[k * count : (k + 1) * count].astype(BF)
        outs[YS + k][0] = total[near + k * count : near + (k + 1) * count].astype(BF)


def collect_kernel(place_ref, pick_ref, *refs):
    grads = refs[: 2 * YS]
    out = refs[2 * YS]
    z = place_ref[0]
    pick = pick_ref[...]
    for c in range(3):
        total = dot(pick, jnp.concatenate([grad[c] for grad in grads], 0)).astype(BF)
        for p in range(ZS):
            offset = (p + 1) // 2 if p % 2 else -(p // 2)
            out[lax.rem(z - offset + ZS, ZS), c] = total[p * ROWS : (p + 1) * ROWS]


def whole(count):
    return [pl.BlockSpec(memory_space=pltpu.VMEM)] * count


def on_device(
    regions,
    synthetic,
    observed,
    nearby_receiver_slots,
    far_rows,
    first_slot,
    second_slot,
    window_start,
    pair_delay_indices,
):
    ticks = synthetic.shape[2]
    pairs = first_slot.shape[0]
    forward_np, lag_np = tables(ticks)
    forward, lag = jnp.asarray(forward_np), jnp.asarray(lag_np)
    params = pltpu.CompilerParams(vmem_limit_bytes=VMEM_BYTES)
    scalars = pl.BlockSpec(memory_space=pltpu.SMEM)
    here = lax.axis_index("dev")
    z, y = here // YS, here % YS
    place = jnp.stack([z, y]).astype(jnp.int32)
    count = ZS * CAP

    far_index = lax.ppermute(far_rows, "region", [(r, r + 1) for r in range(regions - 1)])
    traces = jnp.stack([synthetic, observed]).transpose(0, 2, 1, 3).reshape(Q * ROWS, ticks)
    spectra = jnp.dot(traces, forward, preferred_element_type=F32).astype(BF).reshape(Q, ROWS, 2 * F)
    index = jnp.concatenate([nearby_receiver_slots.reshape(-1), far_index.reshape(-1)]).astype(BF)
    index = jnp.pad(index.reshape(1, 1, -1), ((0, 0), (0, ROWS - 1), (0, 2 * F - index.shape[0])))
    own = jnp.concatenate([spectra, index], 0)

    up = down = own
    blocks = [own]
    for _ in range(ZS // 2 - 1):
        up = lax.ppermute(up, "dev", z_pairs(1))
        down = lax.ppermute(down, "dev", z_pairs(-1))
        blocks += [up, down]
    split = (Q + 1) // 2
    halves = [
        lax.ppermute(up[:split], "dev", z_pairs(1)),
        lax.ppermute(down[split:], "dev", z_pairs(-1)),
    ]
    picked = pl.pallas_call(
        select_kernel,
        out_shape=[jax.ShapeDtypeStruct((2, 3, count, 2 * F), BF)] * (2 * YS)
        + [jax.ShapeDtypeStruct((ZS * ROWS, 2 * YS * count), BF)],
        in_specs=[scalars] + whole(ZS + 1),
        out_specs=whole(2 * YS + 1),
        compiler_params=params,
    )(place, *blocks, *halves)
    pick = picked[-1]
    slots = [picked[0]]
    slots += [
        lax.ppermute(picked[k], ("region", "dev"), y_pairs(k, regions, 0)) for k in range(1, YS)
    ]
    slots += [
        lax.ppermute(picked[YS + k], ("region", "dev"), y_pairs(k, regions, -1)) for k in range(YS)
    ]

    def moved(slot):
        side, member, cap = slot // (ZS * YS * CAP), slot // CAP % (ZS * YS), slot % CAP
        step = lax.rem(y - member % YS + YS, YS)
        ring = ring_place(z - member // YS)
        return ((side * YS + step) * ZS + ring) * CAP + cap

    first, second = moved(first_slot), moved(second_slot)
    column = jnp.stack([first, second, window_start, pair_delay_indices], 1)
    row = jnp.stack([first, second])
    results = pl.pallas_call(
        pair_kernel,
        grid=(3,),
        out_shape=[jax.ShapeDtypeStruct((pairs, 1), F32)]
        + [jax.ShapeDtypeStruct((3, count, 2 * F), BF)] * (2 * YS),
        in_specs=[
            pl.BlockSpec((pairs, 4), lambda c: (0, 0)),
            pl.BlockSpec((2, pairs), lambda c: (0, 0)),
            pl.BlockSpec((2 * F, LAGS), lambda c: (0, 0)),
        ]
        + [pl.BlockSpec((2, 1, count, 2 * F), lambda c: (0, c, 0, 0))] * (2 * YS),
        out_specs=[pl.BlockSpec((pairs, 1), lambda c: (0, 0))]
        + [pl.BlockSpec((1, count, 2 * F), lambda c: (c, 0, 0))] * (2 * YS),
        compiler_params=params,
    )(column, row, lag, *slots)
    misfit, grads = results[0].reshape(pairs), results[1:]
    back = [grads[0]]
    back += [
        lax.ppermute(grads[k], ("region", "dev"), y_pairs(-k, regions, 0)) for k in range(1, YS)
    ]
    back += [
        lax.ppermute(grads[YS + k], ("region", "dev"), y_pairs(-k, regions, 1)) for k in range(YS)
    ]
    sums = pl.pallas_call(
        collect_kernel,
        out_shape=jax.ShapeDtypeStruct((ZS, 3, ROWS, 2 * F), BF),
        in_specs=[scalars] + whole(2 * YS + 1),
        out_specs=pl.BlockSpec(memory_space=pltpu.VMEM),
        compiler_params=params,
    )(place, pick, *back)
    groups = [[z * YS + y for z in range(ZS)] for y in range(YS)]
    parts = lax.all_to_all(
        sums, "dev", split_axis=0, concat_axis=0, tiled=True, axis_index_groups=groups
    )
    total = jnp.sum(parts.astype(F32), 0).astype(BF).reshape(3 * ROWS, 2 * F)
    adjoint = lax.dot_general(
        total, forward, (((1,), (1,)), ((), ())), preferred_element_type=F32
    )
    adjoint = adjoint.astype(BF).reshape(3, ROWS, ticks).transpose(1, 0, 2)
    return (adjoint, misfit)


def solution(mesh):
    both = ("region", "dev")
    placed = (P(both, None, None),) * 2 + (P(both, None),) * 2 + (P(both),) * 4
    return jax.shard_map(
        functools.partial(on_device, mesh.shape["region"]),
        mesh=mesh,
        in_specs=placed,
        out_specs=(P(both, None, None), P(both)),
        check_vma=False,
    )
```

time: 455 us -> 164 us (0.36)
  the two profiles are of different devices: /device:TPU:20 before, /device:TPU:1 now
where the time goes in v1:
time: 164 us; the launch traced here: 162 us
  starting transfers between devices  78.3 us (48%)
  waiting for transfers between devices  54 us (33%)
  Pallas kernels  13.9 us (8%)
  matrix products  11.7 us (7%)
  other arithmetic  2.17 us (1%)
    ppermute x4, starting transfers between devices, on_device(): lax.ppermute(picked[YS + k], ('region', 'dev'), y_pairs(k, regions, -1))  23.8 us
    all_to_all x1, waiting for transfers between devices, on_device(): lax.all_to_all(sums, 'dev', split_axis=0, concat_axis=0, tiled=True, axis...  22.2 us
    ppermute x4, starting transfers between devices, on_device(): lax.ppermute(grads[YS + k], ('region', 'dev'), y_pairs(-k, regions, 1))  18.3 us
    ppermute x3, waiting for transfers between devices, on_device(): down = lax.ppermute(down, 'dev', z_pairs(-1))  13.8 us
    ppermute x3, starting transfers between devices, on_device(): down = lax.ppermute(down, 'dev', z_pairs(-1))  12.2 us
    pallas_call x1, Pallas kernels, on_device(): pl.pallas_call(pair_kernel, grid=(3,), out_shape=[jax.ShapeDtypeStruct((p...  9.11 us
    ppermute x4, waiting for transfers between devices, on_device(): lax.ppermute(picked[YS + k], ('region', 'dev'), y_pairs(k, regions, -1))  8.21 us
    ppermute x3, starting transfers between devices, on_device(): lax.ppermute(grads[k], ('region', 'dev'), y_pairs(-k, regions, 0))  7.4 us
  transfers between devices with their start and end apart: 24, of which 11 were waited for; matrix products, arithmetic and copies ran while one was open for 5% of the time, Pallas kernels for 0%

profile of v1, /device:TPU:1, one launch (start us, length us, event | category | flops | bytes accessed | tf_op | source)
XLA Modules:
  0.0 161.7 jit_solution(6197382314248624454)
XLA Ops:
  0.6 4.5 %collective-permute-start = (s32[32,4]{0,1:T(4,128)}, s32[32,4]{0,1:T(4,128)S(1)}, u32[]{:S(2)}, u32[]{:S(2)}) collective-permute-start(s32[32,4]{0,1:T(4,128)} %param.13), channel_id=1, source_target_pairs={{0,32},{32,64},{64,96},{96,128},{128,160},{160,192},{192,224},{1,3... | collective-permute-start | bytes 1544 | tf_op jit(solution)/shard_map/ppermute | solution.py:187
  5.1 1.2 pad_maximum_fusion
  6.3 0.0 copy-start.1
  6.4 0.0 copy-start.4
  6.4 0.0 copy-start
  6.4 4.9 %convolution_convert_fusion.1 = bf16[96,1024]{1,0:T(8,128)(2,1)S(1)} fusion(bf16[96,4096]{1,0:T(8,128)(2,1)S(1)} %bitcast.22, bf16[4096,1024]{1,0:T(8,128)(2,1)} %constant.144.clone), kind=kOutput, calls=%fused_computation.1 | convolution fusion | flops 805404672 | bytes 9371648 | tf_op jit(solution)/shard_map/dot_general | solution.py:189
  11.4 0.1 copy.20
  11.5 0.1 concatenate.18
  11.6 0.1 copy.21
  11.7 0.1 concatenate.19
  11.9 5.7 %collective-permute-start.2 = (bf16[7,16,1024]{2,1,0:T(8,128)(2,1)S(1)}, bf16[7,16,1024]{2,1,0:T(8,128)(2,1)S(1)}, u32[]{:S(2)}, u32[]{:S(2)}) collective-permute-start(bf16[7,16,1024]{2,1,0:T(8,128)(2,1)S(1)} %pad_maximum_fusion.1.refs_0_), channel_id=1, source_target_pairs={{0,28},{1,29},{2,30},{3,31},{4,0},{5,1},{6,2},{7,3},{8,4},{9,5},{1... | collective-permute-start | bytes 688136 | tf_op jit(solution)/shard_map/ppermute | solution.py:198
  17.5 4.6 %collective-permute-done.2.refs_2_ = bf16[7,16,1024]{2,1,0:T(8,128)(2,1)S(1)} collective-permute-done((bf16[7,16,1024]{2,1,0:T(8,128)(2,1)S(1)}, bf16[7,16,1024]{2,1,0:T(8,128)(2,1)S(1)}, u32[]{:S(2)}, u32[]{:S(2)}) %collective-permute-start.2) | collective-permute-done | bytes 229408 | tf_op jit(solution)/shard_map/ppermute | solution.py:198
  22.2 3.1 %collective-permute-start.4 = (bf16[7,16,1024]{2,1,0:T(8,128)(2,1)S(1)}, bf16[7,16,1024]{2,1,0:T(8,128)(2,1)S(1)}, u32[]{:S(2)}, u32[]{:S(2)}) collective-permute-start(bf16[7,16,1024]{2,1,0:T(8,128)(2,1)S(1)} %collective-permute-done.2.refs_2_), channel_id=1, source_target_pairs={{0,28},{1,29},{2,30},{3,31},{4,0},{5,1},{6,2},{7,3},{8,4},{9,5},{1... | collective-permute-start | bytes 688136 | tf_op jit(solution)/shard_map/ppermute | solution.py:198
  25.3 0.3 collective-permute-done.1.refs_1_
  25.6 4.9 %collective-permute-done.4.refs_4_ = bf16[7,16,1024]{2,1,0:T(8,128)(2,1)S(1)} collective-permute-done((bf16[7,16,1024]{2,1,0:T(8,128)(2,1)S(1)}, bf16[7,16,1024]{2,1,0:T(8,128)(2,1)S(1)}, u32[]{:S(2)}, u32[]{:S(2)}) %collective-permute-start.4) | collective-permute-done | bytes 229408 | tf_op jit(solution)/shard_map/ppermute | solution.py:198
  30.4 3.4 %collective-permute-start.6 = (bf16[7,16,1024]{2,1,0:T(8,128)(2,1)S(1)}, bf16[7,16,1024]{2,1,0:T(8,128)(2,1)S(1)}, u32[]{:S(2)}, u32[]{:S(2)}) collective-permute-start(bf16[7,16,1024]{2,1,0:T(8,128)(2,1)S(1)} %collective-permute-done.4.refs_4_), channel_id=1, source_target_pairs={{0,28},{1,29},{2,30},{3,31},{4,0},{5,1},{6,2},{7,3},{8,4},{9,5},{1... | collective-permute-start | bytes 688136 | tf_op jit(solution)/shard_map/ppermute | solution.py:198
  33.8 4.3 %collective-permute-done.6.refs_6_ = bf16[7,16,1024]{2,1,0:T(8,128)(2,1)S(1)} collective-permute-done((bf16[7,16,1024]{2,1,0:T(8,128)(2,1)S(1)}, bf16[7,16,1024]{2,1,0:T(8,128)(2,1)S(1)}, u32[]{:S(2)}, u32[]{:S(2)}) %collective-permute-start.6) | collective-permute-done | bytes 229408 | tf_op jit(solution)/shard_map/ppermute | solution.py:198
  38.1 3.5 %collective-permute-start.8 = (bf16[4,16,1024]{2,1,0:T(8,128)(2,1)S(1)}, bf16[4,16,1024]{2,1,0:T(8,128)(2,1)S(1)}, u32[]{:S(2)}, u32[]{:S(2)}) collective-permute-start(bf16[4,16,1024]{2,1,0:T(8,128)(2,1)S(1)} %slice.9), channel_id=1, source_target_pairs={{0,28},{1,29},{2,30},{3,31},{4,0},{5,1},{6,2},{7,3},{8,4},{9,5},{1... | collective-permute-start | bytes 393224 | tf_op jit(solution)/shard_map/ppermute | solution.py:203
  41.6 0.1 collective-permute-start.7
  41.7 0.1 pad_add_fusion.2.place_ref
  41.8 4.6 %collective-permute-done.7.refs_7_ = bf16[3,16,1024]{2,1,0:T(8,128)(2,1)S(1)} collective-permute-done((bf16[3,16,1024]{2,1,0:T(8,128)(2,1)S(1)}, bf16[3,16,1024]{2,1,0:T(8,128)(2,1)S(1)}, u32[]{:S(2)}, u32[]{:S(2)}) %collective-permute-start.7) | collective-permute-done | bytes 98336 | tf_op jit(solution)/shard_map/ppermute | solution.py:202
  46.4 3.0 %shard_map.113 = (bf16[2,3,32,1024]{3,2,1,0:T(8,128)(2,1)S(1)}, bf16[2,3,32,1024]{3,2,1,0:T(8,128)(2,1)S(1)}, bf16[2,3,32,1024]{3,2,1,0:T(8,128)(2,1)S(1)}, bf16...) custom-call(s32[2]{0:T(128)S(1)} %pad_add_fusion.2.place_ref, ...), custom_call_target="tpu_custom_call" | custom-call | tf_op jit(solution)/shard_map/pallas_call | solution.py:205
  49.4 1.3 collective-permute-start.9
  50.7 2.6 %collective-permute-start.10 = (bf16[2,3,32,1024]{3,2,1,0:T(8,128)(2,1)S(1)}, bf16[2,3,32,1024]{3,2,1,0:T(8,128)(2,1)S(1)}, u32[]{:S(2)}, u32[]{:S(2)}) collective-permute-start(bf16[2,3,32,1024]{3,2,1,0:T(8,128)(2,1)S(1)} %get-tuple-element.23), channel_id=1, source_target_pairs={{0,2},{1,3},{2,0},{3,1},{4,6},{5,7},{6,4},{7,5},{8,10},{9,11},{10,... | collective-permute-start | bytes 1179656 | tf_op jit(solution)/shard_map/ppermute | solution.py:216
  53.3 1.1 collective-permute-start.11
  54.3 5.7 %collective-permute-start.12 = (bf16[2,3,32,1024]{3,2,1,0:T(8,128)(2,1)}, bf16[2,3,32,1024]{3,2,1,0:T(8,128)(2,1)S(1)}, u32[]{:S(2)}, u32[]{:S(2)}) collective-permute-start(bf16[2,3,32,1024]{3,2,1,0:T(8,128)(2,1)} %get-tuple-element.25), channel_id=1, source_target_pairs={{32,0},{33,1},{34,2},{35,3},{36,4},{37,5},{38,6},{39,7},{40,8},{41... | collective-permute-start | bytes 1179656 | tf_op jit(solution)/shard_map/ppermute | solution.py:219
  60.1 1.9 %collective-permute-start.13 = (bf16[2,3,32,1024]{3,2,1,0:T(8,128)(2,1)}, bf16[2,3,32,1024]{3,2,1,0:T(8,128)(2,1)}, u32[]{:S(2)}, u32[]{:S(2)}) collective-permute-start(bf16[2,3,32,1024]{3,2,1,0:T(8,128)(2,1)} %get-tuple-element.26), channel_id=1, source_target_pairs={{32,1},{33,2},{34,3},{35,0},{36,5},{37,6},{38,7},{39,4},{40,9},{41... | collective-permute-start | bytes 1179656 | tf_op jit(solution)/shard_map/ppermute | solution.py:219
  62.0 14.1 %collective-permute-start.14 = (bf16[2,3,32,1024]{3,2,1,0:T(8,128)(2,1)}, bf16[2,3,32,1024]{3,2,1,0:T(8,128)(2,1)}, u32[]{:S(2)}, u32[]{:S(2)}) collective-permute-start(bf16[2,3,32,1024]{3,2,1,0:T(8,128)(2,1)} %get-tuple-element.27), channel_id=1, source_target_pairs={{32,2},{33,3},{34,0},{35,1},{36,6},{37,7},{38,4},{39,5},{40,10},{4... | collective-permute-start | bytes 1179656 | tf_op jit(solution)/shard_map/ppermute | solution.py:219
  76.1 2.1 %collective-permute-start.15 = (bf16[2,3,32,1024]{3,2,1,0:T(8,128)(2,1)}, bf16[2,3,32,1024]{3,2,1,0:T(8,128)(2,1)}, u32[]{:S(2)}, u32[]{:S(2)}) collective-permute-start(bf16[2,3,32,1024]{3,2,1,0:T(8,128)(2,1)} %get-tuple-element.28), channel_id=1, source_target_pairs={{32,3},{33,0},{34,1},{35,2},{36,7},{37,4},{38,5},{39,6},{40,11},{4... | collective-permute-start | bytes 1179656 | tf_op jit(solution)/shard_map/ppermute | solution.py:219
  78.3 0.1 copy.22.column_ref
  78.5 2.3 %collective-permute-done.13.refs_5_ = bf16[2,3,32,1024]{3,2,1,0:T(8,128)(2,1)} collective-permute-done((bf16[2,3,32,1024]{3,2,1,0:T(8,128)(2,1)}, bf16[2,3,32,1024]{3,2,1,0:T(8,128)(2,1)}, u32[]{:S(2)}, u32[]{:S(2)}) %collective-permute-start.13) | collective-permute-done | bytes 393248 | tf_op jit(solution)/shard_map/ppermute | solution.py:219
  80.8 4.2 %collective-permute-done.14.refs_6_ = bf16[2,3,32,1024]{3,2,1,0:T(8,128)(2,1)} collective-permute-done((bf16[2,3,32,1024]{3,2,1,0:T(8,128)(2,1)}, bf16[2,3,32,1024]{3,2,1,0:T(8,128)(2,1)}, u32[]{:S(2)}, u32[]{:S(2)}) %collective-permute-start.14) | collective-permute-done | bytes 393248 | tf_op jit(solution)/shard_map/ppermute | solution.py:219
  85.0 1.7 %collective-permute-done.15.refs_7_ = bf16[2,3,32,1024]{3,2,1,0:T(8,128)(2,1)} collective-permute-done((bf16[2,3,32,1024]{3,2,1,0:T(8,128)(2,1)}, bf16[2,3,32,1024]{3,2,1,0:T(8,128)(2,1)}, u32[]{:S(2)}, u32[]{:S(2)}) %collective-permute-start.15) | collective-permute-done | bytes 393248 | tf_op jit(solution)/shard_map/ppermute | solution.py:219
  86.7 9.1 %shard_map.114 = (f32[256,1]{1,0:T(8,128)S(1)}, bf16[3,32,1024]{2,1,0:T(8,128)(2,1)S(1)}, bf16[3,32,1024]{2,1,0:T(8,128)(2,1)S(1)}, bf16[3,32,1024]{2,1,0:T(8,12...) custom-call(s32[256,4]{1,0:T(8,128)S(1)} %copy.22.column_ref, ...), custom_call_target="tpu_custom_call" | custom-call | tf_op jit(solution)/shard_map/pallas_call | solution.py:231
  95.9 4.9 %collective-permute-start.16 = (bf16[3,32,1024]{2,1,0:T(8,128)(2,1)S(1)}, bf16[3,32,1024]{2,1,0:T(8,128)(2,1)S(1)}, u32[]{:S(2)}, u32[]{:S(2)}) collective-permute-start(bf16[3,32,1024]{2,1,0:T(8,128)(2,1)S(1)} %get-tuple-element.30), channel_id=1, source_target_pairs={{0,3},{1,0},{2,1},{3,2},{4,7},{5,4},{6,5},{7,6},{8,11},{9,8},{10,9... | collective-permute-start | bytes 589832 | tf_op jit(solution)/shard_map/ppermute | solution.py:249
  100.8 2.5 %collective-permute-start.17 = (bf16[3,32,1024]{2,1,0:T(8,128)(2,1)S(1)}, bf16[3,32,1024]{2,1,0:T(8,128)(2,1)S(1)}, u32[]{:S(2)}, u32[]{:S(2)}) collective-permute-start(bf16[3,32,1024]{2,1,0:T(8,128)(2,1)S(1)} %get-tuple-element.31), channel_id=1, source_target_pairs={{0,2},{1,3},{2,0},{3,1},{4,6},{5,7},{6,4},{7,5},{8,10},{9,11},{10,... | collective-permute-start | bytes 589832 | tf_op jit(solution)/shard_map/ppermute | solution.py:249
  103.3 6.5 %collective-permute-start.19 = (bf16[3,32,1024]{2,1,0:T(8,128)(2,1)S(1)}, bf16[3,32,1024]{2,1,0:T(8,128)(2,1)S(1)}, u32[]{:S(2)}, u32[]{:S(2)}) collective-permute-start(bf16[3,32,1024]{2,1,0:T(8,128)(2,1)S(1)} %get-tuple-element.33), channel_id=1, source_target_pairs={{0,32},{1,33},{2,34},{3,35},{4,36},{5,37},{6,38},{7,39},{8,40},{9,... | collective-permute-start | bytes 589832 | tf_op jit(solution)/shard_map/ppermute | solution.py:252
  109.7 3.6 %collective-permute-start.20 = (bf16[3,32,1024]{2,1,0:T(8,128)(2,1)S(1)}, bf16[3,32,1024]{2,1,0:T(8,128)(2,1)S(1)}, u32[]{:S(2)}, u32[]{:S(2)}) collective-permute-start(bf16[3,32,1024]{2,1,0:T(8,128)(2,1)S(1)} %get-tuple-element.34), channel_id=1, source_target_pairs={{0,35},{1,32},{2,33},{3,34},{4,39},{5,36},{6,37},{7,38},{8,43},{9,... | collective-permute-start | bytes 589832 | tf_op jit(solution)/shard_map/ppermute | solution.py:252
  113.3 4.9 %collective-permute-start.21 = (bf16[3,32,1024]{2,1,0:T(8,128)(2,1)S(1)}, bf16[3,32,1024]{2,1,0:T(8,128)(2,1)S(1)}, u32[]{:S(2)}, u32[]{:S(2)}) collective-permute-start(bf16[3,32,1024]{2,1,0:T(8,128)(2,1)S(1)} %get-tuple-element.35), channel_id=1, source_target_pairs={{0,34},{1,35},{2,32},{3,33},{4,38},{5,39},{6,36},{7,37},{8,42},{9,... | collective-permute-start | bytes 589832 | tf_op jit(solution)/shard_map/ppermute | solution.py:252
  118.3 3.3 %collective-permute-start.22 = (bf16[3,32,1024]{2,1,0:T(8,128)(2,1)S(1)}, bf16[3,32,1024]{2,1,0:T(8,128)(2,1)S(1)}, u32[]{:S(2)}, u32[]{:S(2)}) collective-permute-start(bf16[3,32,1024]{2,1,0:T(8,128)(2,1)S(1)} %get-tuple-element.36), channel_id=1, source_target_pairs={{0,33},{1,34},{2,35},{3,32},{4,37},{5,38},{6,39},{7,36},{8,41},{9,... | collective-permute-start | bytes 589832 | tf_op jit(solution)/shard_map/ppermute | solution.py:252
  121.6 0.2 collective-permute-done.21.refs_6_
  121.8 4.7 %collective-permute-done.22.refs_7_ = bf16[3,32,1024]{2,1,0:T(8,128)(2,1)S(1)} collective-permute-done((bf16[3,32,1024]{2,1,0:T(8,128)(2,1)S(1)}, bf16[3,32,1024]{2,1,0:T(8,128)(2,1)S(1)}, u32[]{:S(2)}, u32[]{:S(2)}) %collective-permute-start.22) | collective-permute-done | bytes 196640 | tf_op jit(solution)/shard_map/ppermute | solution.py:252
  126.5 1.8 %shard_map.115 = bf16[8,3,16,1024]{3,2,1,0:T(8,128)(2,1)} custom-call(s32[2]{0:T(128)S(1)} %pad_add_fusion.2.place_ref, bf16[128,256]{1,0:T(8,128)(2,1)S(1)} %get-tuple-element.20.pick_ref, bf16[3,32,1024]{2,1,0:T(8,128)(2,1)S(1)} %get-tuple-element.29.refs_0_, bf16[3,32,1024]{2,1,0:T(8,128)(2,1)S(1)} %collective-permute-done.16.refs_1_, ...), custom_call_target="tpu_custom_call" | custom-call | tf_op jit(solution)/shard_map/pallas_call | solution.py:254
  128.3 3.5 %all-to-all-start = ((bf16[8,3,16,1024]{3,2,1,0:T(8,128)(2,1)}), bf16[8,3,16,1024]{3,2,1,0:T(8,128)(2,1)S(1)}, u32[]{:S(2)}, u32[]{:S(2)}) async-start(bf16[8,3,16,1024]{3,2,1,0:T(8,128)(2,1)} %shard_map.115), calls=%async_computation | async-start | bytes 1572864 | tf_op jit(solution)/shard_map/all_to_all | solution.py:262
  131.9 0.7 reduce.1
  132.5 22.2 %all-to-all-done = bf16[8,3,16,1024]{3,2,1,0:T(8,128)(2,1)S(1)} async-done(((bf16[8,3,16,1024]{3,2,1,0:T(8,128)(2,1)}), bf16[8,3,16,1024]{3,2,1,0:T(8,128)(2,1)S(1)}, u32[]{:S(2)}, u32[]{:S(2)}) %all-to-all-start) | async-done | bytes 786464 | tf_op jit(solution)/shard_map/all_to_all | solution.py:262
  154.8 0.1 reduce_sum.12
  154.9 6.8 %convolution_convert_fusion = bf16[48,4096]{1,0:T(8,128)(2,1)} fusion(bf16[48,1024]{1,0:T(8,128)(2,1)S(1)} %bitcast.24, bf16[4096,1024]{1,0:T(8,128)(2,1)} %constant.144.clone), kind=kOutput, calls=%fused_computation | convolution fusion | flops 402849792 | bytes 8880128 | tf_op jit(solution)/shard_map/dot_general | solution.py:266
  (35 shorter events, 0.2 us)
Async XLA Ops:
  0.6 11.0 %collective-permute-start = (s32[32,4]{0,1:T(4,128)}, s32[32,4]{0,1:T(4,128)S(1)}, u32[]{:S(2)}, u32[]{:S(2)}) collective-permute-start(s32[32,4]{0,1:T(4,128)} %param.13), channel_id=1, source_target_pairs={{0,32},{32,64},{64,96},{96,128},{128,160},{160,192},{192,224},{1,3... | collective-permute-start | bytes 1544 | tf_op jit(solution)/shard_map/ppermute | solution.py:187
  6.3 5.0 %copy-start.1 = (s32[32,4]{0,1:T(4,128)S(1)}, s32[32,4]{0,1:T(4,128)}, u32[]{:S(2)}) copy-start(s32[32,4]{0,1:T(4,128)} %param.12) | copy-start | bytes 1540
  6.3 71.9 %copy-start.2 = (s32[256]{0:T(256)S(1)}, s32[256]{0:T(256)}, u32[]{:S(2)}) copy-start(s32[256]{0:T(256)} %param.14) | copy-start | bytes 3076
  6.4 71.9 %copy-start.3 = (s32[256]{0:T(256)S(1)}, s32[256]{0:T(256)}, u32[]{:S(2)}) copy-start(s32[256]{0:T(256)} %param.15) | copy-start | bytes 3076
  6.4 71.9 %copy-start.4 = (s32[256]{0:T(256)S(1)}, s32[256]{0:T(256)}, u32[]{:S(2)}) copy-start(s32[256]{0:T(256)} %param.17) | copy-start | bytes 3076
  6.4 71.9 %copy-start.5 = (s32[256]{0:T(256)S(1)}, s32[256]{0:T(256)}, u32[]{:S(2)}) copy-start(s32[256]{0:T(256)} %param.16) | copy-start | bytes 3076
  6.4 80.3 %copy-start = (bf16[1024,512]{1,0:T(8,128)(2,1)S(1)}, bf16[1024,512]{1,0:T(8,128)(2,1)}, u32[]{:S(2)}) copy-start(bf16[1024,512]{1,0:T(8,128)(2,1)} %constant.145.clone.lag_ref) | copy-start | bytes 3145732
  11.9 10.3 %collective-permute-start.2 = (bf16[7,16,1024]{2,1,0:T(8,128)(2,1)S(1)}, bf16[7,16,1024]{2,1,0:T(8,128)(2,1)S(1)}, u32[]{:S(2)}, u32[]{:S(2)}) collective-permute-start(bf16[7,16,1024]{2,1,0:T(8,128)(2,1)S(1)} %pad_maximum_fusion.1.refs_0_), channel_id=1, source_target_pairs={{0,28},{1,29},{2,30},{3,31},{4,0},{5,1},{6,2},{7,3},{8,4},{9,5},{1... | collective-permute-start | bytes 688136 | tf_op jit(solution)/shard_map/ppermute | solution.py:198
  17.5 8.0 %collective-permute-start.1 = (bf16[7,16,1024]{2,1,0:T(8,128)(2,1)S(1)}, bf16[7,16,1024]{2,1,0:T(8,128)(2,1)S(1)}, u32[]{:S(2)}, u32[]{:S(2)}) collective-permute-start(bf16[7,16,1024]{2,1,0:T(8,128)(2,1)S(1)} %pad_maximum_fusion.1.refs_0_), channel_id=1, source_target_pairs={{0,4},{1,5},{2,6},{3,7},{4,8},{5,9},{6,10},{7,11},{8,12},{9,13},{1... | collective-permute-start | bytes 688136 | tf_op jit(solution)/shard_map/ppermute | solution.py:197
  22.2 8.3 %collective-permute-start.4 = (bf16[7,16,1024]{2,1,0:T(8,128)(2,1)S(1)}, bf16[7,16,1024]{2,1,0:T(8,128)(2,1)S(1)}, u32[]{:S(2)}, u32[]{:S(2)}) collective-permute-start(bf16[7,16,1024]{2,1,0:T(8,128)(2,1)S(1)} %collective-permute-done.2.refs_2_), channel_id=1, source_target_pairs={{0,28},{1,29},{2,30},{3,31},{4,0},{5,1},{6,2},{7,3},{8,4},{9,5},{1... | collective-permute-start | bytes 688136 | tf_op jit(solution)/shard_map/ppermute | solution.py:198
  25.6 8.3 %collective-permute-start.3 = (bf16[7,16,1024]{2,1,0:T(8,128)(2,1)S(1)}, bf16[7,16,1024]{2,1,0:T(8,128)(2,1)S(1)}, u32[]{:S(2)}, u32[]{:S(2)}) collective-permute-start(bf16[7,16,1024]{2,1,0:T(8,128)(2,1)S(1)} %collective-permute-done.1.refs_1_), channel_id=1, source_target_pairs={{0,4},{1,5},{2,6},{3,7},{4,8},{5,9},{6,10},{7,11},{8,12},{9,13},{1... | collective-permute-start | bytes 688136 | tf_op jit(solution)/shard_map/ppermute | solution.py:197
  30.4 7.7 %collective-permute-start.6 = (bf16[7,16,1024]{2,1,0:T(8,128)(2,1)S(1)}, bf16[7,16,1024]{2,1,0:T(8,128)(2,1)S(1)}, u32[]{:S(2)}, u32[]{:S(2)}) collective-permute-start(bf16[7,16,1024]{2,1,0:T(8,128)(2,1)S(1)} %collective-permute-done.4.refs_4_), channel_id=1, source_target_pairs={{0,28},{1,29},{2,30},{3,31},{4,0},{5,1},{6,2},{7,3},{8,4},{9,5},{1... | collective-permute-start | bytes 688136 | tf_op jit(solution)/shard_map/ppermute | solution.py:198
  33.8 7.8 %collective-permute-start.5 = (bf16[7,16,1024]{2,1,0:T(8,128)(2,1)S(1)}, bf16[7,16,1024]{2,1,0:T(8,128)(2,1)S(1)}, u32[]{:S(2)}, u32[]{:S(2)}) collective-permute-start(bf16[7,16,1024]{2,1,0:T(8,128)(2,1)S(1)} %collective-permute-done.3.refs_3_), channel_id=1, source_target_pairs={{0,4},{1,5},{2,6},{3,7},{4,8},{5,9},{6,10},{7,11},{8,12},{9,13},{1... | collective-permute-start | bytes 688136 | tf_op jit(solution)/shard_map/ppermute | solution.py:197
  38.1 8.3 %collective-permute-start.8 = (bf16[4,16,1024]{2,1,0:T(8,128)(2,1)S(1)}, bf16[4,16,1024]{2,1,0:T(8,128)(2,1)S(1)}, u32[]{:S(2)}, u32[]{:S(2)}) collective-permute-start(bf16[4,16,1024]{2,1,0:T(8,128)(2,1)S(1)} %slice.9), channel_id=1, source_target_pairs={{0,28},{1,29},{2,30},{3,31},{4,0},{5,1},{6,2},{7,3},{8,4},{9,5},{1... | collective-permute-start | bytes 393224 | tf_op jit(solution)/shard_map/ppermute | solution.py:203
  41.6 4.8 %collective-permute-start.7 = (bf16[3,16,1024]{2,1,0:T(8,128)(2,1)S(1)}, bf16[3,16,1024]{2,1,0:T(8,128)(2,1)S(1)}, u32[]{:S(2)}, u32[]{:S(2)}) collective-permute-start(bf16[3,16,1024]{2,1,0:T(8,128)(2,1)S(1)} %slice.8), channel_id=1, source_target_pairs={{0,4},{1,5},{2,6},{3,7},{4,8},{5,9},{6,10},{7,11},{8,12},{9,13},{1... | collective-permute-start | bytes 294920 | tf_op jit(solution)/shard_map/ppermute | solution.py:202
  49.4 12.6 %collective-permute-start.9 = (bf16[2,3,32,1024]{3,2,1,0:T(8,128)(2,1)S(1)}, bf16[2,3,32,1024]{3,2,1,0:T(8,128)(2,1)S(1)}, u32[]{:S(2)}, u32[]{:S(2)}) collective-permute-start(bf16[2,3,32,1024]{3,2,1,0:T(8,128)(2,1)S(1)} %get-tuple-element.22), channel_id=1, source_target_pairs={{0,1},{1,2},{2,3},{3,0},{4,5},{5,6},{6,7},{7,4},{8,9},{9,10},{10,1... | collective-permute-start | bytes 1179656 | tf_op jit(solution)/shard_map/ppermute | solution.py:216
  50.7 25.5 %collective-permute-start.10 = (bf16[2,3,32,1024]{3,2,1,0:T(8,128)(2,1)S(1)}, bf16[2,3,32,1024]{3,2,1,0:T(8,128)(2,1)S(1)}, u32[]{:S(2)}, u32[]{:S(2)}) collective-permute-start(bf16[2,3,32,1024]{3,2,1,0:T(8,128)(2,1)S(1)} %get-tuple-element.23), channel_id=1, source_target_pairs={{0,2},{1,3},{2,0},{3,1},{4,6},{5,7},{6,4},{7,5},{8,10},{9,11},{10,... | collective-permute-start | bytes 1179656 | tf_op jit(solution)/shard_map/ppermute | solution.py:216
  53.3 25.2 %collective-permute-start.11 = (bf16[2,3,32,1024]{3,2,1,0:T(8,128)(2,1)}, bf16[2,3,32,1024]{3,2,1,0:T(8,128)(2,1)S(1)}, u32[]{:S(2)}, u32[]{:S(2)}) collective-permute-start(bf16[2,3,32,1024]{3,2,1,0:T(8,128)(2,1)} %get-tuple-element.24), channel_id=1, source_target_pairs={{0,3},{1,0},{2,1},{3,2},{4,7},{5,4},{6,5},{7,6},{8,11},{9,8},{10,9... | collective-permute-start | bytes 1179656 | tf_op jit(solution)/shard_map/ppermute | solution.py:216
  54.3 24.2 %collective-permute-start.12 = (bf16[2,3,32,1024]{3,2,1,0:T(8,128)(2,1)}, bf16[2,3,32,1024]{3,2,1,0:T(8,128)(2,1)S(1)}, u32[]{:S(2)}, u32[]{:S(2)}) collective-permute-start(bf16[2,3,32,1024]{3,2,1,0:T(8,128)(2,1)} %get-tuple-element.25), channel_id=1, source_target_pairs={{32,0},{33,1},{34,2},{35,3},{36,4},{37,5},{38,6},{39,7},{40,8},{41... | collective-permute-start | bytes 1179656 | tf_op jit(solution)/shard_map/ppermute | solution.py:219
  60.1 20.8 %collective-permute-start.13 = (bf16[2,3,32,1024]{3,2,1,0:T(8,128)(2,1)}, bf16[2,3,32,1024]{3,2,1,0:T(8,128)(2,1)}, u32[]{:S(2)}, u32[]{:S(2)}) collective-permute-start(bf16[2,3,32,1024]{3,2,1,0:T(8,128)(2,1)} %get-tuple-element.26), channel_id=1, source_target_pairs={{32,1},{33,2},{34,3},{35,0},{36,5},{37,6},{38,7},{39,4},{40,9},{41... | collective-permute-start | bytes 1179656 | tf_op jit(solution)/shard_map/ppermute | solution.py:219
  62.0 23.0 %collective-permute-start.14 = (bf16[2,3,32,1024]{3,2,1,0:T(8,128)(2,1)}, bf16[2,3,32,1024]{3,2,1,0:T(8,128)(2,1)}, u32[]{:S(2)}, u32[]{:S(2)}) collective-permute-start(bf16[2,3,32,1024]{3,2,1,0:T(8,128)(2,1)} %get-tuple-element.27), channel_id=1, source_target_pairs={{32,2},{33,3},{34,0},{35,1},{36,6},{37,7},{38,4},{39,5},{40,10},{4... | collective-permute-start | bytes 1179656 | tf_op jit(solution)/shard_map/ppermute | solution.py:219
  76.1 10.6 %collective-permute-start.15 = (bf16[2,3,32,1024]{3,2,1,0:T(8,128)(2,1)}, bf16[2,3,32,1024]{3,2,1,0:T(8,128)(2,1)}, u32[]{:S(2)}, u32[]{:S(2)}) collective-permute-start(bf16[2,3,32,1024]{3,2,1,0:T(8,128)(2,1)} %get-tuple-element.28), channel_id=1, source_target_pairs={{32,3},{33,0},{34,1},{35,2},{36,7},{37,4},{38,5},{39,6},{40,11},{4... | collective-permute-start | bytes 1179656 | tf_op jit(solution)/shard_map/ppermute | solution.py:219
  95.9 17.5 %collective-permute-start.16 = (bf16[3,32,1024]{2,1,0:T(8,128)(2,1)S(1)}, bf16[3,32,1024]{2,1,0:T(8,128)(2,1)S(1)}, u32[]{:S(2)}, u32[]{:S(2)}) collective-permute-start(bf16[3,32,1024]{2,1,0:T(8,128)(2,1)S(1)} %get-tuple-element.30), channel_id=1, source_target_pairs={{0,3},{1,0},{2,1},{3,2},{4,7},{5,4},{6,5},{7,6},{8,11},{9,8},{10,9... | collective-permute-start | bytes 589832 | tf_op jit(solution)/shard_map/ppermute | solution.py:249
  100.8 17.5 %collective-permute-start.17 = (bf16[3,32,1024]{2,1,0:T(8,128)(2,1)S(1)}, bf16[3,32,1024]{2,1,0:T(8,128)(2,1)S(1)}, u32[]{:S(2)}, u32[]{:S(2)}) collective-permute-start(bf16[3,32,1024]{2,1,0:T(8,128)(2,1)S(1)} %get-tuple-element.31), channel_id=1, source_target_pairs={{0,2},{1,3},{2,0},{3,1},{4,6},{5,7},{6,4},{7,5},{8,10},{9,11},{10,... | collective-permute-start | bytes 589832 | tf_op jit(solution)/shard_map/ppermute | solution.py:249
  103.3 18.3 %collective-permute-start.18 = (bf16[3,32,1024]{2,1,0:T(8,128)(2,1)S(1)}, bf16[3,32,1024]{2,1,0:T(8,128)(2,1)S(1)}, u32[]{:S(2)}, u32[]{:S(2)}) collective-permute-start(bf16[3,32,1024]{2,1,0:T(8,128)(2,1)S(1)} %get-tuple-element.32), channel_id=1, source_target_pairs={{0,1},{1,2},{2,3},{3,0},{4,5},{5,6},{6,7},{7,4},{8,9},{9,10},{10,1... | collective-permute-start | bytes 589832 | tf_op jit(solution)/shard_map/ppermute | solution.py:249
  103.3 18.3 %collective-permute-start.19 = (bf16[3,32,1024]{2,1,0:T(8,128)(2,1)S(1)}, bf16[3,32,1024]{2,1,0:T(8,128)(2,1)S(1)}, u32[]{:S(2)}, u32[]{:S(2)}) collective-permute-start(bf16[3,32,1024]{2,1,0:T(8,128)(2,1)S(1)} %get-tuple-element.33), channel_id=1, source_target_pairs={{0,32},{1,33},{2,34},{3,35},{4,36},{5,37},{6,38},{7,39},{8,40},{9,... | collective-permute-start | bytes 589832 | tf_op jit(solution)/shard_map/ppermute | solution.py:252
  109.7 11.9 %collective-permute-start.20 = (bf16[3,32,1024]{2,1,0:T(8,128)(2,1)S(1)}, bf16[3,32,1024]{2,1,0:T(8,128)(2,1)S(1)}, u32[]{:S(2)}, u32[]{:S(2)}) collective-permute-start(bf16[3,32,1024]{2,1,0:T(8,128)(2,1)S(1)} %get-tuple-element.34), channel_id=1, source_target_pairs={{0,35},{1,32},{2,33},{3,34},{4,39},{5,36},{6,37},{7,38},{8,43},{9,... | collective-permute-start | bytes 589832 | tf_op jit(solution)/shard_map/ppermute | solution.py:252
  113.3 8.5 %collective-permute-start.21 = (bf16[3,32,1024]{2,1,0:T(8,128)(2,1)S(1)}, bf16[3,32,1024]{2,1,0:T(8,128)(2,1)S(1)}, u32[]{:S(2)}, u32[]{:S(2)}) collective-permute-start(bf16[3,32,1024]{2,1,0:T(8,128)(2,1)S(1)} %get-tuple-element.35), channel_id=1, source_target_pairs={{0,34},{1,35},{2,32},{3,33},{4,38},{5,39},{6,36},{7,37},{8,42},{9,... | collective-permute-start | bytes 589832 | tf_op jit(solution)/shard_map/ppermute | solution.py:252
  118.3 8.2 %collective-permute-start.22 = (bf16[3,32,1024]{2,1,0:T(8,128)(2,1)S(1)}, bf16[3,32,1024]{2,1,0:T(8,128)(2,1)S(1)}, u32[]{:S(2)}, u32[]{:S(2)}) collective-permute-start(bf16[3,32,1024]{2,1,0:T(8,128)(2,1)S(1)} %get-tuple-element.36), channel_id=1, source_target_pairs={{0,33},{1,34},{2,35},{3,32},{4,37},{5,38},{6,39},{7,36},{8,41},{9,... | collective-permute-start | bytes 589832 | tf_op jit(solution)/shard_map/ppermute | solution.py:252
  128.3 26.5 %all-to-all-start = ((bf16[8,3,16,1024]{3,2,1,0:T(8,128)(2,1)}), bf16[8,3,16,1024]{3,2,1,0:T(8,128)(2,1)S(1)}, u32[]{:S(2)}, u32[]{:S(2)}) async-start(bf16[8,3,16,1024]{3,2,1,0:T(8,128)(2,1)} %shard_map.115), calls=%async_computation | async-start | bytes 1572864 | tf_op jit(solution)/shard_map/all_to_all | solution.py:262

commit v2 on v1

v2 whole, which is shorter than its diff:
```python
import functools
import math

import jax
import jax.numpy as jnp
import ml_dtypes
import numpy as np
from jax import lax
from jax.experimental import pallas as pl
from jax.experimental.pallas import tpu as pltpu
from jax.sharding import PartitionSpec as P

F = 512
FLOW = 64
LAGS = 512
ZS = 8
YS = 4
CAP = 4
ROWS = 16
Q = 6
RADIX = 4
EARLY, LATE = (0, 1, 2, 3), (4, 5, 6, 7)
VMEM_BYTES = 40 * 1024 * 1024
BF = jnp.bfloat16
F32 = jnp.float32


def tables(ticks):
    rate = FLOW + np.arange(F, dtype=np.int64).reshape(-1, RADIX).T.reshape(-1)
    quarter = ticks // RADIX
    turn = (np.arange(quarter, dtype=np.int64)[:, None] * rate[None, :]) % ticks
    angle = (turn.astype(np.float32) * np.float32(2.0 * math.pi / ticks)).astype(np.float64)
    forward = np.stack([np.cos(angle), -np.sin(angle)], 1).astype(np.float32)
    forward = (forward / np.float32(math.sqrt(ticks))).astype(ml_dtypes.bfloat16)
    forward = forward.reshape(quarter, 2, RADIX, F // RADIX).transpose(2, 0, 1, 3)
    forward = forward.reshape(RADIX, quarter, 2 * F // RADIX)
    shifts = np.arange(LAGS, dtype=np.int64) - LAGS // 2
    turn = (rate[:, None] * shifts[None, :]) % ticks
    angle = (turn.astype(np.float32) * np.float32(2.0 * math.pi / ticks)).astype(np.float64)
    lag = np.concatenate([np.cos(angle), -np.sin(angle)], 0).astype(np.float32)
    lag = (lag / np.float32(math.sqrt(F))).astype(ml_dtypes.bfloat16)
    return forward, np.ascontiguousarray(forward.transpose(0, 2, 1)), lag


def z_pairs(step):
    return [(z * YS + y, (z + step) % ZS * YS + y) for z in range(ZS) for y in range(YS)]


def y_pairs(step, regions, shift):
    devs = ZS * YS
    return [
        (r * devs + z * YS + y, (r + shift) * devs + z * YS + (y + step) % YS)
        for r in range(max(0, -shift), min(regions, regions - shift))
        for z in range(ZS)
        for y in range(YS)
    ]


def iota(shape, axis):
    return lax.broadcasted_iota(jnp.int32, shape, axis)


def dot(a, b):
    return jnp.dot(a, b, preferred_element_type=F32)


def forward_kernel(synthetic_ref, observed_ref, table_ref, out_ref):
    quarter = synthetic_ref.shape[2] // RADIX
    group = F // RADIX
    out_ref[Q] = jnp.zeros((ROWS, 2 * F), BF)
    traces = [ref[c] for ref in (synthetic_ref, observed_ref) for c in range(3)]
    traces = jnp.concatenate(traces, 0)
    for c in range(RADIX):
        sums = [dot(traces[:, j * quarter : (j + 1) * quarter], table_ref[c]) for j in range(RADIX)]
        (r0, i0), (r1, i1), (r2, i2), (r3, i3) = [(p[:, :group], p[:, group:]) for p in sums]
        if c == 0:
            real, imag = (r0 + r1) + (r2 + r3), (i0 + i1) + (i2 + i3)
        elif c == 1:
            real, imag = (r0 - r2) + (i1 - i3), (i0 - i2) - (r1 - r3)
        elif c == 2:
            real, imag = (r0 - r1) + (r2 - r3), (i0 - i1) + (i2 - i3)
        else:
            real, imag = (r0 - r2) - (i1 - i3), (i0 - i2) + (r1 - r3)
        at = c * group
        out_ref[:Q, :, at : at + group] = real.astype(BF).reshape(Q, ROWS, group)
        out_ref[:Q, :, F + at : F + at + group] = imag.astype(BF).reshape(Q, ROWS, group)


def inverse_kernel(near_ref, far_ref, table_ref, out_ref):
    rows = out_ref.shape[0]
    quarter = out_ref.shape[1] // RADIX
    part = table_ref.shape[2]
    group = F // RADIX
    total = (near_ref[...] + far_ref[...]).astype(BF)
    real = [total[:, c * group : (c + 1) * group] for c in range(RADIX)]
    imag = [total[:, F + c * group : F + (c + 1) * group] for c in range(RADIX)]
    plain = [jnp.concatenate([real[c], imag[c]], 1) for c in range(RADIX)]
    turned = [jnp.concatenate([-imag[c], real[c]], 1) for c in range(RADIX)]
    p0, p2 = dot(plain[0], table_ref[0]), dot(plain[2], table_ref[2])
    one = dot(jnp.concatenate([plain[1], turned[1]], 0), table_ref[1])
    three = dot(jnp.concatenate([plain[3], turned[3]], 0), table_ref[3])
    p1, q1, p3, q3 = one[:rows], one[rows:], three[:rows], three[rows:]
    parts = (p0 + p2) + (p1 + p3), (p0 - p2) + (q1 - q3), (p0 + p2) - (p1 + p3), (p0 - p2) - (q1 - q3)
    start = pl.program_id(0) * part
    for j, value in enumerate(parts):
        at = pl.multiple_of(start + j * quarter, part)
        out_ref[:, pl.ds(at, part)] = value.astype(BF)


def position():
    here = lax.axis_index("dev")
    return here // YS, here % YS


def select_kernel(jobs, places, *refs):
    blocks, outs = dict(zip(places, refs)), refs[len(places) :]
    z, y = position()
    for n, (side, ring) in enumerate(jobs):
        out, size = outs[n * YS : (n + 1) * YS], len(ring)
        count, wide = size * CAP, size * ROWS
        row = iota((YS * count, 1), 0)
        cap, block, step = row % CAP, row // CAP % size, row // count
        expand = (iota((YS * count, wide), 1) == block * ROWS + side * CAP + cap).astype(BF)
        index = jnp.concatenate([blocks[p][Q, :, : 4 * ZS * YS] for p in ring], 0)
        spread = dot(expand, index)
        lane = z * YS + (y + step) % YS
        value = jnp.sum(jnp.where(iota(spread.shape, 1) == lane, spread, 0.0), 1, keepdims=True)
        pick = iota((YS * count, wide), 1) == block * ROWS + value.astype(jnp.int32)
        pick = pick.astype(BF)
        for q in range(Q):
            got = dot(pick, jnp.concatenate([blocks[p][q] for p in ring], 0)).astype(BF)
            for k in range(YS):
                out[k][q // 3, q % 3] = got[k * count : (k + 1) * count]


def ring_place(offset):
    offset = offset % ZS
    return jnp.where(offset == 0, 0, jnp.where(offset <= ZS // 2, 2 * offset - 1, 2 * (ZS - offset)))


def pair_kernel(slots_ref, lag_ref, *refs):
    pieces, (misfit_ref, out_ref) = refs[:-2], refs[-2:]
    pairs = slots_ref.shape[1]
    peers = ZS * YS
    near = peers * CAP
    z, y = position()
    lag = lag_ref[...]
    slots = slots_ref[:2]
    side, member, cap = slots // near, slots // CAP % peers, slots % CAP
    step = (y - member % YS + YS) % YS
    held = ((side * YS + step) * ZS + ring_place(z - member // YS + ZS)) * CAP + cap
    back = (member * 2 + side) * CAP + cap
    first_back = (iota((2 * near, pairs), 0) == back[:1]).astype(BF)
    second_back = (iota((2 * near, pairs), 0) == back[1:]).astype(BF)
    column = jnp.concatenate([held, slots_ref[2:4], held, held], 0).astype(F32).T.astype(jnp.int32)
    first = (iota((pairs, near), 1) == column[:, 0:1]).astype(BF)
    second = (iota((pairs, 2 * near), 1) == column[:, 1:2]).astype(BF)

    def both(kind):
        spectra = jnp.concatenate([piece[kind, 0] for piece in pieces], 0)
        a = dot(first, spectra[:near])
        b = dot(second, spectra)
        return a[:, :F], a[:, F:], b[:, :F], b[:, F:]

    ar, ai, br, bi = both(0)
    cr, ci, dr, di = both(1)
    real = (ar * br + ai * bi) - (cr * dr + ci * di)
    imag = (ai * br - ar * bi) - (ci * dr - cr * di)
    shifted = dot(real.astype(BF), lag[:F]) + dot(imag.astype(BF), lag[F:])
    at = iota((pairs, LAGS), 1)
    start = column[:, 2:3]
    inside = (at >= start) & (at < start + column[:, 3:4])
    residual = jnp.where(inside, shifted, 0.0)
    part = jnp.sum(residual * residual, axis=1, keepdims=True)

    @pl.when(pl.program_id(0) == 0)
    def _():
        misfit_ref[...] = jnp.zeros_like(misfit_ref)

    misfit_ref[...] += part * (1.0 / (2.0 * LAGS))
    slope = lax.dot_general(
        residual.astype(BF), lag, (((1,), (1,)), ((), ())), preferred_element_type=F32
    )
    gr, gi = slope[:, :F], slope[:, F:]
    grad_first = jnp.concatenate([gr * br - gi * bi, gr * bi + gi * br], 1).astype(BF)
    grad_second = jnp.concatenate([gr * ar + gi * ai, gr * ai - gi * ar], 1).astype(BF)
    total = dot(first_back, grad_first) + dot(second_back, grad_second)
    total = total.reshape(peers, 2 * CAP, 2 * F)
    out_ref[...] = jnp.concatenate([total[..., :F], total[..., F:]], 1).astype(BF)


def collect_kernel(held_ref, grad_ref, near_ref, far_ref):
    rows = held_ref.shape[1]
    pick = (iota((4 * ROWS, rows), 0) == held_ref[...]).astype(BF)
    total = dot(pick, grad_ref[...].reshape(rows, F))
    near_ref[...] = jnp.concatenate([total[:ROWS], total[2 * ROWS : 3 * ROWS]], 1)
    far_ref[...] = jnp.concatenate([total[ROWS : 2 * ROWS], total[3 * ROWS :]], 1)


def whole(count):
    return [pl.BlockSpec(memory_space=pltpu.VMEM)] * count


def shape(dims, kind=BF):
    return jax.ShapeDtypeStruct(dims, kind)


def cost(flops, size):
    return pl.CostEstimate(flops=flops, bytes_accessed=size, transcendentals=0)


def on_device(
    regions,
    synthetic,
    observed,
    nearby_receiver_slots,
    far_rows,
    first_slot,
    second_slot,
    window_start,
    pair_delay_indices,
):
    ticks = synthetic.shape[2]
    pairs = first_slot.shape[0]
    forward, inverse, lag = [jnp.asarray(table) for table in tables(ticks)]
    params = pltpu.CompilerParams(vmem_limit_bytes=VMEM_BYTES)
    peers = ZS * YS

    def z_move(value, step):
        return lax.ppermute(value, "dev", z_pairs(step))

    def y_move(value, step, shift):
        return lax.ppermute(value, ("region", "dev"), y_pairs(step, regions, shift))

    far_index = lax.ppermute(far_rows.T, "region", [(r, r + 1) for r in range(regions - 1)])
    sources = [synthetic.transpose(1, 0, 2), observed.transpose(1, 0, 2)]
    own = pl.pallas_call(
        forward_kernel,
        grid=(1,),
        out_shape=shape((Q + 1, ROWS, 2 * F)),
        in_specs=[pl.BlockSpec((3, ROWS, ticks), lambda i: (0, 0, 0))] * 2
        + [pl.BlockSpec(forward.shape, lambda i: (0, 0, 0))],
        out_specs=pl.BlockSpec((Q + 1, ROWS, 2 * F), lambda i: (0, 0, 0)),
        compiler_params=pltpu.CompilerParams(vmem_limit_bytes=60 * 1024 * 1024),
        cost_estimate=cost(2 * Q * ROWS * ticks * 2 * F, 3 << 20),
    )(*sources, forward)
    index = jnp.concatenate([nearby_receiver_slots.T, far_index]).astype(BF)
    index = jnp.pad(index, ((0, ROWS - index.shape[0]), (0, 2 * F - index.shape[1])))
    own = lax.dynamic_update_slice(own, index[None], (Q, 0, 0))

    def select(jobs, blocks):
        sizes = [len(ring) * CAP for _, ring in jobs for _ in range(YS)]
        return pl.pallas_call(
            functools.partial(select_kernel, jobs, tuple(blocks)),
            out_shape=[shape((2, 3, size, 2 * F)) for size in sizes],
            in_specs=whole(len(blocks)),
            out_specs=whole(len(sizes)),
            compiler_params=params,
            cost_estimate=cost(1 << 29, 5 << 20),
        )(*blocks.values())

    up, down = z_move(own, 1), z_move(own, -1)
    up2, down2 = z_move(up, 1), z_move(down, -1)
    up3, down3 = z_move(up2, 1), z_move(down2, -1)
    early = select([(0, EARLY)], dict(zip(EARLY, [own, up, down, up2])))
    early = [early[0]] + [y_move(early[k], k, 0) for k in range(1, YS)]
    split = Q // 2
    half_up, half_down = up3[:split], down3[split:]
    half_up, early[0] = lax.optimization_barrier((half_up, early[0]))
    last = jnp.concatenate([z_move(half_up, 1), z_move(half_down, -1)], 0)
    blocks = dict(enumerate([own, up, down, up2, down2, up3, down3, last]))
    late = select([(0, LATE), (1, EARLY + LATE)], blocks)
    far = [y_move(piece, k, -1) for k, piece in enumerate(late[YS:])]
    late = [late[0]] + [y_move(late[k], k, 0) for k in range(1, YS)]
    pieces = [piece for pair in zip(early, late) for piece in pair] + far
    slots = jnp.stack([first_slot, second_slot, window_start, pair_delay_indices])
    misfit, grads = pl.pallas_call(
        pair_kernel,
        grid=(3,),
        out_shape=[shape((pairs, 1), F32), shape((peers, 3 * ROWS, F))],
        in_specs=[
            pl.BlockSpec((4, pairs), lambda c: (0, 0)),
            pl.BlockSpec((2 * F, LAGS), lambda c: (0, 0)),
        ]
        + [
            pl.BlockSpec((2, 1) + piece.shape[2:], lambda c: (0, c, 0, 0)) for piece in pieces
        ],
        out_specs=[
            pl.BlockSpec((pairs, 1), lambda c: (0, 0)),
            pl.BlockSpec((peers, ROWS, F), lambda c: (0, c, 0)),
        ],
        compiler_params=params,
        cost_estimate=cost(9 << 30, 9 << 20),
    )(slots, lag, *pieces)
    grads = lax.all_to_all(grads, "dev", split_axis=0, concat_axis=0, tiled=True)
    held = jnp.concatenate([nearby_receiver_slots, far_rows + ROWS], 1)
    held = jnp.concatenate([held, held + 2 * ROWS], 1).reshape(1, peers * ROWS)
    near_sum, far_sum = pl.pallas_call(
        collect_kernel,
        grid=(3,),
        out_shape=[shape((3 * ROWS, 2 * F), F32)] * 2,
        in_specs=[
            pl.BlockSpec((1, peers * ROWS), lambda c: (0, 0)),
            pl.BlockSpec((peers, ROWS, F), lambda c: (0, c, 0)),
        ],
        out_specs=[pl.BlockSpec((ROWS, 2 * F), lambda c: (c, 0))] * 2,
        compiler_params=params,
        cost_estimate=cost(1 << 26, 2 << 20),
    )(held, grads)
    far_sum = lax.ppermute(far_sum, "region", [(r, r + 1) for r in range(regions - 1)])
    part = ticks // RADIX // 2
    adjoint = pl.pallas_call(
        inverse_kernel,
        grid=(2,),
        out_shape=shape((3 * ROWS, ticks)),
        in_specs=[pl.BlockSpec((3 * ROWS, 2 * F), lambda i: (0, 0))] * 2
        + [pl.BlockSpec((RADIX, 2 * F // RADIX, part), lambda i: (0, 0, i))],
        out_specs=pl.BlockSpec((3 * ROWS, ticks), lambda i: (0, 0)),
        compiler_params=pltpu.CompilerParams(vmem_limit_bytes=60 * 1024 * 1024),
        cost_estimate=cost(2 * 3 * ROWS * ticks * 2 * F, 3 << 20),
    )(near_sum, far_sum, inverse)
    adjoint = adjoint.reshape(3, ROWS, ticks).transpose(1, 0, 2)
    return (adjoint, misfit.reshape(pairs))


def solution(mesh):
    both = ("region", "dev")
    placed = (P(both, None, None),) * 2 + (P(both, None),) * 2 + (P(both),) * 4
    return jax.shard_map(
        functools.partial(on_device, mesh.shape["region"]),
        mesh=mesh,
        in_specs=placed,
        out_specs=(P(both, None, None), P(both)),
        check_vma=False,
    )
```

time: 164 us -> 151 us (0.921); the launches traced: 162 us -> 151 us
  starting transfers between devices: 78.3 us -> 49.9 us
  waiting for transfers between devices: 54 us -> 76.6 us
  matrix products: 11.7 us -> 0 us
  Pallas kernels: 13.9 us -> 19.1 us
  local copies, waits for them, and re-layouts: 0.62 us -> 2.49 us
    ppermute x23 -> x20, starting transfers between devices: 74.8 us -> 42.5 us  [the longest x10 19.7 us: y_move(): return lax.ppermute(value, ('region', 'dev'), y_pairs(step, regions, shift))]
    all_to_all x1, waiting for transfers between devices: 22.2 us -> 38 us  [on_device(): lax.all_to_all(grads, 'dev', split_axis=0, concat_axis=0, tiled=True)]
    dot_general x2 -> x0, matrix products: 11.7 us -> none  [the longest x1 6.8 us: on_device(): lax.dot_general(total, forward, (((1,), (1,)), ((), ())), preferred_eleme...]
    ppermute x23 -> x20, waiting for transfers between devices: 31.7 us -> 38.5 us  [the longest x10 22.1 us: y_move(): return lax.ppermute(value, ('region', 'dev'), y_pairs(step, regions, shift))]
    pallas_call x3 -> x6, Pallas kernels: 13.9 us -> 19.1 us  [the longest x1 9.83 us: on_device(): pl.pallas_call(pair_kernel, grid=(3,), out_shape=[shape((pairs, 1), F32),...]
    all_to_all x1, starting transfers between devices: 3.55 us -> 7.39 us  [on_device(): lax.all_to_all(grads, 'dev', split_axis=0, concat_axis=0, tiled=True)]
    unnamed x12 -> x22, local copies, waits for them, and re-layouts: 0.04 us -> 2.31 us
  transfers between devices with their start and end apart: 24 -> 21, of which waited for: 11 -> 9; matrix products, arithmetic and copies ran while one was open for 5% -> 1% of each run, Pallas kernels for 0% -> 4%
where the time goes in v2:
time: 151 us
  waiting for transfers between devices  76.6 us (51%)
  starting transfers between devices  49.9 us (33%)
  Pallas kernels  19.1 us (13%)
  local copies, waits for them, and re-layouts  2.49 us (2%)
  other arithmetic  2.05 us (1%)
    all_to_all x1, waiting for transfers between devices, on_device(): lax.all_to_all(grads, 'dev', split_axis=0, concat_axis=0, tiled=True)  38 us
    ppermute x10, waiting for transfers between devices, y_move(): return lax.ppermute(value, ('region', 'dev'), y_pairs(step, regions, shift))  22.1 us
    ppermute x10, starting transfers between devices, y_move(): return lax.ppermute(value, ('region', 'dev'), y_pairs(step, regions, shift))  19.7 us
    ppermute x8, starting transfers between devices, z_move(): return lax.ppermute(value, 'dev', z_pairs(step))  15.6 us
    ppermute x8, waiting for transfers between devices, z_move(): return lax.ppermute(value, 'dev', z_pairs(step))  14.5 us
    pallas_call x1, Pallas kernels, on_device(): pl.pallas_call(pair_kernel, grid=(3,), out_shape=[shape((pairs, 1), F32),...  9.83 us
    all_to_all x1, starting transfers between devices, on_device(): lax.all_to_all(grads, 'dev', split_axis=0, concat_axis=0, tiled=True)  7.39 us
    ppermute x1, starting transfers between devices, on_device(): lax.ppermute(far_rows.T, 'region', [(r, r + 1) for r in range(regions - 1)])  4.51 us
  transfers between devices with their start and end apart: 21, of which 9 were waited for; matrix products, arithmetic and copies ran while one was open for 1% of the time, Pallas kernels for 4%

profile of v2, /device:TPU:1, one launch (start us, length us, event | category | flops | bytes accessed | tf_op | source)
XLA Modules:
  0.0 151.0 jit_solution(8276405747001101986)
XLA Ops:
  0.6 4.5 %collective-permute-start = (s32[4,32]{1,0:T(4,128)}, s32[4,32]{1,0:T(4,128)S(1)}, u32[]{:S(2)}, u32[]{:S(2)}) collective-permute-start(s32[4,32]{1,0:T(4,128)} %bitcast.19), channel_id=1, source_target_pairs={{0,32},{32,64},{64,96},{96,128},{128,160},{160,192},{192,224},{1,3... | collective-permute-start | bytes 1544 | tf_op jit(solution)/shard_map/ppermute | solution.py:235
  5.1 0.7 convert_bitcast_fusion
  5.8 4.0 %shard_map.122 = bf16[7,16,1024]{2,1,0:T(8,128)(2,1)} custom-call(bf16[3,16,4096]{2,1,0:T(8,128)(2,1)} %bitcast.16, bf16[3,16,4096]{2,1,0:T(8,128)(2,1)} %bitcast.17, bf16[4,1024,256]{2,1,0:T(8,128)(2,1)} %constant.16.clone.table_ref), custom_call_target="tpu_custom_call" | custom-call | flops 805306368 | bytes 3145728 | tf_op jit(solution)/shard_map/pallas_call | solution.py:237
  9.8 0.0 collective-permute-done
  9.8 0.6 fusion.7.refs_0_
  10.5 5.6 %collective-permute-start.4 = (bf16[7,16,1024]{2,1,0:T(8,128)(2,1)}, bf16[7,16,1024]{2,1,0:T(8,128)(2,1)S(1)}, u32[]{:S(2)}, u32[]{:S(2)}) collective-permute-start(bf16[7,16,1024]{2,1,0:T(8,128)(2,1)} %fusion.7.refs_0_), channel_id=1, source_target_pairs={{0,28},{1,29},{2,30},{3,31},{4,0},{5,1},{6,2},{7,3},{8,4},{9,5},{1... | collective-permute-start | bytes 688136 | tf_op jit(solution)/shard_map/ppermute | solution.py:230
  16.0 4.9 %collective-permute-done.4.refs_2_ = bf16[7,16,1024]{2,1,0:T(8,128)(2,1)S(1)} collective-permute-done((bf16[7,16,1024]{2,1,0:T(8,128)(2,1)}, bf16[7,16,1024]{2,1,0:T(8,128)(2,1)S(1)}, u32[]{:S(2)}, u32[]{:S(2)}) %collective-permute-start.4) | collective-permute-done | bytes 229408 | tf_op jit(solution)/shard_map/ppermute | solution.py:230
  21.0 3.0 %collective-permute-start.5 = (bf16[7,16,1024]{2,1,0:T(8,128)(2,1)S(1)}, bf16[7,16,1024]{2,1,0:T(8,128)(2,1)S(1)}, u32[]{:S(2)}, u32[]{:S(2)}) collective-permute-start(bf16[7,16,1024]{2,1,0:T(8,128)(2,1)S(1)} %collective-permute-done.4.refs_2_), channel_id=1, source_target_pairs={{0,28},{1,29},{2,30},{3,31},{4,0},{5,1},{6,2},{7,3},{8,4},{9,5},{1... | collective-permute-start | bytes 688136 | tf_op jit(solution)/shard_map/ppermute | solution.py:230
  24.0 0.3 collective-permute-done.1.refs_1_
  24.3 0.0 collective-permute-start.2
  24.3 4.9 %collective-permute-done.5.refs_4_ = bf16[7,16,1024]{2,1,0:T(8,128)(2,1)S(1)} collective-permute-done((bf16[7,16,1024]{2,1,0:T(8,128)(2,1)S(1)}, bf16[7,16,1024]{2,1,0:T(8,128)(2,1)S(1)}, u32[]{:S(2)}, u32[]{:S(2)}) %collective-permute-start.5) | collective-permute-done | bytes 229408 | tf_op jit(solution)/shard_map/ppermute | solution.py:230
  29.1 3.4 %collective-permute-start.6 = (bf16[7,16,1024]{2,1,0:T(8,128)(2,1)S(1)}, bf16[7,16,1024]{2,1,0:T(8,128)(2,1)S(1)}, u32[]{:S(2)}, u32[]{:S(2)}) collective-permute-start(bf16[7,16,1024]{2,1,0:T(8,128)(2,1)S(1)} %collective-permute-done.5.refs_4_), channel_id=1, source_target_pairs={{0,28},{1,29},{2,30},{3,31},{4,0},{5,1},{6,2},{7,3},{8,4},{9,5},{1... | collective-permute-start | bytes 688136 | tf_op jit(solution)/shard_map/ppermute | solution.py:230
  32.5 0.0 collective-permute-done.2.refs_3_
  32.5 0.0 collective-permute-start.3
  32.5 4.3 %collective-permute-done.6.refs_6_ = bf16[7,16,1024]{2,1,0:T(8,128)(2,1)S(1)} collective-permute-done((bf16[7,16,1024]{2,1,0:T(8,128)(2,1)S(1)}, bf16[7,16,1024]{2,1,0:T(8,128)(2,1)S(1)}, u32[]{:S(2)}, u32[]{:S(2)}) %collective-permute-start.6) | collective-permute-done | bytes 229408 | tf_op jit(solution)/shard_map/ppermute | solution.py:230
  36.8 3.5 %collective-permute-start.8 = (bf16[4,16,1024]{2,1,0:T(8,128)(2,1)S(1)}, bf16[4,16,1024]{2,1,0:T(8,128)(2,1)S(1)}, u32[]{:S(2)}, u32[]{:S(2)}) collective-permute-start(bf16[4,16,1024]{2,1,0:T(8,128)(2,1)S(1)} %slice.9), channel_id=1, source_target_pairs={{0,28},{1,29},{2,30},{3,31},{4,0},{5,1},{6,2},{7,3},{8,4},{9,5},{1... | collective-permute-start | bytes 393224 | tf_op jit(solution)/shard_map/ppermute | solution.py:230
  40.3 0.9 copy-done
  41.3 0.0 copy-start.3
  41.3 0.6 shard_map.123
  41.8 0.0 collective-permute-done.3.refs_5_
  41.9 0.1 collective-permute-start.7
  41.9 3.0 %collective-permute-start.11 = (bf16[2,3,16,1024]{3,2,1,0:T(8,128)(2,1)S(1)}, bf16[2,3,16,1024]{3,2,1,0:T(8,128)(2,1)S(1)}, u32[]{:S(2)}, u32[]{:S(2)}) collective-permute-start(bf16[2,3,16,1024]{3,2,1,0:T(8,128)(2,1)S(1)} %get-tuple-element.26), channel_id=1, source_target_pairs={{0,2},{1,3},{2,0},{3,1},{4,6},{5,7},{6,4},{7,5},{8,10},{9,11},{10,... | collective-permute-start | bytes 589832 | tf_op jit(solution)/shard_map/ppermute | solution.py:233
  45.0 0.8 collective-permute-start.13
  45.7 0.7 collective-permute-start.9
  46.4 0.2 collective-permute-done.7
  46.6 0.0 collective-permute-done.8
  46.7 1.2 shard_map.124
  47.8 1.4 collective-permute-start.10
  49.2 5.1 %collective-permute-start.15 = (bf16[2,3,32,1024]{3,2,1,0:T(8,128)(2,1)S(1)}, bf16[2,3,32,1024]{3,2,1,0:T(8,128)(2,1)S(1)}, u32[]{:S(2)}, u32[]{:S(2)}) collective-permute-start(bf16[2,3,32,1024]{3,2,1,0:T(8,128)(2,1)S(1)} %get-tuple-element.30), channel_id=1, source_target_pairs={{32,0},{33,1},{34,2},{35,3},{36,4},{37,5},{38,6},{39,7},{40,8},{41... | collective-permute-start | bytes 1179656 | tf_op jit(solution)/shard_map/ppermute | solution.py:233
  54.4 0.0 collective-permute-done.11.refs_4_
  54.4 2.5 %collective-permute-start.16 = (bf16[2,3,32,1024]{3,2,1,0:T(8,128)(2,1)S(1)}, bf16[2,3,32,1024]{3,2,1,0:T(8,128)(2,1)S(1)}, u32[]{:S(2)}, u32[]{:S(2)}) collective-permute-start(bf16[2,3,32,1024]{3,2,1,0:T(8,128)(2,1)S(1)} %get-tuple-element.31), channel_id=1, source_target_pairs={{32,1},{33,2},{34,3},{35,0},{36,5},{37,6},{38,7},{39,4},{40,9},{41... | collective-permute-start | bytes 1179656 | tf_op jit(solution)/shard_map/ppermute | solution.py:233
  56.9 2.3 %collective-permute-start.12 = (bf16[2,3,16,1024]{3,2,1,0:T(8,128)(2,1)S(1)}, bf16[2,3,16,1024]{3,2,1,0:T(8,128)(2,1)S(1)}, u32[]{:S(2)}, u32[]{:S(2)}) collective-permute-start(bf16[2,3,16,1024]{3,2,1,0:T(8,128)(2,1)S(1)} %get-tuple-element.27), channel_id=1, source_target_pairs={{0,2},{1,3},{2,0},{3,1},{4,6},{5,7},{6,4},{7,5},{8,10},{9,11},{10,... | collective-permute-start | bytes 589832 | tf_op jit(solution)/shard_map/ppermute | solution.py:233
  59.2 1.9 %collective-permute-start.17 = (bf16[2,3,32,1024]{3,2,1,0:T(8,128)(2,1)S(1)}, bf16[2,3,32,1024]{3,2,1,0:T(8,128)(2,1)S(1)}, u32[]{:S(2)}, u32[]{:S(2)}) collective-permute-start(bf16[2,3,32,1024]{3,2,1,0:T(8,128)(2,1)S(1)} %get-tuple-element.32), channel_id=1, source_target_pairs={{32,2},{33,3},{34,0},{35,1},{36,6},{37,7},{38,4},{39,5},{40,10},{4... | collective-permute-start | bytes 1179656 | tf_op jit(solution)/shard_map/ppermute | solution.py:233
  61.2 1.9 %collective-permute-start.18 = (bf16[2,3,32,1024]{3,2,1,0:T(8,128)(2,1)S(1)}, bf16[2,3,32,1024]{3,2,1,0:T(8,128)(2,1)S(1)}, u32[]{:S(2)}, u32[]{:S(2)}) collective-permute-start(bf16[2,3,32,1024]{3,2,1,0:T(8,128)(2,1)S(1)} %get-tuple-element.33), channel_id=1, source_target_pairs={{32,3},{33,0},{34,1},{35,2},{36,7},{37,4},{38,5},{39,6},{40,11},{4... | collective-permute-start | bytes 1179656 | tf_op jit(solution)/shard_map/ppermute | solution.py:233
  63.1 13.6 %collective-permute-done.12.refs_5_ = bf16[2,3,16,1024]{3,2,1,0:T(8,128)(2,1)S(1)} collective-permute-done((bf16[2,3,16,1024]{3,2,1,0:T(8,128)(2,1)S(1)}, bf16[2,3,16,1024]{3,2,1,0:T(8,128)(2,1)S(1)}, u32[]{:S(2)}, u32[]{:S(2)}) %collective-permute-start.12) | collective-permute-done | bytes 196640 | tf_op jit(solution)/shard_map/ppermute | solution.py:233
  76.7 8.5 %collective-permute-done.14.refs_7_ = bf16[2,3,16,1024]{3,2,1,0:T(8,128)(2,1)S(1)} collective-permute-done((bf16[2,3,16,1024]{3,2,1,0:T(8,128)(2,1)S(1)}, bf16[2,3,16,1024]{3,2,1,0:T(8,128)(2,1)S(1)}, u32[]{:S(2)}, u32[]{:S(2)}) %collective-permute-start.14) | collective-permute-done | bytes 196640 | tf_op jit(solution)/shard_map/ppermute | solution.py:233
  85.2 9.8 %shard_map.125 = (f32[256,1]{1,0:T(8,128)S(1)}, bf16[32,48,512]{2,1,0:T(8,128)(2,1)}) custom-call(s32[4,256]{1,0:T(4,128)S(1)} %pad_add_fusion.1.slots_ref, bf16[1024,512]{1,0:T(8,128)(2,1)S(1)} %copy-done.3, bf16[2,3,16,1024]{3,2,1,0:T(8,128)(2,1)S(1)} %get-tuple-element.21.refs_0_, bf16[2,3,16,1024]{3,2,1,0:T(8,128)(2,1)S(1)} %get-tuple-element.23.refs_1_, ...), custom_call_target="tpu_custom_call" | custom-call | flops 9663676416 | bytes 9437184 | tf_op jit(solution)/shard_map/pallas_call | solution.py:277
  95.1 7.4 %all-to-all-start = ((bf16[32,48,512]{2,1,0:T(8,128)(2,1)}), bf16[32,48,512]{2,1,0:T(8,128)(2,1)S(1)}, u32[]{:S(2)}, u32[]{:S(2)}) async-start(bf16[32,48,512]{2,1,0:T(8,128)(2,1)} %get-tuple-element.34), calls=%async_computation | async-start | bytes 3145728 | tf_op jit(solution)/shard_map/all_to_all | solution.py:295
  102.5 0.1 copy.14
  102.6 0.1 reshape.13.held_ref
  102.7 38.0 %all-to-all-done.grad_ref = bf16[32,48,512]{2,1,0:T(8,128)(2,1)S(1)} async-done(((bf16[32,48,512]{2,1,0:T(8,128)(2,1)}), bf16[32,48,512]{2,1,0:T(8,128)(2,1)S(1)}, u32[]{:S(2)}, u32[]{:S(2)}) %all-to-all-start) | async-done | bytes 1572896 | tf_op jit(solution)/shard_map/all_to_all | solution.py:295
  140.7 0.8 shard_map.126
  141.5 0.7 copy-done.2
  142.2 2.8 %collective-permute-start.19 = (f32[48,1024]{1,0:T(8,128)S(1)}, f32[48,1024]{1,0:T(8,128)S(1)}, u32[]{:S(2)}, u32[]{:S(2)}) collective-permute-start(f32[48,1024]{1,0:T(8,128)S(1)} %get-tuple-element.36), channel_id=1, source_target_pairs={{0,32},{32,64},{64,96},{96,128},{128,160},{160,192},{192,224},{1,3... | collective-permute-start | bytes 589832 | tf_op jit(solution)/shard_map/ppermute | solution.py:310
  145.0 0.7 reduce
  145.7 1.9 %collective-permute-done.19.far_ref = f32[48,1024]{1,0:T(8,128)S(1)} collective-permute-done((f32[48,1024]{1,0:T(8,128)S(1)}, f32[48,1024]{1,0:T(8,128)S(1)}, u32[]{:S(2)}, u32[]{:S(2)}) %collective-permute-start.19) | collective-permute-done | bytes 196640 | tf_op jit(solution)/shard_map/ppermute | solution.py:310
  147.6 0.7 copy-done.4
  148.3 2.7 %shard_map.127 = bf16[48,4096]{1,0:T(8,128)(2,1)} custom-call(f32[48,1024]{1,0:T(8,128)} %copy-done.2, f32[48,1024]{1,0:T(8,128)} %copy-done.4, bf16[4,256,1024]{2,1,0:T(8,128)(2,1)} %constant.17.clone.table_ref), custom_call_target="tpu_custom_call" | custom-call | flops 402653184 | bytes 3145728 | tf_op jit(solution)/shard_map/pallas_call | solution.py:312
  (35 shorter events, 0.1 us)
Async XLA Ops:
  0.6 9.2 %collective-permute-start = (s32[4,32]{1,0:T(4,128)}, s32[4,32]{1,0:T(4,128)S(1)}, u32[]{:S(2)}, u32[]{:S(2)}) collective-permute-start(s32[4,32]{1,0:T(4,128)} %bitcast.19), channel_id=1, source_target_pairs={{0,32},{32,64},{64,96},{96,128},{128,160},{160,192},{192,224},{1,3... | collective-permute-start | bytes 1544 | tf_op jit(solution)/shard_map/ppermute | solution.py:235
  10.5 36.2 %copy-start.1 = (bf16[7,16,1024]{2,1,0:T(8,128)(2,1)S(1)}, bf16[7,16,1024]{2,1,0:T(8,128)(2,1)}, u32[]{:S(2)}) copy-start(bf16[7,16,1024]{2,1,0:T(8,128)(2,1)} %fusion.7.refs_0_) | copy-start | bytes 688132
  10.5 10.5 %collective-permute-start.4 = (bf16[7,16,1024]{2,1,0:T(8,128)(2,1)}, bf16[7,16,1024]{2,1,0:T(8,128)(2,1)S(1)}, u32[]{:S(2)}, u32[]{:S(2)}) collective-permute-start(bf16[7,16,1024]{2,1,0:T(8,128)(2,1)} %fusion.7.refs_0_), channel_id=1, source_target_pairs={{0,28},{1,29},{2,30},{3,31},{4,0},{5,1},{6,2},{7,3},{8,4},{9,5},{1... | collective-permute-start | bytes 688136 | tf_op jit(solution)/shard_map/ppermute | solution.py:230
  16.0 8.2 %collective-permute-start.1 = (bf16[7,16,1024]{2,1,0:T(8,128)(2,1)}, bf16[7,16,1024]{2,1,0:T(8,128)(2,1)S(1)}, u32[]{:S(2)}, u32[]{:S(2)}) collective-permute-start(bf16[7,16,1024]{2,1,0:T(8,128)(2,1)} %fusion.7.refs_0_), channel_id=1, source_target_pairs={{0,4},{1,5},{2,6},{3,7},{4,8},{5,9},{6,10},{7,11},{8,12},{9,13},{1... | collective-permute-start | bytes 688136 | tf_op jit(solution)/shard_map/ppermute | solution.py:230
  21.0 8.1 %collective-permute-start.5 = (bf16[7,16,1024]{2,1,0:T(8,128)(2,1)S(1)}, bf16[7,16,1024]{2,1,0:T(8,128)(2,1)S(1)}, u32[]{:S(2)}, u32[]{:S(2)}) collective-permute-start(bf16[7,16,1024]{2,1,0:T(8,128)(2,1)S(1)} %collective-permute-done.4.refs_2_), channel_id=1, source_target_pairs={{0,28},{1,29},{2,30},{3,31},{4,0},{5,1},{6,2},{7,3},{8,4},{9,5},{1... | collective-permute-start | bytes 688136 | tf_op jit(solution)/shard_map/ppermute | solution.py:230
  24.3 8.3 %collective-permute-start.2 = (bf16[7,16,1024]{2,1,0:T(8,128)(2,1)S(1)}, bf16[7,16,1024]{2,1,0:T(8,128)(2,1)S(1)}, u32[]{:S(2)}, u32[]{:S(2)}) collective-permute-start(bf16[7,16,1024]{2,1,0:T(8,128)(2,1)S(1)} %collective-permute-done.1.refs_1_), channel_id=1, source_target_pairs={{0,4},{1,5},{2,6},{3,7},{4,8},{5,9},{6,10},{7,11},{8,12},{9,13},{1... | collective-permute-start | bytes 688136 | tf_op jit(solution)/shard_map/ppermute | solution.py:230
  29.1 7.7 %collective-permute-start.6 = (bf16[7,16,1024]{2,1,0:T(8,128)(2,1)S(1)}, bf16[7,16,1024]{2,1,0:T(8,128)(2,1)S(1)}, u32[]{:S(2)}, u32[]{:S(2)}) collective-permute-start(bf16[7,16,1024]{2,1,0:T(8,128)(2,1)S(1)} %collective-permute-done.5.refs_4_), channel_id=1, source_target_pairs={{0,28},{1,29},{2,30},{3,31},{4,0},{5,1},{6,2},{7,3},{8,4},{9,5},{1... | collective-permute-start | bytes 688136 | tf_op jit(solution)/shard_map/ppermute | solution.py:230
  32.5 9.3 %collective-permute-start.3 = (bf16[7,16,1024]{2,1,0:T(8,128)(2,1)S(1)}, bf16[7,16,1024]{2,1,0:T(8,128)(2,1)S(1)}, u32[]{:S(2)}, u32[]{:S(2)}) collective-permute-start(bf16[7,16,1024]{2,1,0:T(8,128)(2,1)S(1)} %collective-permute-done.2.refs_3_), channel_id=1, source_target_pairs={{0,4},{1,5},{2,6},{3,7},{4,8},{5,9},{6,10},{7,11},{8,12},{9,13},{1... | collective-permute-start | bytes 688136 | tf_op jit(solution)/shard_map/ppermute | solution.py:230
  36.8 9.8 %collective-permute-start.8 = (bf16[4,16,1024]{2,1,0:T(8,128)(2,1)S(1)}, bf16[4,16,1024]{2,1,0:T(8,128)(2,1)S(1)}, u32[]{:S(2)}, u32[]{:S(2)}) collective-permute-start(bf16[4,16,1024]{2,1,0:T(8,128)(2,1)S(1)} %slice.9), channel_id=1, source_target_pairs={{0,28},{1,29},{2,30},{3,31},{4,0},{5,1},{6,2},{7,3},{8,4},{9,5},{1... | collective-permute-start | bytes 393224 | tf_op jit(solution)/shard_map/ppermute | solution.py:230
  40.3 0.9 copy-start
  41.2 35.4 %copy-start.7 = (s32[256]{0:T(256)S(1)}, s32[256]{0:T(256)}, u32[]{:S(2)}) copy-start(s32[256]{0:T(256)} %param.18) | copy-start | bytes 3076
  41.2 35.4 %copy-start.8 = (s32[256]{0:T(256)S(1)}, s32[256]{0:T(256)}, u32[]{:S(2)}) copy-start(s32[256]{0:T(256)} %param.17) | copy-start | bytes 3076
  41.3 35.4 %copy-start.9 = (s32[256]{0:T(256)S(1)}, s32[256]{0:T(256)}, u32[]{:S(2)}) copy-start(s32[256]{0:T(256)} %param.16) | copy-start | bytes 3076
  41.3 35.4 %copy-start.10 = (s32[256]{0:T(256)S(1)}, s32[256]{0:T(256)}, u32[]{:S(2)}) copy-start(s32[256]{0:T(256)} %param.15) | copy-start | bytes 3076
  41.3 44.0 %copy-start.3 = (bf16[1024,512]{1,0:T(8,128)(2,1)S(1)}, bf16[1024,512]{1,0:T(8,128)(2,1)}, u32[]{:S(2)}) copy-start(bf16[1024,512]{1,0:T(8,128)(2,1)} %constant.18.clone.lag_ref) | copy-start | bytes 3145732
  41.9 4.8 %collective-permute-start.7 = (bf16[3,16,1024]{2,1,0:T(8,128)(2,1)S(1)}, bf16[3,16,1024]{2,1,0:T(8,128)(2,1)S(1)}, u32[]{:S(2)}, u32[]{:S(2)}) collective-permute-start(bf16[3,16,1024]{2,1,0:T(8,128)(2,1)S(1)} %slice.8), channel_id=1, source_target_pairs={{0,4},{1,5},{2,6},{3,7},{4,8},{5,9},{6,10},{7,11},{8,12},{9,13},{1... | collective-permute-start | bytes 294920 | tf_op jit(solution)/shard_map/ppermute | solution.py:230
  41.9 12.5 %collective-permute-start.11 = (bf16[2,3,16,1024]{3,2,1,0:T(8,128)(2,1)S(1)}, bf16[2,3,16,1024]{3,2,1,0:T(8,128)(2,1)S(1)}, u32[]{:S(2)}, u32[]{:S(2)}) collective-permute-start(bf16[2,3,16,1024]{3,2,1,0:T(8,128)(2,1)S(1)} %get-tuple-element.26), channel_id=1, source_target_pairs={{0,2},{1,3},{2,0},{3,1},{4,6},{5,7},{6,4},{7,5},{8,10},{9,11},{10,... | collective-permute-start | bytes 589832 | tf_op jit(solution)/shard_map/ppermute | solution.py:233
  45.0 11.9 %collective-permute-start.13 = (bf16[2,3,16,1024]{3,2,1,0:T(8,128)(2,1)S(1)}, bf16[2,3,16,1024]{3,2,1,0:T(8,128)(2,1)S(1)}, u32[]{:S(2)}, u32[]{:S(2)}) collective-permute-start(bf16[2,3,16,1024]{3,2,1,0:T(8,128)(2,1)S(1)} %get-tuple-element.28), channel_id=1, source_target_pairs={{0,3},{1,0},{2,1},{3,2},{4,7},{5,4},{6,5},{7,6},{8,11},{9,8},{10,9... | collective-permute-start | bytes 589832 | tf_op jit(solution)/shard_map/ppermute | solution.py:233
  45.7 13.5 %collective-permute-start.9 = (bf16[2,3,16,1024]{3,2,1,0:T(8,128)(2,1)S(1)}, bf16[2,3,16,1024]{3,2,1,0:T(8,128)(2,1)S(1)}, u32[]{:S(2)}, u32[]{:S(2)}) collective-permute-start(bf16[2,3,16,1024]{3,2,1,0:T(8,128)(2,1)S(1)} %get-tuple-element.24), channel_id=1, source_target_pairs={{0,1},{1,2},{2,3},{3,0},{4,5},{5,6},{6,7},{7,4},{8,9},{9,10},{10,1... | collective-permute-start | bytes 589832 | tf_op jit(solution)/shard_map/ppermute | solution.py:233
  47.8 13.3 %collective-permute-start.10 = (bf16[2,3,16,1024]{3,2,1,0:T(8,128)(2,1)S(1)}, bf16[2,3,16,1024]{3,2,1,0:T(8,128)(2,1)S(1)}, u32[]{:S(2)}, u32[]{:S(2)}) collective-permute-start(bf16[2,3,16,1024]{3,2,1,0:T(8,128)(2,1)S(1)} %get-tuple-element.25), channel_id=1, source_target_pairs={{0,1},{1,2},{2,3},{3,0},{4,5},{5,6},{6,7},{7,4},{8,9},{9,10},{10,1... | collective-permute-start | bytes 589832 | tf_op jit(solution)/shard_map/ppermute | solution.py:233
  49.2 36.0 %collective-permute-start.15 = (bf16[2,3,32,1024]{3,2,1,0:T(8,128)(2,1)S(1)}, bf16[2,3,32,1024]{3,2,1,0:T(8,128)(2,1)S(1)}, u32[]{:S(2)}, u32[]{:S(2)}) collective-permute-start(bf16[2,3,32,1024]{3,2,1,0:T(8,128)(2,1)S(1)} %get-tuple-element.30), channel_id=1, source_target_pairs={{32,0},{33,1},{34,2},{35,3},{36,4},{37,5},{38,6},{39,7},{40,8},{41... | collective-permute-start | bytes 1179656 | tf_op jit(solution)/shard_map/ppermute | solution.py:233
  54.4 30.8 %collective-permute-start.16 = (bf16[2,3,32,1024]{3,2,1,0:T(8,128)(2,1)S(1)}, bf16[2,3,32,1024]{3,2,1,0:T(8,128)(2,1)S(1)}, u32[]{:S(2)}, u32[]{:S(2)}) collective-permute-start(bf16[2,3,32,1024]{3,2,1,0:T(8,128)(2,1)S(1)} %get-tuple-element.31), channel_id=1, source_target_pairs={{32,1},{33,2},{34,3},{35,0},{36,5},{37,6},{38,7},{39,4},{40,9},{41... | collective-permute-start | bytes 1179656 | tf_op jit(solution)/shard_map/ppermute | solution.py:233
  56.9 19.8 %collective-permute-start.12 = (bf16[2,3,16,1024]{3,2,1,0:T(8,128)(2,1)S(1)}, bf16[2,3,16,1024]{3,2,1,0:T(8,128)(2,1)S(1)}, u32[]{:S(2)}, u32[]{:S(2)}) collective-permute-start(bf16[2,3,16,1024]{3,2,1,0:T(8,128)(2,1)S(1)} %get-tuple-element.27), channel_id=1, source_target_pairs={{0,2},{1,3},{2,0},{3,1},{4,6},{5,7},{6,4},{7,5},{8,10},{9,11},{10,... | collective-permute-start | bytes 589832 | tf_op jit(solution)/shard_map/ppermute | solution.py:233
  59.2 26.0 %collective-permute-start.17 = (bf16[2,3,32,1024]{3,2,1,0:T(8,128)(2,1)S(1)}, bf16[2,3,32,1024]{3,2,1,0:T(8,128)(2,1)S(1)}, u32[]{:S(2)}, u32[]{:S(2)}) collective-permute-start(bf16[2,3,32,1024]{3,2,1,0:T(8,128)(2,1)S(1)} %get-tuple-element.32), channel_id=1, source_target_pairs={{32,2},{33,3},{34,0},{35,1},{36,6},{37,7},{38,4},{39,5},{40,10},{4... | collective-permute-start | bytes 1179656 | tf_op jit(solution)/shard_map/ppermute | solution.py:233
  61.2 24.1 %collective-permute-start.18 = (bf16[2,3,32,1024]{3,2,1,0:T(8,128)(2,1)S(1)}, bf16[2,3,32,1024]{3,2,1,0:T(8,128)(2,1)S(1)}, u32[]{:S(2)}, u32[]{:S(2)}) collective-permute-start(bf16[2,3,32,1024]{3,2,1,0:T(8,128)(2,1)S(1)} %get-tuple-element.33), channel_id=1, source_target_pairs={{32,3},{33,0},{34,1},{35,2},{36,7},{37,4},{38,5},{39,6},{40,11},{4... | collective-permute-start | bytes 1179656 | tf_op jit(solution)/shard_map/ppermute | solution.py:233
  76.7 8.5 %collective-permute-start.14 = (bf16[2,3,16,1024]{3,2,1,0:T(8,128)(2,1)S(1)}, bf16[2,3,16,1024]{3,2,1,0:T(8,128)(2,1)S(1)}, u32[]{:S(2)}, u32[]{:S(2)}) collective-permute-start(bf16[2,3,16,1024]{3,2,1,0:T(8,128)(2,1)S(1)} %get-tuple-element.29), channel_id=1, source_target_pairs={{0,3},{1,0},{2,1},{3,2},{4,7},{5,4},{6,5},{7,6},{8,11},{9,8},{10,9... | collective-permute-start | bytes 589832 | tf_op jit(solution)/shard_map/ppermute | solution.py:233
  95.1 7.4 %copy-start.6 = (s32[32,4]{0,1:T(4,128)S(1)}, s32[32,4]{0,1:T(4,128)}, u32[]{:S(2)}) copy-start(s32[32,4]{0,1:T(4,128)} %param.14) | copy-start | bytes 1540
  95.1 7.4 %copy-start.5 = (s32[32,4]{0,1:T(4,128)S(1)}, s32[32,4]{0,1:T(4,128)}, u32[]{:S(2)}) copy-start(s32[32,4]{0,1:T(4,128)} %param.13) | copy-start | bytes 1540
  95.1 45.7 %all-to-all-start = ((bf16[32,48,512]{2,1,0:T(8,128)(2,1)}), bf16[32,48,512]{2,1,0:T(8,128)(2,1)S(1)}, u32[]{:S(2)}, u32[]{:S(2)}) async-start(bf16[32,48,512]{2,1,0:T(8,128)(2,1)} %get-tuple-element.34), calls=%async_computation | async-start | bytes 3145728 | tf_op jit(solution)/shard_map/all_to_all | solution.py:295
  141.5 0.7 copy-start.2
  142.2 5.4 %collective-permute-start.19 = (f32[48,1024]{1,0:T(8,128)S(1)}, f32[48,1024]{1,0:T(8,128)S(1)}, u32[]{:S(2)}, u32[]{:S(2)}) collective-permute-start(f32[48,1024]{1,0:T(8,128)S(1)} %get-tuple-element.36), channel_id=1, source_target_pairs={{0,32},{32,64},{64,96},{96,128},{128,160},{160,192},{192,224},{1,3... | collective-permute-start | bytes 589832 | tf_op jit(solution)/shard_map/ppermute | solution.py:310
  147.6 0.7 copy-start.4

commit v3 on v2

--- a/solution.py
+++ b/solution.py
@@ -64,13 +64,24 @@
     return jnp.dot(a, b, preferred_element_type=F32)
 
 
-def forward_kernel(synthetic_ref, observed_ref, table_ref, out_ref):
+def forward_kernel(synthetic_ref, observed_ref, far_table_ref, out_ref, held, table_ref, done):
     quarter = synthetic_ref.shape[2] // RADIX
     group = F // RADIX
-    out_ref[Q] = jnp.zeros((ROWS, 2 * F), BF)
-    traces = [ref[c] for ref in (synthetic_ref, observed_ref) for c in range(3)]
-    traces = jnp.concatenate(traces, 0)
+    copies = [
+        pltpu.make_async_copy(ref, held.at[n], done.at[n])
+        for n, ref in enumerate((synthetic_ref, observed_ref))
+    ]
+    copies += [
+        pltpu.make_async_copy(far_table_ref.at[c], table_ref.at[c], done.at[2 + c])
+        for c in range(RADIX)
+    ]
+    for copy in copies:
+        copy.start()
+    copies[0].wait()
+    copies[1].wait()
+    traces = jnp.concatenate([held[n, c] for n in range(2) for c in range(3)], 0)
     for c in range(RADIX):
+        copies[2 + c].wait()
         sums = [dot(traces[:, j * quarter : (j + 1) * quarter], table_ref[c]) for j in range(RADIX)]
         (r0, i0), (r1, i1), (r2, i2), (r3, i3) = [(p[:, :group], p[:, group:]) for p in sums]
         if c == 0:
@@ -86,12 +97,24 @@
         out_ref[:Q, :, F + at : F + at + group] = imag.astype(BF).reshape(Q, ROWS, group)
 
 
+def index_kernel(near_ref, far_ref, _, out_ref):
+    cap, peers = near_ref.shape
+    both = jnp.concatenate([near_ref[...], far_ref[...]], 0).astype(F32)
+    both = jnp.concatenate([both, jnp.zeros((2 * cap, 4 * peers - peers), F32)], 1)
+    out_ref[Q, :, : 4 * peers] = jnp.concatenate([both, jnp.zeros_like(both)], 0).astype(BF)
+
+
+def fetch_kernel(source_ref, _, out_ref, done):
+    copy = pltpu.make_async_copy(source_ref, out_ref, done)
+    copy.start()
+    copy.wait()
+
+
 def inverse_kernel(near_ref, far_ref, table_ref, out_ref):
     rows = out_ref.shape[0]
     quarter = out_ref.shape[1] // RADIX
-    part = table_ref.shape[2]
     group = F // RADIX
-    total = (near_ref[...] + far_ref[...]).astype(BF)
+    total = (near_ref[...] + far_ref[...].astype(F32)).astype(BF)
     real = [total[:, c * group : (c + 1) * group] for c in range(RADIX)]
     imag = [total[:, F + c * group : F + (c + 1) * group] for c in range(RADIX)]
     plain = [jnp.concatenate([real[c], imag[c]], 1) for c in range(RADIX)]
@@ -100,11 +123,10 @@
     one = dot(jnp.concatenate([plain[1], turned[1]], 0), table_ref[1])
     three = dot(jnp.concatenate([plain[3], turned[3]], 0), table_ref[3])
     p1, q1, p3, q3 = one[:rows], one[rows:], three[:rows], three[rows:]
-    parts = (p0 + p2) + (p1 + p3), (p0 - p2) + (q1 - q3), (p0 + p2) - (p1 + p3), (p0 - p2) - (q1 - q3)
-    start = pl.program_id(0) * part
-    for j, value in enumerate(parts):
-        at = pl.multiple_of(start + j * quarter, part)
-        out_ref[:, pl.ds(at, part)] = value.astype(BF)
+    out_ref[:, :quarter] = ((p0 + p2) + (p1 + p3)).astype(BF)
+    out_ref[:, quarter : 2 * quarter] = ((p0 - p2) + (q1 - q3)).astype(BF)
+    out_ref[:, 2 * quarter : 3 * quarter] = ((p0 + p2) - (p1 + p3)).astype(BF)
+    out_ref[:, 3 * quarter :] = ((p0 - p2) - (q1 - q3)).astype(BF)
 
 
 def position():
@@ -194,7 +216,7 @@
     pick = (iota((4 * ROWS, rows), 0) == held_ref[...]).astype(BF)
     total = dot(pick, grad_ref[...].reshape(rows, F))
     near_ref[...] = jnp.concatenate([total[:ROWS], total[2 * ROWS : 3 * ROWS]], 1)
-    far_ref[...] = jnp.concatenate([total[ROWS : 2 * ROWS], total[3 * ROWS :]], 1)
+    far_ref[...] = jnp.concatenate([total[ROWS : 2 * ROWS], total[3 * ROWS :]], 1).astype(BF)
 
 
 def whole(count):
@@ -236,17 +258,26 @@
     sources = [synthetic.transpose(1, 0, 2), observed.transpose(1, 0, 2)]
     own = pl.pallas_call(
         forward_kernel,
-        grid=(1,),
         out_shape=shape((Q + 1, ROWS, 2 * F)),
-        in_specs=[pl.BlockSpec((3, ROWS, ticks), lambda i: (0, 0, 0))] * 2
-        + [pl.BlockSpec(forward.shape, lambda i: (0, 0, 0))],
-        out_specs=pl.BlockSpec((Q + 1, ROWS, 2 * F), lambda i: (0, 0, 0)),
-        compiler_params=pltpu.CompilerParams(vmem_limit_bytes=60 * 1024 * 1024),
+        in_specs=[pl.BlockSpec(memory_space=pl.ANY)] * 3,
+        out_specs=whole(1)[0],
+        scratch_shapes=[
+            pltpu.VMEM((2, 3, ROWS, ticks), BF),
+            pltpu.VMEM(forward.shape, BF),
+            pltpu.SemaphoreType.DMA((2 + RADIX,)),
+        ],
+        compiler_params=pltpu.CompilerParams(vmem_limit_bytes=63_225_856),
         cost_estimate=cost(2 * Q * ROWS * ticks * 2 * F, 3 << 20),
     )(*sources, forward)
-    index = jnp.concatenate([nearby_receiver_slots.T, far_index]).astype(BF)
-    index = jnp.pad(index, ((0, ROWS - index.shape[0]), (0, 2 * F - index.shape[1])))
-    own = lax.dynamic_update_slice(own, index[None], (Q, 0, 0))
+    own = pl.pallas_call(
+        index_kernel,
+        out_shape=shape(own.shape),
+        in_specs=whole(3),
+        out_specs=whole(1)[0],
+        input_output_aliases={2: 0},
+        compiler_params=pltpu.CompilerParams(vmem_limit_bytes=VMEM_BYTES // 2),
+        cost_estimate=cost(1 << 20, 1 << 16),
+    )(nearby_receiver_slots.T, far_index, own)
 
     def select(jobs, blocks):
         sizes = [len(ring) * CAP for _, ring in jobs for _ in range(YS)]
@@ -293,12 +324,13 @@
         cost_estimate=cost(9 << 30, 9 << 20),
     )(slots, lag, *pieces)
     grads = lax.all_to_all(grads, "dev", split_axis=0, concat_axis=0, tiled=True)
+    grads, misfit = lax.optimization_barrier((grads, misfit.reshape(pairs)))
     held = jnp.concatenate([nearby_receiver_slots, far_rows + ROWS], 1)
     held = jnp.concatenate([held, held + 2 * ROWS], 1).reshape(1, peers * ROWS)
     near_sum, far_sum = pl.pallas_call(
         collect_kernel,
         grid=(3,),
-        out_shape=[shape((3 * ROWS, 2 * F), F32)] * 2,
+        out_shape=[shape((3 * ROWS, 2 * F), F32), shape((3 * ROWS, 2 * F))],
         in_specs=[
             pl.BlockSpec((1, peers * ROWS), lambda c: (0, 0)),
             pl.BlockSpec((peers, ROWS, F), lambda c: (0, c, 0)),
@@ -308,19 +340,25 @@
         cost_estimate=cost(1 << 26, 2 << 20),
     )(held, grads)
     far_sum = lax.ppermute(far_sum, "region", [(r, r + 1) for r in range(regions - 1)])
-    part = ticks // RADIX // 2
+    inverse = pl.pallas_call(
+        fetch_kernel,
+        out_shape=shape(inverse.shape),
+        in_specs=[pl.BlockSpec(memory_space=pl.ANY)] * 2,
+        out_specs=whole(1)[0],
+        scratch_shapes=[pltpu.SemaphoreType.DMA],
+        compiler_params=pltpu.CompilerParams(vmem_limit_bytes=VMEM_BYTES // 2),
+        cost_estimate=cost(0, 4 << 20),
+    )(inverse, near_sum)
     adjoint = pl.pallas_call(
         inverse_kernel,
-        grid=(2,),
         out_shape=shape((3 * ROWS, ticks)),
-        in_specs=[pl.BlockSpec((3 * ROWS, 2 * F), lambda i: (0, 0))] * 2
-        + [pl.BlockSpec((RADIX, 2 * F // RADIX, part), lambda i: (0, 0, i))],
-        out_specs=pl.BlockSpec((3 * ROWS, ticks), lambda i: (0, 0)),
-        compiler_params=pltpu.CompilerParams(vmem_limit_bytes=60 * 1024 * 1024),
+        in_specs=whole(3),
+        out_specs=whole(1)[0],
+        compiler_params=pltpu.CompilerParams(vmem_limit_bytes=VMEM_BYTES // 2),
         cost_estimate=cost(2 * 3 * ROWS * ticks * 2 * F, 3 << 20),
     )(near_sum, far_sum, inverse)
     adjoint = adjoint.reshape(3, ROWS, ticks).transpose(1, 0, 2)
-    return (adjoint, misfit.reshape(pairs))
+    return (adjoint, misfit)
 
 
 def solution(mesh):

time: 151 us -> 147 us (0.974)
  waiting for transfers between devices: 76.6 us -> 73.1 us
  local copies, waits for them, and re-layouts: 2.49 us -> 4.35 us
    ppermute x1, waiting for transfers between devices: 1.91 us -> 0.01 us  [on_device(): lax.ppermute(far_sum, 'region', [(r, r + 1) for r in range(regions - 1)])]
    unnamed x22, local copies, waits for them, and re-layouts: 2.31 us -> 4.18 us
    pallas_call x2 -> x4, Pallas kernels: 6.73 us -> 5.74 us  [the longest x1 4.34 us: on_device(): pl.pallas_call(forward_kernel, out_shape=shape((Q + 1, ROWS, 2 * F)), in_...]
  transfers between devices with their start and end apart: 21 -> 21, of which waited for: 9 -> 8; matrix products, arithmetic and copies ran while one was open for 1% -> 1% of each run, Pallas kernels for 4% -> 4%
where the time goes in v3:
time: 147 us
  waiting for transfers between devices  73.1 us (50%)
  starting transfers between devices  49.8 us (34%)
  Pallas kernels  18.1 us (12%)
  local copies, waits for them, and re-layouts  4.35 us (3%)
    all_to_all x1, waiting for transfers between devices, on_device(): lax.all_to_all(grads, 'dev', split_axis=0, concat_axis=0, tiled=True)  37.4 us
    ppermute x10, waiting for transfers between devices, y_move(): return lax.ppermute(value, ('region', 'dev'), y_pairs(step, regions, shift))  22.1 us
    ppermute x10, starting transfers between devices, y_move(): return lax.ppermute(value, ('region', 'dev'), y_pairs(step, regions, shift))  19.6 us
    ppermute x8, starting transfers between devices, z_move(): return lax.ppermute(value, 'dev', z_pairs(step))  15.7 us
    ppermute x8, waiting for transfers between devices, z_move(): return lax.ppermute(value, 'dev', z_pairs(step))  13.6 us
    pallas_call x1, Pallas kernels, on_device(): pl.pallas_call(pair_kernel, grid=(3,), out_shape=[shape((pairs, 1), F32),...  9.9 us
    all_to_all x1, starting transfers between devices, on_device(): lax.all_to_all(grads, 'dev', split_axis=0, concat_axis=0, tiled=True)  6.18 us
    ppermute x1, starting transfers between devices, on_device(): lax.ppermute(far_rows.T, 'region', [(r, r + 1) for r in range(regions - 1)])  4.51 us
  transfers between devices with their start and end apart: 21, of which 8 were waited for; matrix products, arithmetic and copies ran while one was open for 1% of the time, Pallas kernels for 4%

profile of v3, /device:TPU:1, one launch (start us, length us, event | category | flops | bytes accessed | tf_op | source)
XLA Modules:
  0.0 147.0 jit_solution(11033008164958177448)
XLA Ops:
  0.6 4.5 %collective-permute-start = (s32[4,32]{1,0:T(4,128)}, s32[4,32]{1,0:T(4,128)S(1)}, u32[]{:S(2)}, u32[]{:S(2)}) collective-permute-start(s32[4,32]{1,0:T(4,128)} %bitcast.15), channel_id=1, source_target_pairs={{0,32},{32,64},{64,96},{96,128},{128,160},{160,192},{192,224},{1,3... | collective-permute-start | bytes 1544 | tf_op jit(solution)/shard_map/ppermute | solution.py:257
  5.2 4.3 %shard_map.122._ = bf16[7,16,1024]{2,1,0:T(8,128)(2,1)} custom-call(bf16[3,16,4096]{2,1,0:T(8,128)(2,1)} %bitcast.12, bf16[3,16,4096]{2,1,0:T(8,128)(2,1)} %bitcast.13, bf16[4,1024,256]{2,1,0:T(8,128)(2,1)} %constant.10.clone.far_table_ref), custom_call_target="tpu_custom_call" | custom-call | flops 805306368 | bytes 3145728 | tf_op jit(solution)/shard_map/pallas_call | solution.py:259
  9.5 0.0 copy-start.1
  9.5 0.9 copy-done.1
  10.5 5.6 %collective-permute-start.4 = (bf16[7,16,1024]{2,1,0:T(8,128)(2,1)S(1)}, bf16[7,16,1024]{2,1,0:T(8,128)(2,1)S(1)}, u32[]{:S(2)}, u32[]{:S(2)}) collective-permute-start(bf16[7,16,1024]{2,1,0:T(8,128)(2,1)S(1)} %shard_map.123.refs_0_), channel_id=1, source_target_pairs={{0,28},{1,29},{2,30},{3,31},{4,0},{5,1},{6,2},{7,3},{8,4},{9,5},{1... | collective-permute-start | bytes 688136 | tf_op jit(solution)/shard_map/ppermute | solution.py:252
  16.1 0.0 collective-permute-start.1
  16.1 0.7 copy-done.2
  16.7 3.9 %collective-permute-done.4.refs_2_ = bf16[7,16,1024]{2,1,0:T(8,128)(2,1)S(1)} collective-permute-done((bf16[7,16,1024]{2,1,0:T(8,128)(2,1)S(1)}, bf16[7,16,1024]{2,1,0:T(8,128)(2,1)S(1)}, u32[]{:S(2)}, u32[]{:S(2)}) %collective-permute-start.4) | collective-permute-done | bytes 229408 | tf_op jit(solution)/shard_map/ppermute | solution.py:252
  20.7 3.1 %collective-permute-start.5 = (bf16[7,16,1024]{2,1,0:T(8,128)(2,1)S(1)}, bf16[7,16,1024]{2,1,0:T(8,128)(2,1)S(1)}, u32[]{:S(2)}, u32[]{:S(2)}) collective-permute-start(bf16[7,16,1024]{2,1,0:T(8,128)(2,1)S(1)} %collective-permute-done.4.refs_2_), channel_id=1, source_target_pairs={{0,28},{1,29},{2,30},{3,31},{4,0},{5,1},{6,2},{7,3},{8,4},{9,5},{1... | collective-permute-start | bytes 688136 | tf_op jit(solution)/shard_map/ppermute | solution.py:252
  23.8 0.3 collective-permute-done.1.refs_1_
  24.1 0.0 collective-permute-start.2
  24.1 4.9 %collective-permute-done.5.refs_4_ = bf16[7,16,1024]{2,1,0:T(8,128)(2,1)S(1)} collective-permute-done((bf16[7,16,1024]{2,1,0:T(8,128)(2,1)S(1)}, bf16[7,16,1024]{2,1,0:T(8,128)(2,1)S(1)}, u32[]{:S(2)}, u32[]{:S(2)}) %collective-permute-start.5) | collective-permute-done | bytes 229408 | tf_op jit(solution)/shard_map/ppermute | solution.py:252
  28.9 3.4 %collective-permute-start.6 = (bf16[7,16,1024]{2,1,0:T(8,128)(2,1)S(1)}, bf16[7,16,1024]{2,1,0:T(8,128)(2,1)S(1)}, u32[]{:S(2)}, u32[]{:S(2)}) collective-permute-start(bf16[7,16,1024]{2,1,0:T(8,128)(2,1)S(1)} %collective-permute-done.5.refs_4_), channel_id=1, source_target_pairs={{0,28},{1,29},{2,30},{3,31},{4,0},{5,1},{6,2},{7,3},{8,4},{9,5},{1... | collective-permute-start | bytes 688136 | tf_op jit(solution)/shard_map/ppermute | solution.py:252
  32.4 4.3 %collective-permute-done.6.refs_6_ = bf16[7,16,1024]{2,1,0:T(8,128)(2,1)S(1)} collective-permute-done((bf16[7,16,1024]{2,1,0:T(8,128)(2,1)S(1)}, bf16[7,16,1024]{2,1,0:T(8,128)(2,1)S(1)}, u32[]{:S(2)}, u32[]{:S(2)}) %collective-permute-start.6) | collective-permute-done | bytes 229408 | tf_op jit(solution)/shard_map/ppermute | solution.py:252
  36.6 3.5 %collective-permute-start.8 = (bf16[4,16,1024]{2,1,0:T(8,128)(2,1)S(1)}, bf16[4,16,1024]{2,1,0:T(8,128)(2,1)S(1)}, u32[]{:S(2)}, u32[]{:S(2)}) collective-permute-start(bf16[4,16,1024]{2,1,0:T(8,128)(2,1)S(1)} %slice.9), channel_id=1, source_target_pairs={{0,28},{1,29},{2,30},{3,31},{4,0},{5,1},{6,2},{7,3},{8,4},{9,5},{1... | collective-permute-start | bytes 393224 | tf_op jit(solution)/shard_map/ppermute | solution.py:252
  40.1 0.9 copy-done.3
  41.1 0.0 copy-start.5
  41.1 0.5 shard_map.124
  41.7 0.1 collective-permute-start.7
  41.8 3.0 %collective-permute-start.11 = (bf16[2,3,16,1024]{3,2,1,0:T(8,128)(2,1)S(1)}, bf16[2,3,16,1024]{3,2,1,0:T(8,128)(2,1)S(1)}, u32[]{:S(2)}, u32[]{:S(2)}) collective-permute-start(bf16[2,3,16,1024]{3,2,1,0:T(8,128)(2,1)S(1)} %get-tuple-element.28), channel_id=1, source_target_pairs={{0,2},{1,3},{2,0},{3,1},{4,6},{5,7},{6,4},{7,5},{8,10},{9,11},{10,... | collective-permute-start | bytes 589832 | tf_op jit(solution)/shard_map/ppermute | solution.py:255
  44.7 0.8 collective-permute-start.13
  45.5 0.7 collective-permute-start.9
  46.2 0.2 collective-permute-done.7
  46.5 1.2 shard_map.125
  47.7 1.4 collective-permute-start.10
  49.0 5.1 %collective-permute-start.15 = (bf16[2,3,32,1024]{3,2,1,0:T(8,128)(2,1)S(1)}, bf16[2,3,32,1024]{3,2,1,0:T(8,128)(2,1)S(1)}, u32[]{:S(2)}, u32[]{:S(2)}) collective-permute-start(bf16[2,3,32,1024]{3,2,1,0:T(8,128)(2,1)S(1)} %get-tuple-element.32), channel_id=1, source_target_pairs={{32,0},{33,1},{34,2},{35,3},{36,4},{37,5},{38,6},{39,7},{40,8},{41... | collective-permute-start | bytes 1179656 | tf_op jit(solution)/shard_map/ppermute | solution.py:255
  54.2 2.5 %collective-permute-start.16 = (bf16[2,3,32,1024]{3,2,1,0:T(8,128)(2,1)S(1)}, bf16[2,3,32,1024]{3,2,1,0:T(8,128)(2,1)S(1)}, u32[]{:S(2)}, u32[]{:S(2)}) collective-permute-start(bf16[2,3,32,1024]{3,2,1,0:T(8,128)(2,1)S(1)} %get-tuple-element.33), channel_id=1, source_target_pairs={{32,1},{33,2},{34,3},{35,0},{36,5},{37,6},{38,7},{39,4},{40,9},{41... | collective-permute-start | bytes 1179656 | tf_op jit(solution)/shard_map/ppermute | solution.py:255
  56.6 0.0 collective-permute-done.13.refs_6_
  56.7 2.3 %collective-permute-start.12 = (bf16[2,3,16,1024]{3,2,1,0:T(8,128)(2,1)S(1)}, bf16[2,3,16,1024]{3,2,1,0:T(8,128)(2,1)S(1)}, u32[]{:S(2)}, u32[]{:S(2)}) collective-permute-start(bf16[2,3,16,1024]{3,2,1,0:T(8,128)(2,1)S(1)} %get-tuple-element.29), channel_id=1, source_target_pairs={{0,2},{1,3},{2,0},{3,1},{4,6},{5,7},{6,4},{7,5},{8,10},{9,11},{10,... | collective-permute-start | bytes 589832 | tf_op jit(solution)/shard_map/ppermute | solution.py:255
  59.0 0.0 collective-permute-done.9.refs_2_
  59.0 1.9 %collective-permute-start.17 = (bf16[2,3,32,1024]{3,2,1,0:T(8,128)(2,1)S(1)}, bf16[2,3,32,1024]{3,2,1,0:T(8,128)(2,1)S(1)}, u32[]{:S(2)}, u32[]{:S(2)}) collective-permute-start(bf16[2,3,32,1024]{3,2,1,0:T(8,128)(2,1)S(1)} %get-tuple-element.34), channel_id=1, source_target_pairs={{32,2},{33,3},{34,0},{35,1},{36,6},{37,7},{38,4},{39,5},{40,10},{4... | collective-permute-start | bytes 1179656 | tf_op jit(solution)/shard_map/ppermute | solution.py:255
  60.9 0.0 collective-permute-done.10.refs_3_
  60.9 1.9 %collective-permute-start.18 = (bf16[2,3,32,1024]{3,2,1,0:T(8,128)(2,1)S(1)}, bf16[2,3,32,1024]{3,2,1,0:T(8,128)(2,1)S(1)}, u32[]{:S(2)}, u32[]{:S(2)}) collective-permute-start(bf16[2,3,32,1024]{3,2,1,0:T(8,128)(2,1)S(1)} %get-tuple-element.35), channel_id=1, source_target_pairs={{32,3},{33,0},{34,1},{35,2},{36,7},{37,4},{38,5},{39,6},{40,11},{4... | collective-permute-start | bytes 1179656 | tf_op jit(solution)/shard_map/ppermute | solution.py:255
  62.8 13.6 %collective-permute-done.12.refs_5_ = bf16[2,3,16,1024]{3,2,1,0:T(8,128)(2,1)S(1)} collective-permute-done((bf16[2,3,16,1024]{3,2,1,0:T(8,128)(2,1)S(1)}, bf16[2,3,16,1024]{3,2,1,0:T(8,128)(2,1)S(1)}, u32[]{:S(2)}, u32[]{:S(2)}) %collective-permute-start.12) | collective-permute-done | bytes 196640 | tf_op jit(solution)/shard_map/ppermute | solution.py:255
  76.5 8.5 %collective-permute-done.14.refs_7_ = bf16[2,3,16,1024]{3,2,1,0:T(8,128)(2,1)S(1)} collective-permute-done((bf16[2,3,16,1024]{3,2,1,0:T(8,128)(2,1)S(1)}, bf16[2,3,16,1024]{3,2,1,0:T(8,128)(2,1)S(1)}, u32[]{:S(2)}, u32[]{:S(2)}) %collective-permute-start.14) | collective-permute-done | bytes 196640 | tf_op jit(solution)/shard_map/ppermute | solution.py:255
  85.0 0.0 collective-permute-done.15.refs_8_
  85.0 9.9 %shard_map.126 = (f32[256,1]{1,0:T(8,128)S(1)}, bf16[32,48,512]{2,1,0:T(8,128)(2,1)}) custom-call(s32[4,256]{1,0:T(4,128)S(1)} %pad_add_fusion.1.slots_ref, bf16[1024,512]{1,0:T(8,128)(2,1)S(1)} %copy-done.5, bf16[2,3,16,1024]{3,2,1,0:T(8,128)(2,1)S(1)} %get-tuple-element.23.refs_0_, bf16[2,3,16,1024]{3,2,1,0:T(8,128)(2,1)S(1)} %get-tuple-element.25.refs_1_, ...), custom_call_target="tpu_custom_call" | custom-call | flops 9663676416 | bytes 9437184 | tf_op jit(solution)/shard_map/pallas_call | solution.py:308
  94.9 6.2 %all-to-all-start = ((bf16[32,48,512]{2,1,0:T(8,128)(2,1)}), bf16[32,48,512]{2,1,0:T(8,128)(2,1)S(1)}, u32[]{:S(2)}, u32[]{:S(2)}) async-start(bf16[32,48,512]{2,1,0:T(8,128)(2,1)} %get-tuple-element.36), calls=%async_computation | async-start | bytes 3145728 | tf_op jit(solution)/shard_map/all_to_all | solution.py:326
  101.1 0.1 copy.15
  101.2 0.1 reshape.13.held_ref
  101.3 0.7 reduce
  102.0 37.4 %all-to-all-done.grad_ref = bf16[32,48,512]{2,1,0:T(8,128)(2,1)S(1)} async-done(((bf16[32,48,512]{2,1,0:T(8,128)(2,1)}), bf16[32,48,512]{2,1,0:T(8,128)(2,1)S(1)}, u32[]{:S(2)}, u32[]{:S(2)}) %all-to-all-start) | async-done | bytes 1572896 | tf_op jit(solution)/shard_map/all_to_all | solution.py:326
  139.4 0.8 shard_map.127
  140.2 3.8 %collective-permute-start.19 = (bf16[48,1024]{1,0:T(8,128)(2,1)S(1)}, bf16[48,1024]{1,0:T(8,128)(2,1)S(1)}, u32[]{:S(2)}, u32[]{:S(2)}) collective-permute-start(bf16[48,1024]{1,0:T(8,128)(2,1)S(1)} %get-tuple-element.40), channel_id=1, source_target_pairs={{0,32},{32,64},{64,96},{96,128},{128,160},{160,192},{192,224},{1,3... | collective-permute-start | bytes 294920 | tf_op jit(solution)/shard_map/ppermute | solution.py:342
  144.0 0.0 copy-start
  144.0 1.6 %copy-done = bf16[4,256,1024]{2,1,0:T(8,128)(2,1)S(1)} copy-done((bf16[4,256,1024]{2,1,0:T(8,128)(2,1)S(1)}, bf16[4,256,1024]{2,1,0:T(8,128)(2,1)}, u32[]{:S(2)}) %copy-start) | copy-done | bytes 2097176
  145.6 0.1 shard_map.128.table_ref
  145.8 1.2 shard_map.129
  (34 shorter events, 0.1 us)
Async XLA Ops:
  0.6 8.9 %copy-start.4 = (s32[32,4]{0,1:T(4,128)S(1)}, s32[32,4]{0,1:T(4,128)}, u32[]{:S(2)}) copy-start(s32[32,4]{0,1:T(4,128)} %param.13) | copy-start | bytes 1540
  0.6 8.9 %collective-permute-start = (s32[4,32]{1,0:T(4,128)}, s32[4,32]{1,0:T(4,128)S(1)}, u32[]{:S(2)}, u32[]{:S(2)}) collective-permute-start(s32[4,32]{1,0:T(4,128)} %bitcast.15), channel_id=1, source_target_pairs={{0,32},{32,64},{64,96},{96,128},{128,160},{160,192},{192,224},{1,3... | collective-permute-start | bytes 1544 | tf_op jit(solution)/shard_map/ppermute | solution.py:257
  9.5 0.9 copy-start.1
  10.5 10.2 %collective-permute-start.4 = (bf16[7,16,1024]{2,1,0:T(8,128)(2,1)S(1)}, bf16[7,16,1024]{2,1,0:T(8,128)(2,1)S(1)}, u32[]{:S(2)}, u32[]{:S(2)}) collective-permute-start(bf16[7,16,1024]{2,1,0:T(8,128)(2,1)S(1)} %shard_map.123.refs_0_), channel_id=1, source_target_pairs={{0,28},{1,29},{2,30},{3,31},{4,0},{5,1},{6,2},{7,3},{8,4},{9,5},{1... | collective-permute-start | bytes 688136 | tf_op jit(solution)/shard_map/ppermute | solution.py:252
  16.1 8.0 %collective-permute-start.1 = (bf16[7,16,1024]{2,1,0:T(8,128)(2,1)S(1)}, bf16[7,16,1024]{2,1,0:T(8,128)(2,1)S(1)}, u32[]{:S(2)}, u32[]{:S(2)}) collective-permute-start(bf16[7,16,1024]{2,1,0:T(8,128)(2,1)S(1)} %shard_map.123.refs_0_), channel_id=1, source_target_pairs={{0,4},{1,5},{2,6},{3,7},{4,8},{5,9},{6,10},{7,11},{8,12},{9,13},{1... | collective-permute-start | bytes 688136 | tf_op jit(solution)/shard_map/ppermute | solution.py:252
  16.1 0.7 copy-start.2
  20.7 8.3 %collective-permute-start.5 = (bf16[7,16,1024]{2,1,0:T(8,128)(2,1)S(1)}, bf16[7,16,1024]{2,1,0:T(8,128)(2,1)S(1)}, u32[]{:S(2)}, u32[]{:S(2)}) collective-permute-start(bf16[7,16,1024]{2,1,0:T(8,128)(2,1)S(1)} %collective-permute-done.4.refs_2_), channel_id=1, source_target_pairs={{0,28},{1,29},{2,30},{3,31},{4,0},{5,1},{6,2},{7,3},{8,4},{9,5},{1... | collective-permute-start | bytes 688136 | tf_op jit(solution)/shard_map/ppermute | solution.py:252
  24.1 8.3 %collective-permute-start.2 = (bf16[7,16,1024]{2,1,0:T(8,128)(2,1)S(1)}, bf16[7,16,1024]{2,1,0:T(8,128)(2,1)S(1)}, u32[]{:S(2)}, u32[]{:S(2)}) collective-permute-start(bf16[7,16,1024]{2,1,0:T(8,128)(2,1)S(1)} %collective-permute-done.1.refs_1_), channel_id=1, source_target_pairs={{0,4},{1,5},{2,6},{3,7},{4,8},{5,9},{6,10},{7,11},{8,12},{9,13},{1... | collective-permute-start | bytes 688136 | tf_op jit(solution)/shard_map/ppermute | solution.py:252
  28.9 7.7 %collective-permute-start.6 = (bf16[7,16,1024]{2,1,0:T(8,128)(2,1)S(1)}, bf16[7,16,1024]{2,1,0:T(8,128)(2,1)S(1)}, u32[]{:S(2)}, u32[]{:S(2)}) collective-permute-start(bf16[7,16,1024]{2,1,0:T(8,128)(2,1)S(1)} %collective-permute-done.5.refs_4_), channel_id=1, source_target_pairs={{0,28},{1,29},{2,30},{3,31},{4,0},{5,1},{6,2},{7,3},{8,4},{9,5},{1... | collective-permute-start | bytes 688136 | tf_op jit(solution)/shard_map/ppermute | solution.py:252
  32.4 9.3 %collective-permute-start.3 = (bf16[7,16,1024]{2,1,0:T(8,128)(2,1)S(1)}, bf16[7,16,1024]{2,1,0:T(8,128)(2,1)S(1)}, u32[]{:S(2)}, u32[]{:S(2)}) collective-permute-start(bf16[7,16,1024]{2,1,0:T(8,128)(2,1)S(1)} %collective-permute-done.2.refs_3_), channel_id=1, source_target_pairs={{0,4},{1,5},{2,6},{3,7},{4,8},{5,9},{6,10},{7,11},{8,12},{9,13},{1... | collective-permute-start | bytes 688136 | tf_op jit(solution)/shard_map/ppermute | solution.py:252
  36.6 9.8 %collective-permute-start.8 = (bf16[4,16,1024]{2,1,0:T(8,128)(2,1)S(1)}, bf16[4,16,1024]{2,1,0:T(8,128)(2,1)S(1)}, u32[]{:S(2)}, u32[]{:S(2)}) collective-permute-start(bf16[4,16,1024]{2,1,0:T(8,128)(2,1)S(1)} %slice.9), channel_id=1, source_target_pairs={{0,28},{1,29},{2,30},{3,31},{4,0},{5,1},{6,2},{7,3},{8,4},{9,5},{1... | collective-permute-start | bytes 393224 | tf_op jit(solution)/shard_map/ppermute | solution.py:252
  40.1 0.9 copy-start.3
  41.1 35.4 %copy-start.7 = (s32[256]{0:T(256)S(1)}, s32[256]{0:T(256)}, u32[]{:S(2)}) copy-start(s32[256]{0:T(256)} %param.18) | copy-start | bytes 3076
  41.1 35.4 %copy-start.8 = (s32[256]{0:T(256)S(1)}, s32[256]{0:T(256)}, u32[]{:S(2)}) copy-start(s32[256]{0:T(256)} %param.17) | copy-start | bytes 3076
  41.1 35.4 %copy-start.9 = (s32[256]{0:T(256)S(1)}, s32[256]{0:T(256)}, u32[]{:S(2)}) copy-start(s32[256]{0:T(256)} %param.16) | copy-start | bytes 3076
  41.1 35.4 %copy-start.10 = (s32[256]{0:T(256)S(1)}, s32[256]{0:T(256)}, u32[]{:S(2)}) copy-start(s32[256]{0:T(256)} %param.15) | copy-start | bytes 3076
  41.1 43.9 %copy-start.5 = (bf16[1024,512]{1,0:T(8,128)(2,1)S(1)}, bf16[1024,512]{1,0:T(8,128)(2,1)}, u32[]{:S(2)}) copy-start(bf16[1024,512]{1,0:T(8,128)(2,1)} %constant.12.clone.lag_ref) | copy-start | bytes 3145732
  41.7 4.8 %collective-permute-start.7 = (bf16[3,16,1024]{2,1,0:T(8,128)(2,1)S(1)}, bf16[3,16,1024]{2,1,0:T(8,128)(2,1)S(1)}, u32[]{:S(2)}, u32[]{:S(2)}) collective-permute-start(bf16[3,16,1024]{2,1,0:T(8,128)(2,1)S(1)} %slice.8), channel_id=1, source_target_pairs={{0,4},{1,5},{2,6},{3,7},{4,8},{5,9},{6,10},{7,11},{8,12},{9,13},{1... | collective-permute-start | bytes 294920 | tf_op jit(solution)/shard_map/ppermute | solution.py:252
  41.8 12.4 %collective-permute-start.11 = (bf16[2,3,16,1024]{3,2,1,0:T(8,128)(2,1)S(1)}, bf16[2,3,16,1024]{3,2,1,0:T(8,128)(2,1)S(1)}, u32[]{:S(2)}, u32[]{:S(2)}) collective-permute-start(bf16[2,3,16,1024]{3,2,1,0:T(8,128)(2,1)S(1)} %get-tuple-element.28), channel_id=1, source_target_pairs={{0,2},{1,3},{2,0},{3,1},{4,6},{5,7},{6,4},{7,5},{8,10},{9,11},{10,... | collective-permute-start | bytes 589832 | tf_op jit(solution)/shard_map/ppermute | solution.py:255
  44.7 11.9 %collective-permute-start.13 = (bf16[2,3,16,1024]{3,2,1,0:T(8,128)(2,1)S(1)}, bf16[2,3,16,1024]{3,2,1,0:T(8,128)(2,1)S(1)}, u32[]{:S(2)}, u32[]{:S(2)}) collective-permute-start(bf16[2,3,16,1024]{3,2,1,0:T(8,128)(2,1)S(1)} %get-tuple-element.30), channel_id=1, source_target_pairs={{0,3},{1,0},{2,1},{3,2},{4,7},{5,4},{6,5},{7,6},{8,11},{9,8},{10,9... | collective-permute-start | bytes 589832 | tf_op jit(solution)/shard_map/ppermute | solution.py:255
  45.5 13.5 %collective-permute-start.9 = (bf16[2,3,16,1024]{3,2,1,0:T(8,128)(2,1)S(1)}, bf16[2,3,16,1024]{3,2,1,0:T(8,128)(2,1)S(1)}, u32[]{:S(2)}, u32[]{:S(2)}) collective-permute-start(bf16[2,3,16,1024]{3,2,1,0:T(8,128)(2,1)S(1)} %get-tuple-element.26), channel_id=1, source_target_pairs={{0,1},{1,2},{2,3},{3,0},{4,5},{5,6},{6,7},{7,4},{8,9},{9,10},{10,1... | collective-permute-start | bytes 589832 | tf_op jit(solution)/shard_map/ppermute | solution.py:255
  47.7 13.3 %collective-permute-start.10 = (bf16[2,3,16,1024]{3,2,1,0:T(8,128)(2,1)S(1)}, bf16[2,3,16,1024]{3,2,1,0:T(8,128)(2,1)S(1)}, u32[]{:S(2)}, u32[]{:S(2)}) collective-permute-start(bf16[2,3,16,1024]{3,2,1,0:T(8,128)(2,1)S(1)} %get-tuple-element.27), channel_id=1, source_target_pairs={{0,1},{1,2},{2,3},{3,0},{4,5},{5,6},{6,7},{7,4},{8,9},{9,10},{10,1... | collective-permute-start | bytes 589832 | tf_op jit(solution)/shard_map/ppermute | solution.py:255
  49.0 36.0 %collective-permute-start.15 = (bf16[2,3,32,1024]{3,2,1,0:T(8,128)(2,1)S(1)}, bf16[2,3,32,1024]{3,2,1,0:T(8,128)(2,1)S(1)}, u32[]{:S(2)}, u32[]{:S(2)}) collective-permute-start(bf16[2,3,32,1024]{3,2,1,0:T(8,128)(2,1)S(1)} %get-tuple-element.32), channel_id=1, source_target_pairs={{32,0},{33,1},{34,2},{35,3},{36,4},{37,5},{38,6},{39,7},{40,8},{41... | collective-permute-start | bytes 1179656 | tf_op jit(solution)/shard_map/ppermute | solution.py:255
  54.2 30.8 %collective-permute-start.16 = (bf16[2,3,32,1024]{3,2,1,0:T(8,128)(2,1)S(1)}, bf16[2,3,32,1024]{3,2,1,0:T(8,128)(2,1)S(1)}, u32[]{:S(2)}, u32[]{:S(2)}) collective-permute-start(bf16[2,3,32,1024]{3,2,1,0:T(8,128)(2,1)S(1)} %get-tuple-element.33), channel_id=1, source_target_pairs={{32,1},{33,2},{34,3},{35,0},{36,5},{37,6},{38,7},{39,4},{40,9},{41... | collective-permute-start | bytes 1179656 | tf_op jit(solution)/shard_map/ppermute | solution.py:255
  56.7 19.8 %collective-permute-start.12 = (bf16[2,3,16,1024]{3,2,1,0:T(8,128)(2,1)S(1)}, bf16[2,3,16,1024]{3,2,1,0:T(8,128)(2,1)S(1)}, u32[]{:S(2)}, u32[]{:S(2)}) collective-permute-start(bf16[2,3,16,1024]{3,2,1,0:T(8,128)(2,1)S(1)} %get-tuple-element.29), channel_id=1, source_target_pairs={{0,2},{1,3},{2,0},{3,1},{4,6},{5,7},{6,4},{7,5},{8,10},{9,11},{10,... | collective-permute-start | bytes 589832 | tf_op jit(solution)/shard_map/ppermute | solution.py:255
  59.0 26.0 %collective-permute-start.17 = (bf16[2,3,32,1024]{3,2,1,0:T(8,128)(2,1)S(1)}, bf16[2,3,32,1024]{3,2,1,0:T(8,128)(2,1)S(1)}, u32[]{:S(2)}, u32[]{:S(2)}) collective-permute-start(bf16[2,3,32,1024]{3,2,1,0:T(8,128)(2,1)S(1)} %get-tuple-element.34), channel_id=1, source_target_pairs={{32,2},{33,3},{34,0},{35,1},{36,6},{37,7},{38,4},{39,5},{40,10},{4... | collective-permute-start | bytes 1179656 | tf_op jit(solution)/shard_map/ppermute | solution.py:255
  60.9 24.1 %collective-permute-start.18 = (bf16[2,3,32,1024]{3,2,1,0:T(8,128)(2,1)S(1)}, bf16[2,3,32,1024]{3,2,1,0:T(8,128)(2,1)S(1)}, u32[]{:S(2)}, u32[]{:S(2)}) collective-permute-start(bf16[2,3,32,1024]{3,2,1,0:T(8,128)(2,1)S(1)} %get-tuple-element.35), channel_id=1, source_target_pairs={{32,3},{33,0},{34,1},{35,2},{36,7},{37,4},{38,5},{39,6},{40,11},{4... | collective-permute-start | bytes 1179656 | tf_op jit(solution)/shard_map/ppermute | solution.py:255
  76.4 8.5 %collective-permute-start.14 = (bf16[2,3,16,1024]{3,2,1,0:T(8,128)(2,1)S(1)}, bf16[2,3,16,1024]{3,2,1,0:T(8,128)(2,1)S(1)}, u32[]{:S(2)}, u32[]{:S(2)}) collective-permute-start(bf16[2,3,16,1024]{3,2,1,0:T(8,128)(2,1)S(1)} %get-tuple-element.31), channel_id=1, source_target_pairs={{0,3},{1,0},{2,1},{3,2},{4,7},{5,4},{6,5},{7,6},{8,11},{9,8},{10,9... | collective-permute-start | bytes 589832 | tf_op jit(solution)/shard_map/ppermute | solution.py:255
  94.9 6.2 %copy-start.6 = (s32[32,4]{0,1:T(4,128)S(1)}, s32[32,4]{0,1:T(4,128)}, u32[]{:S(2)}) copy-start(s32[32,4]{0,1:T(4,128)} %param.14) | copy-start | bytes 1540
  94.9 44.5 %all-to-all-start = ((bf16[32,48,512]{2,1,0:T(8,128)(2,1)}), bf16[32,48,512]{2,1,0:T(8,128)(2,1)S(1)}, u32[]{:S(2)}, u32[]{:S(2)}) async-start(bf16[32,48,512]{2,1,0:T(8,128)(2,1)} %get-tuple-element.36), calls=%async_computation | async-start | bytes 3145728 | tf_op jit(solution)/shard_map/all_to_all | solution.py:326
  140.2 5.6 %collective-permute-start.19 = (bf16[48,1024]{1,0:T(8,128)(2,1)S(1)}, bf16[48,1024]{1,0:T(8,128)(2,1)S(1)}, u32[]{:S(2)}, u32[]{:S(2)}) collective-permute-start(bf16[48,1024]{1,0:T(8,128)(2,1)S(1)} %get-tuple-element.40), channel_id=1, source_target_pairs={{0,32},{32,64},{64,96},{96,128},{128,160},{160,192},{192,224},{1,3... | collective-permute-start | bytes 294920 | tf_op jit(solution)/shard_map/ppermute | solution.py:342
  144.0 1.6 %copy-start = (bf16[4,256,1024]{2,1,0:T(8,128)(2,1)S(1)}, bf16[4,256,1024]{2,1,0:T(8,128)(2,1)}, u32[]{:S(2)}) copy-start(bf16[4,256,1024]{2,1,0:T(8,128)(2,1)} %constant.11.clone.source_ref) | copy-start | bytes 6291460

commit v4 on v3

--- a/solution.py
+++ b/solution.py
@@ -75,13 +75,15 @@
         pltpu.make_async_copy(far_table_ref.at[c], table_ref.at[c], done.at[2 + c])
         for c in range(RADIX)
     ]
-    for copy in copies:
+    for copy in copies[:4]:
         copy.start()
     copies[0].wait()
     copies[1].wait()
     traces = jnp.concatenate([held[n, c] for n in range(2) for c in range(3)], 0)
     for c in range(RADIX):
         copies[2 + c].wait()
+        if c + 2 < RADIX:
+            copies[4 + c].start()
         sums = [dot(traces[:, j * quarter : (j + 1) * quarter], table_ref[c]) for j in range(RADIX)]
         (r0, i0), (r1, i1), (r2, i2), (r3, i3) = [(p[:, :group], p[:, group:]) for p in sums]
         if c == 0:
@@ -178,37 +180,38 @@
     first = (iota((pairs, near), 1) == column[:, 0:1]).astype(BF)
     second = (iota((pairs, 2 * near), 1) == column[:, 1:2]).astype(BF)
 
-    def both(kind):
-        spectra = jnp.concatenate([piece[kind, 0] for piece in pieces], 0)
-        a = dot(first, spectra[:near])
-        b = dot(second, spectra)
-        return a[:, :F], a[:, F:], b[:, :F], b[:, F:]
-
-    ar, ai, br, bi = both(0)
-    cr, ci, dr, di = both(1)
-    real = (ar * br + ai * bi) - (cr * dr + ci * di)
-    imag = (ai * br - ar * bi) - (ci * dr - cr * di)
-    shifted = dot(real.astype(BF), lag[:F]) + dot(imag.astype(BF), lag[F:])
     at = iota((pairs, LAGS), 1)
     start = column[:, 2:3]
     inside = (at >= start) & (at < start + column[:, 3:4])
-    residual = jnp.where(inside, shifted, 0.0)
-    part = jnp.sum(residual * residual, axis=1, keepdims=True)
-
-    @pl.when(pl.program_id(0) == 0)
-    def _():
-        misfit_ref[...] = jnp.zeros_like(misfit_ref)
-
-    misfit_ref[...] += part * (1.0 / (2.0 * LAGS))
-    slope = lax.dot_general(
-        residual.astype(BF), lag, (((1,), (1,)), ((), ())), preferred_element_type=F32
-    )
-    gr, gi = slope[:, :F], slope[:, F:]
-    grad_first = jnp.concatenate([gr * br - gi * bi, gr * bi + gi * br], 1).astype(BF)
-    grad_second = jnp.concatenate([gr * ar + gi * ai, gr * ai - gi * ar], 1).astype(BF)
-    total = dot(first_back, grad_first) + dot(second_back, grad_second)
-    total = total.reshape(peers, 2 * CAP, 2 * F)
-    out_ref[...] = jnp.concatenate([total[..., :F], total[..., F:]], 1).astype(BF)
+    kept, reals, imags = [], [], []
+    for c in range(3):
+
+        def both(kind):
+            spectra = jnp.concatenate([piece[kind, c] for piece in pieces], 0)
+            a = dot(first, spectra[:near])
+            b = dot(second, spectra)
+            return a[:, :F], a[:, F:], b[:, :F], b[:, F:]
+
+        ar, ai, br, bi = both(0)
+        cr, ci, dr, di = both(1)
+        reals.append(((ar * br + ai * bi) - (cr * dr + ci * di)).astype(BF))
+        imags.append(((ai * br - ar * bi) - (ci * dr - cr * di)).astype(BF))
+        kept.append([v.astype(BF) for v in (ar, ai, br, bi)])
+    shifted = dot(jnp.concatenate(reals, 0), lag[:F]) + dot(jnp.concatenate(imags, 0), lag[F:])
+    residuals = [jnp.where(inside, shifted[c * pairs : (c + 1) * pairs], 0.0) for c in range(3)]
+    misfit = sum(jnp.sum(r * r, axis=1, keepdims=True) for r in residuals)
+    misfit_ref[...] = misfit * (1.0 / (2.0 * LAGS))
+    rounded = jnp.concatenate([r.astype(BF) for r in residuals], 0)
+    slope = lax.dot_general(rounded, lag, (((1,), (1,)), ((), ())), preferred_element_type=F32)
+    for c in range(3):
+        ar, ai, br, bi = [v.astype(F32) for v in kept[c]]
+        gr, gi = slope[c * pairs : (c + 1) * pairs, :F], slope[c * pairs : (c + 1) * pairs, F:]
+        grad_first = jnp.concatenate([gr * br - gi * bi, gr * bi + gi * br], 1).astype(BF)
+        grad_second = jnp.concatenate([gr * ar + gi * ai, gr * ai - gi * ar], 1).astype(BF)
+        total = dot(first_back, grad_first) + dot(second_back, grad_second)
+        total = total.reshape(peers, 2 * CAP, 2 * F)
+        total = jnp.concatenate([total[..., :F], total[..., F:]], 1).astype(BF)
+        out_ref[:, c * ROWS : (c + 1) * ROWS] = total
 
 
 def collect_kernel(held_ref, grad_ref, near_ref, far_ref):
@@ -307,19 +310,9 @@
     slots = jnp.stack([first_slot, second_slot, window_start, pair_delay_indices])
     misfit, grads = pl.pallas_call(
         pair_kernel,
-        grid=(3,),
         out_shape=[shape((pairs, 1), F32), shape((peers, 3 * ROWS, F))],
-        in_specs=[
-            pl.BlockSpec((4, pairs), lambda c: (0, 0)),
-            pl.BlockSpec((2 * F, LAGS), lambda c: (0, 0)),
-        ]
-        + [
-            pl.BlockSpec((2, 1) + piece.shape[2:], lambda c: (0, c, 0, 0)) for piece in pieces
-        ],
-        out_specs=[
-            pl.BlockSpec((pairs, 1), lambda c: (0, 0)),
-            pl.BlockSpec((peers, ROWS, F), lambda c: (0, c, 0)),
-        ],
+        in_specs=whole(2 + len(pieces)),
+        out_specs=whole(2),
         compiler_params=params,
         cost_estimate=cost(9 << 30, 9 << 20),
     )(slots, lag, *pieces)

time: 147 us -> 145 us (0.986)
  Pallas kernels: 18.1 us -> 15.5 us
    pallas_call x1, Pallas kernels: 9.9 us -> 7.28 us  [on_device(): pl.pallas_call(pair_kernel, out_shape=[shape((pairs, 1), F32), shape((pee...]
where the time goes in v4:
time: 145 us
  waiting for transfers between devices  73.1 us (50%)
  starting transfers between devices  50.1 us (35%)
  Pallas kernels  15.5 us (11%)
  local copies, waits for them, and re-layouts  4.35 us (3%)
    all_to_all x1, waiting for transfers between devices, on_device(): lax.all_to_all(grads, 'dev', split_axis=0, concat_axis=0, tiled=True)  37.4 us
    ppermute x10, waiting for transfers between devices, y_move(): return lax.ppermute(value, ('region', 'dev'), y_pairs(step, regions, shift))  22.1 us
    ppermute x10, starting transfers between devices, y_move(): return lax.ppermute(value, ('region', 'dev'), y_pairs(step, regions, shift))  19.6 us
    ppermute x8, starting transfers between devices, z_move(): return lax.ppermute(value, 'dev', z_pairs(step))  15.7 us
    ppermute x8, waiting for transfers between devices, z_move(): return lax.ppermute(value, 'dev', z_pairs(step))  13.6 us
    pallas_call x1, Pallas kernels, on_device(): pl.pallas_call(pair_kernel, out_shape=[shape((pairs, 1), F32), shape((pee...  7.28 us
    all_to_all x1, starting transfers between devices, on_device(): lax.all_to_all(grads, 'dev', split_axis=0, concat_axis=0, tiled=True)  6.19 us
    ppermute x1, starting transfers between devices, on_device(): lax.ppermute(far_rows.T, 'region', [(r, r + 1) for r in range(regions - 1)])  4.51 us
  transfers between devices with their start and end apart: 21, of which 8 were waited for; matrix products, arithmetic and copies ran while one was open for 1% of the time, Pallas kernels for 4%

profile of v4, /device:TPU:1, one launch (start us, length us, event | category | flops | bytes accessed | tf_op | source)
XLA Modules:
  0.0 144.7 jit_solution(15160476702666107665)
XLA Ops:
  0.6 4.5 %collective-permute-start = (s32[4,32]{1,0:T(4,128)}, s32[4,32]{1,0:T(4,128)S(1)}, u32[]{:S(2)}, u32[]{:S(2)}) collective-permute-start(s32[4,32]{1,0:T(4,128)} %bitcast.15), channel_id=1, source_target_pairs={{0,32},{32,64},{64,96},{96,128},{128,160},{160,192},{192,224},{1,3... | collective-permute-start | bytes 1544 | tf_op jit(solution)/shard_map/ppermute | solution.py:260
  5.2 4.3 %shard_map.122._ = bf16[7,16,1024]{2,1,0:T(8,128)(2,1)} custom-call(bf16[3,16,4096]{2,1,0:T(8,128)(2,1)} %bitcast.12, bf16[3,16,4096]{2,1,0:T(8,128)(2,1)} %bitcast.13, bf16[4,1024,256]{2,1,0:T(8,128)(2,1)} %constant.10.clone.far_table_ref), custom_call_target="tpu_custom_call" | custom-call | flops 805306368 | bytes 3145728 | tf_op jit(solution)/shard_map/pallas_call | solution.py:262
  9.5 0.0 collective-permute-done.far_ref
  9.5 0.0 copy-start.1
  9.5 0.9 copy-done.1
  10.5 5.6 %collective-permute-start.4 = (bf16[7,16,1024]{2,1,0:T(8,128)(2,1)S(1)}, bf16[7,16,1024]{2,1,0:T(8,128)(2,1)S(1)}, u32[]{:S(2)}, u32[]{:S(2)}) collective-permute-start(bf16[7,16,1024]{2,1,0:T(8,128)(2,1)S(1)} %shard_map.123.refs_0_), channel_id=1, source_target_pairs={{0,28},{1,29},{2,30},{3,31},{4,0},{5,1},{6,2},{7,3},{8,4},{9,5},{1... | collective-permute-start | bytes 688136 | tf_op jit(solution)/shard_map/ppermute | solution.py:255
  16.1 0.7 copy-done.2
  16.8 3.9 %collective-permute-done.4.refs_2_ = bf16[7,16,1024]{2,1,0:T(8,128)(2,1)S(1)} collective-permute-done((bf16[7,16,1024]{2,1,0:T(8,128)(2,1)S(1)}, bf16[7,16,1024]{2,1,0:T(8,128)(2,1)S(1)}, u32[]{:S(2)}, u32[]{:S(2)}) %collective-permute-start.4) | collective-permute-done | bytes 229408 | tf_op jit(solution)/shard_map/ppermute | solution.py:255
  20.7 3.1 %collective-permute-start.5 = (bf16[7,16,1024]{2,1,0:T(8,128)(2,1)S(1)}, bf16[7,16,1024]{2,1,0:T(8,128)(2,1)S(1)}, u32[]{:S(2)}, u32[]{:S(2)}) collective-permute-start(bf16[7,16,1024]{2,1,0:T(8,128)(2,1)S(1)} %collective-permute-done.4.refs_2_), channel_id=1, source_target_pairs={{0,28},{1,29},{2,30},{3,31},{4,0},{5,1},{6,2},{7,3},{8,4},{9,5},{1... | collective-permute-start | bytes 688136 | tf_op jit(solution)/shard_map/ppermute | solution.py:255
  23.8 0.3 collective-permute-done.1.refs_1_
  24.1 0.0 collective-permute-start.2
  24.1 4.9 %collective-permute-done.5.refs_4_ = bf16[7,16,1024]{2,1,0:T(8,128)(2,1)S(1)} collective-permute-done((bf16[7,16,1024]{2,1,0:T(8,128)(2,1)S(1)}, bf16[7,16,1024]{2,1,0:T(8,128)(2,1)S(1)}, u32[]{:S(2)}, u32[]{:S(2)}) %collective-permute-start.5) | collective-permute-done | bytes 229408 | tf_op jit(solution)/shard_map/ppermute | solution.py:255
  28.9 3.4 %collective-permute-start.6 = (bf16[7,16,1024]{2,1,0:T(8,128)(2,1)S(1)}, bf16[7,16,1024]{2,1,0:T(8,128)(2,1)S(1)}, u32[]{:S(2)}, u32[]{:S(2)}) collective-permute-start(bf16[7,16,1024]{2,1,0:T(8,128)(2,1)S(1)} %collective-permute-done.5.refs_4_), channel_id=1, source_target_pairs={{0,28},{1,29},{2,30},{3,31},{4,0},{5,1},{6,2},{7,3},{8,4},{9,5},{1... | collective-permute-start | bytes 688136 | tf_op jit(solution)/shard_map/ppermute | solution.py:255
  32.4 4.3 %collective-permute-done.6.refs_6_ = bf16[7,16,1024]{2,1,0:T(8,128)(2,1)S(1)} collective-permute-done((bf16[7,16,1024]{2,1,0:T(8,128)(2,1)S(1)}, bf16[7,16,1024]{2,1,0:T(8,128)(2,1)S(1)}, u32[]{:S(2)}, u32[]{:S(2)}) %collective-permute-start.6) | collective-permute-done | bytes 229408 | tf_op jit(solution)/shard_map/ppermute | solution.py:255
  36.6 3.5 %collective-permute-start.8 = (bf16[4,16,1024]{2,1,0:T(8,128)(2,1)S(1)}, bf16[4,16,1024]{2,1,0:T(8,128)(2,1)S(1)}, u32[]{:S(2)}, u32[]{:S(2)}) collective-permute-start(bf16[4,16,1024]{2,1,0:T(8,128)(2,1)S(1)} %slice.9), channel_id=1, source_target_pairs={{0,28},{1,29},{2,30},{3,31},{4,0},{5,1},{6,2},{7,3},{8,4},{9,5},{1... | collective-permute-start | bytes 393224 | tf_op jit(solution)/shard_map/ppermute | solution.py:255
  40.1 0.9 copy-done.3
  41.1 0.0 copy-start.5
  41.1 0.6 shard_map.124
  41.7 0.0 collective-permute-done.3.refs_5_
  41.7 0.1 collective-permute-start.7
  41.8 3.0 %collective-permute-start.11 = (bf16[2,3,16,1024]{3,2,1,0:T(8,128)(2,1)S(1)}, bf16[2,3,16,1024]{3,2,1,0:T(8,128)(2,1)S(1)}, u32[]{:S(2)}, u32[]{:S(2)}) collective-permute-start(bf16[2,3,16,1024]{3,2,1,0:T(8,128)(2,1)S(1)} %get-tuple-element.28), channel_id=1, source_target_pairs={{0,2},{1,3},{2,0},{3,1},{4,6},{5,7},{6,4},{7,5},{8,10},{9,11},{10,... | collective-permute-start | bytes 589832 | tf_op jit(solution)/shard_map/ppermute | solution.py:258
  44.8 0.8 collective-permute-start.13
  45.5 0.7 collective-permute-start.9
  46.2 0.2 collective-permute-done.7
  46.5 1.2 shard_map.125
  47.7 1.4 collective-permute-start.10
  49.0 5.1 %collective-permute-start.15 = (bf16[2,3,32,1024]{3,2,1,0:T(8,128)(2,1)S(1)}, bf16[2,3,32,1024]{3,2,1,0:T(8,128)(2,1)S(1)}, u32[]{:S(2)}, u32[]{:S(2)}) collective-permute-start(bf16[2,3,32,1024]{3,2,1,0:T(8,128)(2,1)S(1)} %get-tuple-element.32), channel_id=1, source_target_pairs={{32,0},{33,1},{34,2},{35,3},{36,4},{37,5},{38,6},{39,7},{40,8},{41... | collective-permute-start | bytes 1179656 | tf_op jit(solution)/shard_map/ppermute | solution.py:258
  54.2 2.5 %collective-permute-start.16 = (bf16[2,3,32,1024]{3,2,1,0:T(8,128)(2,1)S(1)}, bf16[2,3,32,1024]{3,2,1,0:T(8,128)(2,1)S(1)}, u32[]{:S(2)}, u32[]{:S(2)}) collective-permute-start(bf16[2,3,32,1024]{3,2,1,0:T(8,128)(2,1)S(1)} %get-tuple-element.33), channel_id=1, source_target_pairs={{32,1},{33,2},{34,3},{35,0},{36,5},{37,6},{38,7},{39,4},{40,9},{41... | collective-permute-start | bytes 1179656 | tf_op jit(solution)/shard_map/ppermute | solution.py:258
  56.7 0.0 collective-permute-done.13.refs_6_
  56.7 2.3 %collective-permute-start.12 = (bf16[2,3,16,1024]{3,2,1,0:T(8,128)(2,1)S(1)}, bf16[2,3,16,1024]{3,2,1,0:T(8,128)(2,1)S(1)}, u32[]{:S(2)}, u32[]{:S(2)}) collective-permute-start(bf16[2,3,16,1024]{3,2,1,0:T(8,128)(2,1)S(1)} %get-tuple-element.29), channel_id=1, source_target_pairs={{0,2},{1,3},{2,0},{3,1},{4,6},{5,7},{6,4},{7,5},{8,10},{9,11},{10,... | collective-permute-start | bytes 589832 | tf_op jit(solution)/shard_map/ppermute | solution.py:258
  59.0 1.9 %collective-permute-start.17 = (bf16[2,3,32,1024]{3,2,1,0:T(8,128)(2,1)S(1)}, bf16[2,3,32,1024]{3,2,1,0:T(8,128)(2,1)S(1)}, u32[]{:S(2)}, u32[]{:S(2)}) collective-permute-start(bf16[2,3,32,1024]{3,2,1,0:T(8,128)(2,1)S(1)} %get-tuple-element.34), channel_id=1, source_target_pairs={{32,2},{33,3},{34,0},{35,1},{36,6},{37,7},{38,4},{39,5},{40,10},{4... | collective-permute-start | bytes 1179656 | tf_op jit(solution)/shard_map/ppermute | solution.py:258
  61.0 1.9 %collective-permute-start.18 = (bf16[2,3,32,1024]{3,2,1,0:T(8,128)(2,1)S(1)}, bf16[2,3,32,1024]{3,2,1,0:T(8,128)(2,1)S(1)}, u32[]{:S(2)}, u32[]{:S(2)}) collective-permute-start(bf16[2,3,32,1024]{3,2,1,0:T(8,128)(2,1)S(1)} %get-tuple-element.35), channel_id=1, source_target_pairs={{32,3},{33,0},{34,1},{35,2},{36,7},{37,4},{38,5},{39,6},{40,11},{4... | collective-permute-start | bytes 1179656 | tf_op jit(solution)/shard_map/ppermute | solution.py:258
  62.9 13.6 %collective-permute-done.12.refs_5_ = bf16[2,3,16,1024]{3,2,1,0:T(8,128)(2,1)S(1)} collective-permute-done((bf16[2,3,16,1024]{3,2,1,0:T(8,128)(2,1)S(1)}, bf16[2,3,16,1024]{3,2,1,0:T(8,128)(2,1)S(1)}, u32[]{:S(2)}, u32[]{:S(2)}) %collective-permute-start.12) | collective-permute-done | bytes 196640 | tf_op jit(solution)/shard_map/ppermute | solution.py:258
  76.5 8.5 %collective-permute-done.14.refs_7_ = bf16[2,3,16,1024]{3,2,1,0:T(8,128)(2,1)S(1)} collective-permute-done((bf16[2,3,16,1024]{3,2,1,0:T(8,128)(2,1)S(1)}, bf16[2,3,16,1024]{3,2,1,0:T(8,128)(2,1)S(1)}, u32[]{:S(2)}, u32[]{:S(2)}) %collective-permute-start.14) | collective-permute-done | bytes 196640 | tf_op jit(solution)/shard_map/ppermute | solution.py:258
  85.0 0.0 collective-permute-done.15.refs_8_
  85.0 0.0 collective-permute-done.16.refs_9_
  85.0 7.3 %shard_map.126 = (f32[256,1]{1,0:T(8,128)S(1)}, bf16[32,48,512]{2,1,0:T(8,128)(2,1)}) custom-call(s32[4,256]{1,0:T(4,128)S(1)} %pad_add_fusion.1.slots_ref, bf16[1024,512]{1,0:T(8,128)(2,1)S(1)} %copy-done.5, bf16[2,3,16,1024]{3,2,1,0:T(8,128)(2,1)S(1)} %get-tuple-element.23.refs_0_, bf16[2,3,16,1024]{3,2,1,0:T(8,128)(2,1)S(1)} %get-tuple-element.25.refs_1_, ...), custom_call_target="tpu_custom_call" | custom-call | flops 9663676416 | bytes 9437184 | tf_op jit(solution)/shard_map/pallas_call | solution.py:311
  92.3 6.2 %all-to-all-start = ((bf16[32,48,512]{2,1,0:T(8,128)(2,1)}), bf16[32,48,512]{2,1,0:T(8,128)(2,1)S(1)}, u32[]{:S(2)}, u32[]{:S(2)}) async-start(bf16[32,48,512]{2,1,0:T(8,128)(2,1)} %get-tuple-element.36), calls=%async_computation | async-start | bytes 3145728 | tf_op jit(solution)/shard_map/all_to_all | solution.py:319
  98.6 0.1 copy.15
  98.6 0.1 reshape.13.held_ref
  98.7 0.7 reduce
  99.4 37.4 %all-to-all-done.grad_ref = bf16[32,48,512]{2,1,0:T(8,128)(2,1)S(1)} async-done(((bf16[32,48,512]{2,1,0:T(8,128)(2,1)}), bf16[32,48,512]{2,1,0:T(8,128)(2,1)S(1)}, u32[]{:S(2)}, u32[]{:S(2)}) %all-to-all-start) | async-done | bytes 1572896 | tf_op jit(solution)/shard_map/all_to_all | solution.py:319
  136.8 0.8 shard_map.127
  137.6 4.1 %collective-permute-start.19 = (bf16[48,1024]{1,0:T(8,128)(2,1)S(1)}, bf16[48,1024]{1,0:T(8,128)(2,1)S(1)}, u32[]{:S(2)}, u32[]{:S(2)}) collective-permute-start(bf16[48,1024]{1,0:T(8,128)(2,1)S(1)} %get-tuple-element.40), channel_id=1, source_target_pairs={{0,32},{32,64},{64,96},{96,128},{128,160},{160,192},{192,224},{1,3... | collective-permute-start | bytes 294920 | tf_op jit(solution)/shard_map/ppermute | solution.py:335
  141.7 0.0 copy-start
  141.7 1.6 %copy-done = bf16[4,256,1024]{2,1,0:T(8,128)(2,1)S(1)} copy-done((bf16[4,256,1024]{2,1,0:T(8,128)(2,1)S(1)}, bf16[4,256,1024]{2,1,0:T(8,128)(2,1)}, u32[]{:S(2)}) %copy-start) | copy-done | bytes 2097176
  143.3 0.1 shard_map.128.table_ref
  143.4 1.2 shard_map.129
  (34 shorter events, 0.1 us)
Async XLA Ops:
  0.6 8.9 %copy-start.4 = (s32[32,4]{0,1:T(4,128)S(1)}, s32[32,4]{0,1:T(4,128)}, u32[]{:S(2)}) copy-start(s32[32,4]{0,1:T(4,128)} %param.13) | copy-start | bytes 1540
  0.6 8.9 %collective-permute-start = (s32[4,32]{1,0:T(4,128)}, s32[4,32]{1,0:T(4,128)S(1)}, u32[]{:S(2)}, u32[]{:S(2)}) collective-permute-start(s32[4,32]{1,0:T(4,128)} %bitcast.15), channel_id=1, source_target_pairs={{0,32},{32,64},{64,96},{96,128},{128,160},{160,192},{192,224},{1,3... | collective-permute-start | bytes 1544 | tf_op jit(solution)/shard_map/ppermute | solution.py:260
  9.5 0.9 copy-start.1
  10.5 10.2 %collective-permute-start.4 = (bf16[7,16,1024]{2,1,0:T(8,128)(2,1)S(1)}, bf16[7,16,1024]{2,1,0:T(8,128)(2,1)S(1)}, u32[]{:S(2)}, u32[]{:S(2)}) collective-permute-start(bf16[7,16,1024]{2,1,0:T(8,128)(2,1)S(1)} %shard_map.123.refs_0_), channel_id=1, source_target_pairs={{0,28},{1,29},{2,30},{3,31},{4,0},{5,1},{6,2},{7,3},{8,4},{9,5},{1... | collective-permute-start | bytes 688136 | tf_op jit(solution)/shard_map/ppermute | solution.py:255
  16.1 8.0 %collective-permute-start.1 = (bf16[7,16,1024]{2,1,0:T(8,128)(2,1)S(1)}, bf16[7,16,1024]{2,1,0:T(8,128)(2,1)S(1)}, u32[]{:S(2)}, u32[]{:S(2)}) collective-permute-start(bf16[7,16,1024]{2,1,0:T(8,128)(2,1)S(1)} %shard_map.123.refs_0_), channel_id=1, source_target_pairs={{0,4},{1,5},{2,6},{3,7},{4,8},{5,9},{6,10},{7,11},{8,12},{9,13},{1... | collective-permute-start | bytes 688136 | tf_op jit(solution)/shard_map/ppermute | solution.py:255
  16.1 0.7 copy-start.2
  20.7 8.3 %collective-permute-start.5 = (bf16[7,16,1024]{2,1,0:T(8,128)(2,1)S(1)}, bf16[7,16,1024]{2,1,0:T(8,128)(2,1)S(1)}, u32[]{:S(2)}, u32[]{:S(2)}) collective-permute-start(bf16[7,16,1024]{2,1,0:T(8,128)(2,1)S(1)} %collective-permute-done.4.refs_2_), channel_id=1, source_target_pairs={{0,28},{1,29},{2,30},{3,31},{4,0},{5,1},{6,2},{7,3},{8,4},{9,5},{1... | collective-permute-start | bytes 688136 | tf_op jit(solution)/shard_map/ppermute | solution.py:255
  24.1 8.3 %collective-permute-start.2 = (bf16[7,16,1024]{2,1,0:T(8,128)(2,1)S(1)}, bf16[7,16,1024]{2,1,0:T(8,128)(2,1)S(1)}, u32[]{:S(2)}, u32[]{:S(2)}) collective-permute-start(bf16[7,16,1024]{2,1,0:T(8,128)(2,1)S(1)} %collective-permute-done.1.refs_1_), channel_id=1, source_target_pairs={{0,4},{1,5},{2,6},{3,7},{4,8},{5,9},{6,10},{7,11},{8,12},{9,13},{1... | collective-permute-start | bytes 688136 | tf_op jit(solution)/shard_map/ppermute | solution.py:255
  28.9 7.7 %collective-permute-start.6 = (bf16[7,16,1024]{2,1,0:T(8,128)(2,1)S(1)}, bf16[7,16,1024]{2,1,0:T(8,128)(2,1)S(1)}, u32[]{:S(2)}, u32[]{:S(2)}) collective-permute-start(bf16[7,16,1024]{2,1,0:T(8,128)(2,1)S(1)} %collective-permute-done.5.refs_4_), channel_id=1, source_target_pairs={{0,28},{1,29},{2,30},{3,31},{4,0},{5,1},{6,2},{7,3},{8,4},{9,5},{1... | collective-permute-start | bytes 688136 | tf_op jit(solution)/shard_map/ppermute | solution.py:255
  32.4 9.3 %collective-permute-start.3 = (bf16[7,16,1024]{2,1,0:T(8,128)(2,1)S(1)}, bf16[7,16,1024]{2,1,0:T(8,128)(2,1)S(1)}, u32[]{:S(2)}, u32[]{:S(2)}) collective-permute-start(bf16[7,16,1024]{2,1,0:T(8,128)(2,1)S(1)} %collective-permute-done.2.refs_3_), channel_id=1, source_target_pairs={{0,4},{1,5},{2,6},{3,7},{4,8},{5,9},{6,10},{7,11},{8,12},{9,13},{1... | collective-permute-start | bytes 688136 | tf_op jit(solution)/shard_map/ppermute | solution.py:255
  36.6 9.8 %collective-permute-start.8 = (bf16[4,16,1024]{2,1,0:T(8,128)(2,1)S(1)}, bf16[4,16,1024]{2,1,0:T(8,128)(2,1)S(1)}, u32[]{:S(2)}, u32[]{:S(2)}) collective-permute-start(bf16[4,16,1024]{2,1,0:T(8,128)(2,1)S(1)} %slice.9), channel_id=1, source_target_pairs={{0,28},{1,29},{2,30},{3,31},{4,0},{5,1},{6,2},{7,3},{8,4},{9,5},{1... | collective-permute-start | bytes 393224 | tf_op jit(solution)/shard_map/ppermute | solution.py:255
  40.1 0.9 copy-start.3
  41.1 35.4 %copy-start.7 = (s32[256]{0:T(256)S(1)}, s32[256]{0:T(256)}, u32[]{:S(2)}) copy-start(s32[256]{0:T(256)} %param.18) | copy-start | bytes 3076
  41.1 35.4 %copy-start.8 = (s32[256]{0:T(256)S(1)}, s32[256]{0:T(256)}, u32[]{:S(2)}) copy-start(s32[256]{0:T(256)} %param.17) | copy-start | bytes 3076
  41.1 35.4 %copy-start.9 = (s32[256]{0:T(256)S(1)}, s32[256]{0:T(256)}, u32[]{:S(2)}) copy-start(s32[256]{0:T(256)} %param.16) | copy-start | bytes 3076
  41.1 35.4 %copy-start.10 = (s32[256]{0:T(256)S(1)}, s32[256]{0:T(256)}, u32[]{:S(2)}) copy-start(s32[256]{0:T(256)} %param.15) | copy-start | bytes 3076
  41.1 43.9 %copy-start.5 = (bf16[1024,512]{1,0:T(8,128)(2,1)S(1)}, bf16[1024,512]{1,0:T(8,128)(2,1)}, u32[]{:S(2)}) copy-start(bf16[1024,512]{1,0:T(8,128)(2,1)} %constant.12.clone.lag_ref) | copy-start | bytes 3145732
  41.7 4.8 %collective-permute-start.7 = (bf16[3,16,1024]{2,1,0:T(8,128)(2,1)S(1)}, bf16[3,16,1024]{2,1,0:T(8,128)(2,1)S(1)}, u32[]{:S(2)}, u32[]{:S(2)}) collective-permute-start(bf16[3,16,1024]{2,1,0:T(8,128)(2,1)S(1)} %slice.8), channel_id=1, source_target_pairs={{0,4},{1,5},{2,6},{3,7},{4,8},{5,9},{6,10},{7,11},{8,12},{9,13},{1... | collective-permute-start | bytes 294920 | tf_op jit(solution)/shard_map/ppermute | solution.py:255
  41.8 12.4 %collective-permute-start.11 = (bf16[2,3,16,1024]{3,2,1,0:T(8,128)(2,1)S(1)}, bf16[2,3,16,1024]{3,2,1,0:T(8,128)(2,1)S(1)}, u32[]{:S(2)}, u32[]{:S(2)}) collective-permute-start(bf16[2,3,16,1024]{3,2,1,0:T(8,128)(2,1)S(1)} %get-tuple-element.28), channel_id=1, source_target_pairs={{0,2},{1,3},{2,0},{3,1},{4,6},{5,7},{6,4},{7,5},{8,10},{9,11},{10,... | collective-permute-start | bytes 589832 | tf_op jit(solution)/shard_map/ppermute | solution.py:258
  44.8 11.9 %collective-permute-start.13 = (bf16[2,3,16,1024]{3,2,1,0:T(8,128)(2,1)S(1)}, bf16[2,3,16,1024]{3,2,1,0:T(8,128)(2,1)S(1)}, u32[]{:S(2)}, u32[]{:S(2)}) collective-permute-start(bf16[2,3,16,1024]{3,2,1,0:T(8,128)(2,1)S(1)} %get-tuple-element.30), channel_id=1, source_target_pairs={{0,3},{1,0},{2,1},{3,2},{4,7},{5,4},{6,5},{7,6},{8,11},{9,8},{10,9... | collective-permute-start | bytes 589832 | tf_op jit(solution)/shard_map/ppermute | solution.py:258
  45.5 13.5 %collective-permute-start.9 = (bf16[2,3,16,1024]{3,2,1,0:T(8,128)(2,1)S(1)}, bf16[2,3,16,1024]{3,2,1,0:T(8,128)(2,1)S(1)}, u32[]{:S(2)}, u32[]{:S(2)}) collective-permute-start(bf16[2,3,16,1024]{3,2,1,0:T(8,128)(2,1)S(1)} %get-tuple-element.26), channel_id=1, source_target_pairs={{0,1},{1,2},{2,3},{3,0},{4,5},{5,6},{6,7},{7,4},{8,9},{9,10},{10,1... | collective-permute-start | bytes 589832 | tf_op jit(solution)/shard_map/ppermute | solution.py:258
  47.7 13.3 %collective-permute-start.10 = (bf16[2,3,16,1024]{3,2,1,0:T(8,128)(2,1)S(1)}, bf16[2,3,16,1024]{3,2,1,0:T(8,128)(2,1)S(1)}, u32[]{:S(2)}, u32[]{:S(2)}) collective-permute-start(bf16[2,3,16,1024]{3,2,1,0:T(8,128)(2,1)S(1)} %get-tuple-element.27), channel_id=1, source_target_pairs={{0,1},{1,2},{2,3},{3,0},{4,5},{5,6},{6,7},{7,4},{8,9},{9,10},{10,1... | collective-permute-start | bytes 589832 | tf_op jit(solution)/shard_map/ppermute | solution.py:258
  49.0 36.0 %collective-permute-start.15 = (bf16[2,3,32,1024]{3,2,1,0:T(8,128)(2,1)S(1)}, bf16[2,3,32,1024]{3,2,1,0:T(8,128)(2,1)S(1)}, u32[]{:S(2)}, u32[]{:S(2)}) collective-permute-start(bf16[2,3,32,1024]{3,2,1,0:T(8,128)(2,1)S(1)} %get-tuple-element.32), channel_id=1, source_target_pairs={{32,0},{33,1},{34,2},{35,3},{36,4},{37,5},{38,6},{39,7},{40,8},{41... | collective-permute-start | bytes 1179656 | tf_op jit(solution)/shard_map/ppermute | solution.py:258
  54.2 30.8 %collective-permute-start.16 = (bf16[2,3,32,1024]{3,2,1,0:T(8,128)(2,1)S(1)}, bf16[2,3,32,1024]{3,2,1,0:T(8,128)(2,1)S(1)}, u32[]{:S(2)}, u32[]{:S(2)}) collective-permute-start(bf16[2,3,32,1024]{3,2,1,0:T(8,128)(2,1)S(1)} %get-tuple-element.33), channel_id=1, source_target_pairs={{32,1},{33,2},{34,3},{35,0},{36,5},{37,6},{38,7},{39,4},{40,9},{41... | collective-permute-start | bytes 1179656 | tf_op jit(solution)/shard_map/ppermute | solution.py:258
  56.7 19.8 %collective-permute-start.12 = (bf16[2,3,16,1024]{3,2,1,0:T(8,128)(2,1)S(1)}, bf16[2,3,16,1024]{3,2,1,0:T(8,128)(2,1)S(1)}, u32[]{:S(2)}, u32[]{:S(2)}) collective-permute-start(bf16[2,3,16,1024]{3,2,1,0:T(8,128)(2,1)S(1)} %get-tuple-element.29), channel_id=1, source_target_pairs={{0,2},{1,3},{2,0},{3,1},{4,6},{5,7},{6,4},{7,5},{8,10},{9,11},{10,... | collective-permute-start | bytes 589832 | tf_op jit(solution)/shard_map/ppermute | solution.py:258
  59.0 26.0 %collective-permute-start.17 = (bf16[2,3,32,1024]{3,2,1,0:T(8,128)(2,1)S(1)}, bf16[2,3,32,1024]{3,2,1,0:T(8,128)(2,1)S(1)}, u32[]{:S(2)}, u32[]{:S(2)}) collective-permute-start(bf16[2,3,32,1024]{3,2,1,0:T(8,128)(2,1)S(1)} %get-tuple-element.34), channel_id=1, source_target_pairs={{32,2},{33,3},{34,0},{35,1},{36,6},{37,7},{38,4},{39,5},{40,10},{4... | collective-permute-start | bytes 1179656 | tf_op jit(solution)/shard_map/ppermute | solution.py:258
  61.0 24.1 %collective-permute-start.18 = (bf16[2,3,32,1024]{3,2,1,0:T(8,128)(2,1)S(1)}, bf16[2,3,32,1024]{3,2,1,0:T(8,128)(2,1)S(1)}, u32[]{:S(2)}, u32[]{:S(2)}) collective-permute-start(bf16[2,3,32,1024]{3,2,1,0:T(8,128)(2,1)S(1)} %get-tuple-element.35), channel_id=1, source_target_pairs={{32,3},{33,0},{34,1},{35,2},{36,7},{37,4},{38,5},{39,6},{40,11},{4... | collective-permute-start | bytes 1179656 | tf_op jit(solution)/shard_map/ppermute | solution.py:258
  76.5 8.5 %collective-permute-start.14 = (bf16[2,3,16,1024]{3,2,1,0:T(8,128)(2,1)S(1)}, bf16[2,3,16,1024]{3,2,1,0:T(8,128)(2,1)S(1)}, u32[]{:S(2)}, u32[]{:S(2)}) collective-permute-start(bf16[2,3,16,1024]{3,2,1,0:T(8,128)(2,1)S(1)} %get-tuple-element.31), channel_id=1, source_target_pairs={{0,3},{1,0},{2,1},{3,2},{4,7},{5,4},{6,5},{7,6},{8,11},{9,8},{10,9... | collective-permute-start | bytes 589832 | tf_op jit(solution)/shard_map/ppermute | solution.py:258
  92.3 6.2 %copy-start.6 = (s32[32,4]{0,1:T(4,128)S(1)}, s32[32,4]{0,1:T(4,128)}, u32[]{:S(2)}) copy-start(s32[32,4]{0,1:T(4,128)} %param.14) | copy-start | bytes 1540
  92.3 44.5 %all-to-all-start = ((bf16[32,48,512]{2,1,0:T(8,128)(2,1)}), bf16[32,48,512]{2,1,0:T(8,128)(2,1)S(1)}, u32[]{:S(2)}, u32[]{:S(2)}) async-start(bf16[32,48,512]{2,1,0:T(8,128)(2,1)} %get-tuple-element.36), calls=%async_computation | async-start | bytes 3145728 | tf_op jit(solution)/shard_map/all_to_all | solution.py:319
  137.6 5.8 %collective-permute-start.19 = (bf16[48,1024]{1,0:T(8,128)(2,1)S(1)}, bf16[48,1024]{1,0:T(8,128)(2,1)S(1)}, u32[]{:S(2)}, u32[]{:S(2)}) collective-permute-start(bf16[48,1024]{1,0:T(8,128)(2,1)S(1)} %get-tuple-element.40), channel_id=1, source_target_pairs={{0,32},{32,64},{64,96},{96,128},{128,160},{160,192},{192,224},{1,3... | collective-permute-start | bytes 294920 | tf_op jit(solution)/shard_map/ppermute | solution.py:335
  141.7 1.6 %copy-start = (bf16[4,256,1024]{2,1,0:T(8,128)(2,1)S(1)}, bf16[4,256,1024]{2,1,0:T(8,128)(2,1)}, u32[]{:S(2)}) copy-start(bf16[4,256,1024]{2,1,0:T(8,128)(2,1)} %constant.11.clone.source_ref) | copy-start | bytes 6291460

commit v5 on v4

--- a/solution.py
+++ b/solution.py
@@ -300,12 +300,16 @@
     early = [early[0]] + [y_move(early[k], k, 0) for k in range(1, YS)]
     split = Q // 2
     half_up, half_down = up3[:split], down3[split:]
-    half_up, early[0] = lax.optimization_barrier((half_up, early[0]))
+    half_up, half_down, early[1], early[3] = lax.optimization_barrier(
+        (half_up, half_down, early[1], early[3])
+    )
     last = jnp.concatenate([z_move(half_up, 1), z_move(half_down, -1)], 0)
     blocks = dict(enumerate([own, up, down, up2, down2, up3, down3, last]))
     late = select([(0, LATE), (1, EARLY + LATE)], blocks)
-    far = [y_move(piece, k, -1) for k, piece in enumerate(late[YS:])]
+    far = list(late[YS:])
     late = [late[0]] + [y_move(late[k], k, 0) for k in range(1, YS)]
+    *late, early[2], far[0] = lax.optimization_barrier((*late, early[2], far[0]))
+    far = [y_move(piece, k, -1) for k, piece in enumerate(far)]
     pieces = [piece for pair in zip(early, late) for piece in pair] + far
     slots = jnp.stack([first_slot, second_slot, window_start, pair_delay_indices])
     misfit, grads = pl.pallas_call(

time: 145 us -> 143 us (0.986)
  waiting for transfers between devices: 73.1 us -> 59.6 us
  starting transfers between devices: 50.1 us -> 61.7 us
    ppermute x10, waiting for transfers between devices: 22.1 us -> 13 us  [y_move(): return lax.ppermute(value, ('region', 'dev'), y_pairs(step, regions, shift))]
    ppermute x10, starting transfers between devices: 19.6 us -> 25.9 us  [y_move(): return lax.ppermute(value, ('region', 'dev'), y_pairs(step, regions, shift))]
    ppermute x1, starting transfers between devices: 4.08 us -> 10.3 us  [on_device(): lax.ppermute(far_sum, 'region', [(r, r + 1) for r in range(regions - 1)])]
    ppermute x8, starting transfers between devices: 15.7 us -> 13 us  [z_move(): return lax.ppermute(value, 'dev', z_pairs(step))]
    all_to_all x1, waiting for transfers between devices: 37.4 us -> 34.9 us  [on_device(): lax.all_to_all(grads, 'dev', split_axis=0, concat_axis=0, tiled=True)]
    ppermute x8, waiting for transfers between devices: 13.6 us -> 11.8 us  [z_move(): return lax.ppermute(value, 'dev', z_pairs(step))]
    all_to_all x1, starting transfers between devices: 6.19 us -> 7.95 us  [on_device(): lax.all_to_all(grads, 'dev', split_axis=0, concat_axis=0, tiled=True)]
  transfers between devices with their start and end apart: 21 -> 21, of which waited for: 8 -> 10; matrix products, arithmetic and copies ran while one was open for 1% -> 1% of each run, Pallas kernels for 4% -> 4%
where the time goes in v5:
time: 143 us
  starting transfers between devices  61.7 us (43%)
  waiting for transfers between devices  59.6 us (42%)
  Pallas kernels  15.6 us (11%)
  local copies, waits for them, and re-layouts  4.35 us (3%)
    all_to_all x1, waiting for transfers between devices, on_device(): lax.all_to_all(grads, 'dev', split_axis=0, concat_axis=0, tiled=True)  34.9 us
    ppermute x10, starting transfers between devices, y_move(): return lax.ppermute(value, ('region', 'dev'), y_pairs(step, regions, shift))  25.9 us
    ppermute x8, starting transfers between devices, z_move(): return lax.ppermute(value, 'dev', z_pairs(step))  13 us
    ppermute x10, waiting for transfers between devices, y_move(): return lax.ppermute(value, ('region', 'dev'), y_pairs(step, regions, shift))  13 us
    ppermute x8, waiting for transfers between devices, z_move(): return lax.ppermute(value, 'dev', z_pairs(step))  11.8 us
    ppermute x1, starting transfers between devices, on_device(): lax.ppermute(far_sum, 'region', [(r, r + 1) for r in range(regions - 1)])  10.3 us
    all_to_all x1, starting transfers between devices, on_device(): lax.all_to_all(grads, 'dev', split_axis=0, concat_axis=0, tiled=True)  7.95 us
    pallas_call x1, Pallas kernels, on_device(): pl.pallas_call(pair_kernel, out_shape=[shape((pairs, 1), F32), shape((pee...  7.28 us
  transfers between devices with their start and end apart: 21, of which 10 were waited for; matrix products, arithmetic and copies ran while one was open for 1% of the time, Pallas kernels for 4%

profile of v5, /device:TPU:1, one launch (start us, length us, event | category | flops | bytes accessed | tf_op | source)
XLA Modules:
  0.0 142.9 jit_solution(4727266858723106738)
XLA Ops:
  0.6 4.5 %collective-permute-start = (s32[4,32]{1,0:T(4,128)}, s32[4,32]{1,0:T(4,128)S(1)}, u32[]{:S(2)}, u32[]{:S(2)}) collective-permute-start(s32[4,32]{1,0:T(4,128)} %bitcast.15), channel_id=1, source_target_pairs={{0,32},{32,64},{64,96},{96,128},{128,160},{160,192},{192,224},{1,3... | collective-permute-start | bytes 1544 | tf_op jit(solution)/shard_map/ppermute | solution.py:260
  5.2 0.0 copy-start.5
  5.2 4.4 %shard_map.122._ = bf16[7,16,1024]{2,1,0:T(8,128)(2,1)} custom-call(bf16[3,16,4096]{2,1,0:T(8,128)(2,1)} %bitcast.12, bf16[3,16,4096]{2,1,0:T(8,128)(2,1)} %bitcast.13, bf16[4,1024,256]{2,1,0:T(8,128)(2,1)} %constant.10.clone.far_table_ref), custom_call_target="tpu_custom_call" | custom-call | flops 805306368 | bytes 3145728 | tf_op jit(solution)/shard_map/pallas_call | solution.py:262
  9.6 0.0 copy-start.1
  9.6 0.9 copy-done.1
  10.6 1.7 %collective-permute-start.1 = (bf16[7,16,1024]{2,1,0:T(8,128)(2,1)S(1)}, bf16[7,16,1024]{2,1,0:T(8,128)(2,1)S(1)}, u32[]{:S(2)}, u32[]{:S(2)}) collective-permute-start(bf16[7,16,1024]{2,1,0:T(8,128)(2,1)S(1)} %shard_map.123.refs_0_), channel_id=1, source_target_pairs={{0,4},{1,5},{2,6},{3,7},{4,8},{5,9},{6,10},{7,11},{8,12},{9,13},{1... | collective-permute-start | bytes 688136 | tf_op jit(solution)/shard_map/ppermute | solution.py:255
  12.3 4.0 %collective-permute-start.2 = (bf16[7,16,1024]{2,1,0:T(8,128)(2,1)S(1)}, bf16[7,16,1024]{2,1,0:T(8,128)(2,1)S(1)}, u32[]{:S(2)}, u32[]{:S(2)}) collective-permute-start(bf16[7,16,1024]{2,1,0:T(8,128)(2,1)S(1)} %shard_map.123.refs_0_), channel_id=1, source_target_pairs={{0,28},{1,29},{2,30},{3,31},{4,0},{5,1},{6,2},{7,3},{8,4},{9,5},{1... | collective-permute-start | bytes 688136 | tf_op jit(solution)/shard_map/ppermute | solution.py:255
  16.3 0.7 copy-done.2
  17.0 4.0 %collective-permute-done.1.refs_1_ = bf16[7,16,1024]{2,1,0:T(8,128)(2,1)S(1)} collective-permute-done((bf16[7,16,1024]{2,1,0:T(8,128)(2,1)S(1)}, bf16[7,16,1024]{2,1,0:T(8,128)(2,1)S(1)}, u32[]{:S(2)}, u32[]{:S(2)}) %collective-permute-start.1) | collective-permute-done | bytes 229408 | tf_op jit(solution)/shard_map/ppermute | solution.py:255
  21.0 0.0 collective-permute-start.3
  21.0 0.0 collective-permute-done.2.refs_2_
  21.0 3.0 %collective-permute-start.4 = (bf16[7,16,1024]{2,1,0:T(8,128)(2,1)S(1)}, bf16[7,16,1024]{2,1,0:T(8,128)(2,1)S(1)}, u32[]{:S(2)}, u32[]{:S(2)}) collective-permute-start(bf16[7,16,1024]{2,1,0:T(8,128)(2,1)S(1)} %collective-permute-done.2.refs_2_), channel_id=1, source_target_pairs={{0,28},{1,29},{2,30},{3,31},{4,0},{5,1},{6,2},{7,3},{8,4},{9,5},{1... | collective-permute-start | bytes 688136 | tf_op jit(solution)/shard_map/ppermute | solution.py:255
  24.1 5.7 %collective-permute-done.3.refs_3_ = bf16[7,16,1024]{2,1,0:T(8,128)(2,1)S(1)} collective-permute-done((bf16[7,16,1024]{2,1,0:T(8,128)(2,1)S(1)}, bf16[7,16,1024]{2,1,0:T(8,128)(2,1)S(1)}, u32[]{:S(2)}, u32[]{:S(2)}) %collective-permute-start.3) | collective-permute-done | bytes 229408 | tf_op jit(solution)/shard_map/ppermute | solution.py:255
  29.8 2.8 %collective-permute-start.6 = (bf16[7,16,1024]{2,1,0:T(8,128)(2,1)S(1)}, bf16[7,16,1024]{2,1,0:T(8,128)(2,1)S(1)}, u32[]{:S(2)}, u32[]{:S(2)}) collective-permute-start(bf16[7,16,1024]{2,1,0:T(8,128)(2,1)S(1)} %collective-permute-done.4.refs_4_), channel_id=1, source_target_pairs={{0,28},{1,29},{2,30},{3,31},{4,0},{5,1},{6,2},{7,3},{8,4},{9,5},{1... | collective-permute-start | bytes 688136 | tf_op jit(solution)/shard_map/ppermute | solution.py:255
  32.6 0.9 copy-done.3
  33.6 0.6 shard_map.124
  34.1 1.4 collective-permute-start.7
  35.5 1.5 %collective-permute-start.8 = (bf16[2,3,16,1024]{3,2,1,0:T(8,128)(2,1)S(1)}, bf16[2,3,16,1024]{3,2,1,0:T(8,128)(2,1)S(1)}, u32[]{:S(2)}, u32[]{:S(2)}) collective-permute-start(bf16[2,3,16,1024]{3,2,1,0:T(8,128)(2,1)S(1)} %get-tuple-element.32), channel_id=1, source_target_pairs={{0,3},{1,0},{2,1},{3,2},{4,7},{5,4},{6,5},{7,6},{8,11},{9,8},{10,9... | collective-permute-start | bytes 589832 | tf_op jit(solution)/shard_map/ppermute | solution.py:258
  37.0 0.7 collective-permute-done.5.refs_5_
  37.8 3.2 %collective-permute-done.7.refs_2_ = bf16[2,3,16,1024]{3,2,1,0:T(8,128)(2,1)S(1)} collective-permute-done((bf16[2,3,16,1024]{3,2,1,0:T(8,128)(2,1)S(1)}, bf16[2,3,16,1024]{3,2,1,0:T(8,128)(2,1)S(1)}, u32[]{:S(2)}, u32[]{:S(2)}) %collective-permute-start.7) | collective-permute-done | bytes 196640 | tf_op jit(solution)/shard_map/ppermute | solution.py:258
  41.0 0.3 collective-permute-start.10
  41.3 1.1 collective-permute-start.9
  42.5 2.3 %collective-permute-start.14 = (bf16[2,3,16,1024]{3,2,1,0:T(8,128)(2,1)S(1)}, bf16[2,3,16,1024]{3,2,1,0:T(8,128)(2,1)S(1)}, u32[]{:S(2)}, u32[]{:S(2)}) collective-permute-start(bf16[2,3,16,1024]{3,2,1,0:T(8,128)(2,1)S(1)} %get-tuple-element.39), channel_id=1, source_target_pairs={{0,2},{1,3},{2,0},{3,1},{4,6},{5,7},{6,4},{7,5},{8,10},{9,11},{10,... | collective-permute-start | bytes 589832 | tf_op jit(solution)/shard_map/ppermute | solution.py:258
  44.7 1.3 collective-permute-done.9
  46.0 1.2 shard_map.125
  47.2 1.0 collective-permute-start.11
  48.2 2.8 %collective-permute-start.12 = (bf16[2,3,16,1024]{3,2,1,0:T(8,128)(2,1)S(1)}, bf16[2,3,16,1024]{3,2,1,0:T(8,128)(2,1)S(1)}, u32[]{:S(2)}, u32[]{:S(2)}) collective-permute-start(bf16[2,3,16,1024]{3,2,1,0:T(8,128)(2,1)S(1)} %get-tuple-element.37), channel_id=1, source_target_pairs={{0,2},{1,3},{2,0},{3,1},{4,6},{5,7},{6,4},{7,5},{8,10},{9,11},{10,... | collective-permute-start | bytes 589832 | tf_op jit(solution)/shard_map/ppermute | solution.py:258
  51.0 0.6 collective-permute-start.13
  51.6 6.6 %collective-permute-start.16 = (bf16[2,3,32,1024]{3,2,1,0:T(8,128)(2,1)S(1)}, bf16[2,3,32,1024]{3,2,1,0:T(8,128)(2,1)S(1)}, u32[]{:S(2)}, u32[]{:S(2)}) collective-permute-start(bf16[2,3,32,1024]{3,2,1,0:T(8,128)(2,1)S(1)} %get-tuple-element.49), channel_id=1, source_target_pairs={{32,1},{33,2},{34,3},{35,0},{36,5},{37,6},{38,7},{39,4},{40,9},{41... | collective-permute-start | bytes 1179656 | tf_op jit(solution)/shard_map/ppermute | solution.py:258
  58.2 1.9 %collective-permute-start.17 = (bf16[2,3,32,1024]{3,2,1,0:T(8,128)(2,1)S(1)}, bf16[2,3,32,1024]{3,2,1,0:T(8,128)(2,1)S(1)}, u32[]{:S(2)}, u32[]{:S(2)}) collective-permute-start(bf16[2,3,32,1024]{3,2,1,0:T(8,128)(2,1)S(1)} %get-tuple-element.50), channel_id=1, source_target_pairs={{32,2},{33,3},{34,0},{35,1},{36,6},{37,7},{38,4},{39,5},{40,10},{4... | collective-permute-start | bytes 1179656 | tf_op jit(solution)/shard_map/ppermute | solution.py:258
  60.2 1.9 %collective-permute-start.18 = (bf16[2,3,32,1024]{3,2,1,0:T(8,128)(2,1)S(1)}, bf16[2,3,32,1024]{3,2,1,0:T(8,128)(2,1)S(1)}, u32[]{:S(2)}, u32[]{:S(2)}) collective-permute-start(bf16[2,3,32,1024]{3,2,1,0:T(8,128)(2,1)S(1)} %get-tuple-element.51), channel_id=1, source_target_pairs={{32,3},{33,0},{34,1},{35,2},{36,7},{37,4},{38,5},{39,6},{40,11},{4... | collective-permute-start | bytes 1179656 | tf_op jit(solution)/shard_map/ppermute | solution.py:258
  62.1 5.9 %collective-permute-start.15 = (bf16[2,3,32,1024]{3,2,1,0:T(8,128)(2,1)S(1)}, bf16[2,3,32,1024]{3,2,1,0:T(8,128)(2,1)S(1)}, u32[]{:S(2)}, u32[]{:S(2)}) collective-permute-start(bf16[2,3,32,1024]{3,2,1,0:T(8,128)(2,1)S(1)} %get-tuple-element.48), channel_id=1, source_target_pairs={{32,0},{33,1},{34,2},{35,3},{36,4},{37,5},{38,6},{39,7},{40,8},{41... | collective-permute-start | bytes 1179656 | tf_op jit(solution)/shard_map/ppermute | solution.py:258
  68.1 3.5 %collective-permute-done.16.refs_9_ = bf16[2,3,32,1024]{3,2,1,0:T(8,128)(2,1)S(1)} collective-permute-done((bf16[2,3,32,1024]{3,2,1,0:T(8,128)(2,1)S(1)}, bf16[2,3,32,1024]{3,2,1,0:T(8,128)(2,1)S(1)}, u32[]{:S(2)}, u32[]{:S(2)}) %collective-permute-start.16) | collective-permute-done | bytes 393248 | tf_op jit(solution)/shard_map/ppermute | solution.py:258
  71.6 4.2 %collective-permute-done.17.refs_10_ = bf16[2,3,32,1024]{3,2,1,0:T(8,128)(2,1)S(1)} collective-permute-done((bf16[2,3,32,1024]{3,2,1,0:T(8,128)(2,1)S(1)}, bf16[2,3,32,1024]{3,2,1,0:T(8,128)(2,1)S(1)}, u32[]{:S(2)}, u32[]{:S(2)}) %collective-permute-start.17) | collective-permute-done | bytes 393248 | tf_op jit(solution)/shard_map/ppermute | solution.py:258
  75.8 0.8 collective-permute-done.18.refs_11_
  76.6 1.2 collective-permute-done.15.refs_8_
  77.9 7.3 %shard_map.126 = (f32[256,1]{1,0:T(8,128)S(1)}, bf16[32,48,512]{2,1,0:T(8,128)(2,1)}) custom-call(s32[4,256]{1,0:T(4,128)S(1)} %pad_add_fusion.1.slots_ref, bf16[1024,512]{1,0:T(8,128)(2,1)S(1)} %copy-done.5, bf16[2,3,16,1024]{3,2,1,0:T(8,128)(2,1)S(1)} %get-tuple-element.30.refs_0_, bf16[2,3,16,1024]{3,2,1,0:T(8,128)(2,1)S(1)} %get-tuple-element.41.refs_1_, ...), custom_call_target="tpu_custom_call" | custom-call | flops 9663676416 | bytes 9437184 | tf_op jit(solution)/shard_map/pallas_call | solution.py:315
  85.2 8.0 %all-to-all-start = ((bf16[32,48,512]{2,1,0:T(8,128)(2,1)}), bf16[32,48,512]{2,1,0:T(8,128)(2,1)S(1)}, u32[]{:S(2)}, u32[]{:S(2)}) async-start(bf16[32,48,512]{2,1,0:T(8,128)(2,1)} %get-tuple-element.52), calls=%async_computation | async-start | bytes 3145728 | tf_op jit(solution)/shard_map/all_to_all | solution.py:323
  93.2 0.1 copy.15
  93.2 0.1 reshape.13.held_ref
  93.3 0.7 reduce
  94.0 34.9 %all-to-all-done.grad_ref = bf16[32,48,512]{2,1,0:T(8,128)(2,1)S(1)} async-done(((bf16[32,48,512]{2,1,0:T(8,128)(2,1)}), bf16[32,48,512]{2,1,0:T(8,128)(2,1)S(1)}, u32[]{:S(2)}, u32[]{:S(2)}) %all-to-all-start) | async-done | bytes 1572896 | tf_op jit(solution)/shard_map/all_to_all | solution.py:323
  128.9 0.8 shard_map.127
  129.6 10.3 %collective-permute-start.19 = (bf16[48,1024]{1,0:T(8,128)(2,1)S(1)}, bf16[48,1024]{1,0:T(8,128)(2,1)S(1)}, u32[]{:S(2)}, u32[]{:S(2)}) collective-permute-start(bf16[48,1024]{1,0:T(8,128)(2,1)S(1)} %get-tuple-element.56), channel_id=1, source_target_pairs={{0,32},{32,64},{64,96},{96,128},{128,160},{160,192},{192,224},{1,3... | collective-permute-start | bytes 294920 | tf_op jit(solution)/shard_map/ppermute | solution.py:339
  139.9 0.0 copy-start
  139.9 1.6 %copy-done = bf16[4,256,1024]{2,1,0:T(8,128)(2,1)S(1)} copy-done((bf16[4,256,1024]{2,1,0:T(8,128)(2,1)S(1)}, bf16[4,256,1024]{2,1,0:T(8,128)(2,1)}, u32[]{:S(2)}) %copy-start) | copy-done | bytes 2097176
  141.5 0.1 shard_map.128.table_ref
  141.7 1.2 shard_map.129
  (34 shorter events, 0.1 us)
Async XLA Ops:
  0.6 9.0 %copy-start.4 = (s32[32,4]{0,1:T(4,128)S(1)}, s32[32,4]{0,1:T(4,128)}, u32[]{:S(2)}) copy-start(s32[32,4]{0,1:T(4,128)} %param.13) | copy-start | bytes 1540
  0.6 9.0 %collective-permute-start = (s32[4,32]{1,0:T(4,128)}, s32[4,32]{1,0:T(4,128)S(1)}, u32[]{:S(2)}, u32[]{:S(2)}) collective-permute-start(s32[4,32]{1,0:T(4,128)} %bitcast.15), channel_id=1, source_target_pairs={{0,32},{32,64},{64,96},{96,128},{128,160},{160,192},{192,224},{1,3... | collective-permute-start | bytes 1544 | tf_op jit(solution)/shard_map/ppermute | solution.py:260
  5.2 72.7 %copy-start.5 = (bf16[1024,512]{1,0:T(8,128)(2,1)S(1)}, bf16[1024,512]{1,0:T(8,128)(2,1)}, u32[]{:S(2)}) copy-start(bf16[1024,512]{1,0:T(8,128)(2,1)} %constant.12.clone.lag_ref) | copy-start | bytes 3145732
  9.6 0.9 copy-start.1
  10.6 57.5 %copy-start.7 = (s32[256]{0:T(256)S(1)}, s32[256]{0:T(256)}, u32[]{:S(2)}) copy-start(s32[256]{0:T(256)} %param.18) | copy-start | bytes 3076
  10.6 57.5 %copy-start.8 = (s32[256]{0:T(256)S(1)}, s32[256]{0:T(256)}, u32[]{:S(2)}) copy-start(s32[256]{0:T(256)} %param.17) | copy-start | bytes 3076
  10.6 57.5 %copy-start.9 = (s32[256]{0:T(256)S(1)}, s32[256]{0:T(256)}, u32[]{:S(2)}) copy-start(s32[256]{0:T(256)} %param.16) | copy-start | bytes 3076
  10.6 57.5 %copy-start.10 = (s32[256]{0:T(256)S(1)}, s32[256]{0:T(256)}, u32[]{:S(2)}) copy-start(s32[256]{0:T(256)} %param.15) | copy-start | bytes 3076
  10.6 10.4 %collective-permute-start.1 = (bf16[7,16,1024]{2,1,0:T(8,128)(2,1)S(1)}, bf16[7,16,1024]{2,1,0:T(8,128)(2,1)S(1)}, u32[]{:S(2)}, u32[]{:S(2)}) collective-permute-start(bf16[7,16,1024]{2,1,0:T(8,128)(2,1)S(1)} %shard_map.123.refs_0_), channel_id=1, source_target_pairs={{0,4},{1,5},{2,6},{3,7},{4,8},{5,9},{6,10},{7,11},{8,12},{9,13},{1... | collective-permute-start | bytes 688136 | tf_op jit(solution)/shard_map/ppermute | solution.py:255
  12.3 8.7 %collective-permute-start.2 = (bf16[7,16,1024]{2,1,0:T(8,128)(2,1)S(1)}, bf16[7,16,1024]{2,1,0:T(8,128)(2,1)S(1)}, u32[]{:S(2)}, u32[]{:S(2)}) collective-permute-start(bf16[7,16,1024]{2,1,0:T(8,128)(2,1)S(1)} %shard_map.123.refs_0_), channel_id=1, source_target_pairs={{0,28},{1,29},{2,30},{3,31},{4,0},{5,1},{6,2},{7,3},{8,4},{9,5},{1... | collective-permute-start | bytes 688136 | tf_op jit(solution)/shard_map/ppermute | solution.py:255
  16.3 0.7 copy-start.2
  21.0 8.8 %collective-permute-start.3 = (bf16[7,16,1024]{2,1,0:T(8,128)(2,1)S(1)}, bf16[7,16,1024]{2,1,0:T(8,128)(2,1)S(1)}, u32[]{:S(2)}, u32[]{:S(2)}) collective-permute-start(bf16[7,16,1024]{2,1,0:T(8,128)(2,1)S(1)} %collective-permute-done.1.refs_1_), channel_id=1, source_target_pairs={{0,4},{1,5},{2,6},{3,7},{4,8},{5,9},{6,10},{7,11},{8,12},{9,13},{1... | collective-permute-start | bytes 688136 | tf_op jit(solution)/shard_map/ppermute | solution.py:255
  21.0 8.8 %collective-permute-start.4 = (bf16[7,16,1024]{2,1,0:T(8,128)(2,1)S(1)}, bf16[7,16,1024]{2,1,0:T(8,128)(2,1)S(1)}, u32[]{:S(2)}, u32[]{:S(2)}) collective-permute-start(bf16[7,16,1024]{2,1,0:T(8,128)(2,1)S(1)} %collective-permute-done.2.refs_2_), channel_id=1, source_target_pairs={{0,28},{1,29},{2,30},{3,31},{4,0},{5,1},{6,2},{7,3},{8,4},{9,5},{1... | collective-permute-start | bytes 688136 | tf_op jit(solution)/shard_map/ppermute | solution.py:255
  29.8 7.9 %collective-permute-start.5 = (bf16[7,16,1024]{2,1,0:T(8,128)(2,1)S(1)}, bf16[7,16,1024]{2,1,0:T(8,128)(2,1)S(1)}, u32[]{:S(2)}, u32[]{:S(2)}) collective-permute-start(bf16[7,16,1024]{2,1,0:T(8,128)(2,1)S(1)} %collective-permute-done.3.refs_3_), channel_id=1, source_target_pairs={{0,4},{1,5},{2,6},{3,7},{4,8},{5,9},{6,10},{7,11},{8,12},{9,13},{1... | collective-permute-start | bytes 688136 | tf_op jit(solution)/shard_map/ppermute | solution.py:255
  29.8 7.9 %collective-permute-start.6 = (bf16[7,16,1024]{2,1,0:T(8,128)(2,1)S(1)}, bf16[7,16,1024]{2,1,0:T(8,128)(2,1)S(1)}, u32[]{:S(2)}, u32[]{:S(2)}) collective-permute-start(bf16[7,16,1024]{2,1,0:T(8,128)(2,1)S(1)} %collective-permute-done.4.refs_4_), channel_id=1, source_target_pairs={{0,28},{1,29},{2,30},{3,31},{4,0},{5,1},{6,2},{7,3},{8,4},{9,5},{1... | collective-permute-start | bytes 688136 | tf_op jit(solution)/shard_map/ppermute | solution.py:255
  32.6 0.9 copy-start.3
  34.1 6.9 %collective-permute-start.7 = (bf16[2,3,16,1024]{3,2,1,0:T(8,128)(2,1)S(1)}, bf16[2,3,16,1024]{3,2,1,0:T(8,128)(2,1)S(1)}, u32[]{:S(2)}, u32[]{:S(2)}) collective-permute-start(bf16[2,3,16,1024]{3,2,1,0:T(8,128)(2,1)S(1)} %get-tuple-element.31), channel_id=1, source_target_pairs={{0,1},{1,2},{2,3},{3,0},{4,5},{5,6},{6,7},{7,4},{8,9},{9,10},{10,1... | collective-permute-start | bytes 589832 | tf_op jit(solution)/shard_map/ppermute | solution.py:258
  35.5 5.5 %collective-permute-start.8 = (bf16[2,3,16,1024]{3,2,1,0:T(8,128)(2,1)S(1)}, bf16[2,3,16,1024]{3,2,1,0:T(8,128)(2,1)S(1)}, u32[]{:S(2)}, u32[]{:S(2)}) collective-permute-start(bf16[2,3,16,1024]{3,2,1,0:T(8,128)(2,1)S(1)} %get-tuple-element.32), channel_id=1, source_target_pairs={{0,3},{1,0},{2,1},{3,2},{4,7},{5,4},{6,5},{7,6},{8,11},{9,8},{10,9... | collective-permute-start | bytes 589832 | tf_op jit(solution)/shard_map/ppermute | solution.py:258
  41.0 5.0 %collective-permute-start.10 = (bf16[4,16,1024]{2,1,0:T(8,128)(2,1)S(1)}, bf16[4,16,1024]{2,1,0:T(8,128)(2,1)S(1)}, u32[]{:S(2)}, u32[]{:S(2)}) collective-permute-start(bf16[4,16,1024]{2,1,0:T(8,128)(2,1)S(1)} %slice.9), channel_id=1, source_target_pairs={{0,28},{1,29},{2,30},{3,31},{4,0},{5,1},{6,2},{7,3},{8,4},{9,5},{1... | collective-permute-start | bytes 393224 | tf_op jit(solution)/shard_map/ppermute | solution.py:255
  41.3 4.7 %collective-permute-start.9 = (bf16[3,16,1024]{2,1,0:T(8,128)(2,1)S(1)}, bf16[3,16,1024]{2,1,0:T(8,128)(2,1)S(1)}, u32[]{:S(2)}, u32[]{:S(2)}) collective-permute-start(bf16[3,16,1024]{2,1,0:T(8,128)(2,1)S(1)} %slice.8), channel_id=1, source_target_pairs={{0,4},{1,5},{2,6},{3,7},{4,8},{5,9},{6,10},{7,11},{8,12},{9,13},{1... | collective-permute-start | bytes 294920 | tf_op jit(solution)/shard_map/ppermute | solution.py:255
  42.5 15.8 %collective-permute-start.14 = (bf16[2,3,16,1024]{3,2,1,0:T(8,128)(2,1)S(1)}, bf16[2,3,16,1024]{3,2,1,0:T(8,128)(2,1)S(1)}, u32[]{:S(2)}, u32[]{:S(2)}) collective-permute-start(bf16[2,3,16,1024]{3,2,1,0:T(8,128)(2,1)S(1)} %get-tuple-element.39), channel_id=1, source_target_pairs={{0,2},{1,3},{2,0},{3,1},{4,6},{5,7},{6,4},{7,5},{8,10},{9,11},{10,... | collective-permute-start | bytes 589832 | tf_op jit(solution)/shard_map/ppermute | solution.py:258
  47.2 12.9 %collective-permute-start.11 = (bf16[2,3,16,1024]{3,2,1,0:T(8,128)(2,1)S(1)}, bf16[2,3,16,1024]{3,2,1,0:T(8,128)(2,1)S(1)}, u32[]{:S(2)}, u32[]{:S(2)}) collective-permute-start(bf16[2,3,16,1024]{3,2,1,0:T(8,128)(2,1)S(1)} %get-tuple-element.36), channel_id=1, source_target_pairs={{0,1},{1,2},{2,3},{3,0},{4,5},{5,6},{6,7},{7,4},{8,9},{9,10},{10,1... | collective-permute-start | bytes 589832 | tf_op jit(solution)/shard_map/ppermute | solution.py:258
  48.2 13.9 %collective-permute-start.12 = (bf16[2,3,16,1024]{3,2,1,0:T(8,128)(2,1)S(1)}, bf16[2,3,16,1024]{3,2,1,0:T(8,128)(2,1)S(1)}, u32[]{:S(2)}, u32[]{:S(2)}) collective-permute-start(bf16[2,3,16,1024]{3,2,1,0:T(8,128)(2,1)S(1)} %get-tuple-element.37), channel_id=1, source_target_pairs={{0,2},{1,3},{2,0},{3,1},{4,6},{5,7},{6,4},{7,5},{8,10},{9,11},{10,... | collective-permute-start | bytes 589832 | tf_op jit(solution)/shard_map/ppermute | solution.py:258
  51.0 11.1 %collective-permute-start.13 = (bf16[2,3,16,1024]{3,2,1,0:T(8,128)(2,1)S(1)}, bf16[2,3,16,1024]{3,2,1,0:T(8,128)(2,1)S(1)}, u32[]{:S(2)}, u32[]{:S(2)}) collective-permute-start(bf16[2,3,16,1024]{3,2,1,0:T(8,128)(2,1)S(1)} %get-tuple-element.38), channel_id=1, source_target_pairs={{0,3},{1,0},{2,1},{3,2},{4,7},{5,4},{6,5},{7,6},{8,11},{9,8},{10,9... | collective-permute-start | bytes 589832 | tf_op jit(solution)/shard_map/ppermute | solution.py:258
  51.6 20.0 %collective-permute-start.16 = (bf16[2,3,32,1024]{3,2,1,0:T(8,128)(2,1)S(1)}, bf16[2,3,32,1024]{3,2,1,0:T(8,128)(2,1)S(1)}, u32[]{:S(2)}, u32[]{:S(2)}) collective-permute-start(bf16[2,3,32,1024]{3,2,1,0:T(8,128)(2,1)S(1)} %get-tuple-element.49), channel_id=1, source_target_pairs={{32,1},{33,2},{34,3},{35,0},{36,5},{37,6},{38,7},{39,4},{40,9},{41... | collective-permute-start | bytes 1179656 | tf_op jit(solution)/shard_map/ppermute | solution.py:258
  58.2 17.6 %collective-permute-start.17 = (bf16[2,3,32,1024]{3,2,1,0:T(8,128)(2,1)S(1)}, bf16[2,3,32,1024]{3,2,1,0:T(8,128)(2,1)S(1)}, u32[]{:S(2)}, u32[]{:S(2)}) collective-permute-start(bf16[2,3,32,1024]{3,2,1,0:T(8,128)(2,1)S(1)} %get-tuple-element.50), channel_id=1, source_target_pairs={{32,2},{33,3},{34,0},{35,1},{36,6},{37,7},{38,4},{39,5},{40,10},{4... | collective-permute-start | bytes 1179656 | tf_op jit(solution)/shard_map/ppermute | solution.py:258
  60.2 16.4 %collective-permute-start.18 = (bf16[2,3,32,1024]{3,2,1,0:T(8,128)(2,1)S(1)}, bf16[2,3,32,1024]{3,2,1,0:T(8,128)(2,1)S(1)}, u32[]{:S(2)}, u32[]{:S(2)}) collective-permute-start(bf16[2,3,32,1024]{3,2,1,0:T(8,128)(2,1)S(1)} %get-tuple-element.51), channel_id=1, source_target_pairs={{32,3},{33,0},{34,1},{35,2},{36,7},{37,4},{38,5},{39,6},{40,11},{4... | collective-permute-start | bytes 1179656 | tf_op jit(solution)/shard_map/ppermute | solution.py:258
  62.1 15.7 %collective-permute-start.15 = (bf16[2,3,32,1024]{3,2,1,0:T(8,128)(2,1)S(1)}, bf16[2,3,32,1024]{3,2,1,0:T(8,128)(2,1)S(1)}, u32[]{:S(2)}, u32[]{:S(2)}) collective-permute-start(bf16[2,3,32,1024]{3,2,1,0:T(8,128)(2,1)S(1)} %get-tuple-element.48), channel_id=1, source_target_pairs={{32,0},{33,1},{34,2},{35,3},{36,4},{37,5},{38,6},{39,7},{40,8},{41... | collective-permute-start | bytes 1179656 | tf_op jit(solution)/shard_map/ppermute | solution.py:258
  85.2 8.0 %copy-start.6 = (s32[32,4]{0,1:T(4,128)S(1)}, s32[32,4]{0,1:T(4,128)}, u32[]{:S(2)}) copy-start(s32[32,4]{0,1:T(4,128)} %param.14) | copy-start | bytes 1540
  85.2 43.7 %all-to-all-start = ((bf16[32,48,512]{2,1,0:T(8,128)(2,1)}), bf16[32,48,512]{2,1,0:T(8,128)(2,1)S(1)}, u32[]{:S(2)}, u32[]{:S(2)}) async-start(bf16[32,48,512]{2,1,0:T(8,128)(2,1)} %get-tuple-element.52), calls=%async_computation | async-start | bytes 3145728 | tf_op jit(solution)/shard_map/all_to_all | solution.py:323
  129.6 12.0 %collective-permute-start.19 = (bf16[48,1024]{1,0:T(8,128)(2,1)S(1)}, bf16[48,1024]{1,0:T(8,128)(2,1)S(1)}, u32[]{:S(2)}, u32[]{:S(2)}) collective-permute-start(bf16[48,1024]{1,0:T(8,128)(2,1)S(1)} %get-tuple-element.56), channel_id=1, source_target_pairs={{0,32},{32,64},{64,96},{96,128},{128,160},{160,192},{192,224},{1,3... | collective-permute-start | bytes 294920 | tf_op jit(solution)/shard_map/ppermute | solution.py:339
  139.9 1.6 %copy-start = (bf16[4,256,1024]{2,1,0:T(8,128)(2,1)S(1)}, bf16[4,256,1024]{2,1,0:T(8,128)(2,1)}, u32[]{:S(2)}) copy-start(bf16[4,256,1024]{2,1,0:T(8,128)(2,1)} %constant.11.clone.source_ref) | copy-start | bytes 6291460

commit v6 on v5

--- a/solution.py
+++ b/solution.py
@@ -95,15 +95,17 @@
         else:
             real, imag = (r0 - r2) - (i1 - i3), (i0 - i2) + (r1 - r3)
         at = c * group
-        out_ref[:Q, :, at : at + group] = real.astype(BF).reshape(Q, ROWS, group)
-        out_ref[:Q, :, F + at : F + at + group] = imag.astype(BF).reshape(Q, ROWS, group)
+        for q in range(Q):
+            rows, low = slice(q * ROWS, (q + 1) * ROWS), 2 * F * q + at
+            out_ref[:, low : low + group] = real[rows].astype(BF)
+            out_ref[:, F + low : F + low + group] = imag[rows].astype(BF)
 
 
 def index_kernel(near_ref, far_ref, _, out_ref):
     cap, peers = near_ref.shape
     both = jnp.concatenate([near_ref[...], far_ref[...]], 0).astype(F32)
     both = jnp.concatenate([both, jnp.zeros((2 * cap, 4 * peers - peers), F32)], 1)
-    out_ref[Q, :, : 4 * peers] = jnp.concatenate([both, jnp.zeros_like(both)], 0).astype(BF)
+    out_ref[:, Q * 2 * F :] = jnp.concatenate([both, jnp.zeros_like(both)], 0).astype(BF)
 
 
 def fetch_kernel(source_ref, _, out_ref, done):
@@ -145,14 +147,14 @@
         row = iota((YS * count, 1), 0)
         cap, block, step = row % CAP, row // CAP % size, row // count
         expand = (iota((YS * count, wide), 1) == block * ROWS + side * CAP + cap).astype(BF)
-        index = jnp.concatenate([blocks[p][Q, :, : 4 * ZS * YS] for p in ring], 0)
+        index = jnp.concatenate([blocks[p][:, Q * 2 * F :] for p in ring], 0)
         spread = dot(expand, index)
         lane = z * YS + (y + step) % YS
         value = jnp.sum(jnp.where(iota(spread.shape, 1) == lane, spread, 0.0), 1, keepdims=True)
         pick = iota((YS * count, wide), 1) == block * ROWS + value.astype(jnp.int32)
         pick = pick.astype(BF)
         for q in range(Q):
-            got = dot(pick, jnp.concatenate([blocks[p][q] for p in ring], 0)).astype(BF)
+            got = dot(pick, jnp.concatenate([blocks[p][:, 2 * F * q : 2 * F * (q + 1)] for p in ring], 0)).astype(BF)
             for k in range(YS):
                 out[k][q // 3, q % 3] = got[k * count : (k + 1) * count]
 
@@ -261,7 +263,7 @@
     sources = [synthetic.transpose(1, 0, 2), observed.transpose(1, 0, 2)]
     own = pl.pallas_call(
         forward_kernel,
-        out_shape=shape((Q + 1, ROWS, 2 * F)),
+        out_shape=shape((ROWS, Q * 2 * F + 4 * peers)),
         in_specs=[pl.BlockSpec(memory_space=pl.ANY)] * 3,
         out_specs=whole(1)[0],
         scratch_shapes=[
@@ -298,12 +300,12 @@
     up3, down3 = z_move(up2, 1), z_move(down2, -1)
     early = select([(0, EARLY)], dict(zip(EARLY, [own, up, down, up2])))
     early = [early[0]] + [y_move(early[k], k, 0) for k in range(1, YS)]
-    split = Q // 2
-    half_up, half_down = up3[:split], down3[split:]
+    split = Q // 2 * 2 * F
+    half_up, half_down = up3[:, :split], down3[:, split:]
     half_up, half_down, early[1], early[3] = lax.optimization_barrier(
         (half_up, half_down, early[1], early[3])
     )
-    last = jnp.concatenate([z_move(half_up, 1), z_move(half_down, -1)], 0)
+    last = jnp.concatenate([z_move(half_up, 1), z_move(half_down, -1)], 1)
     blocks = dict(enumerate([own, up, down, up2, down2, up3, down3, last]))
     late = select([(0, LATE), (1, EARLY + LATE)], blocks)
     far = list(late[YS:])

time: 143 us -> 142 us (level)
    ppermute x8, waiting for transfers between devices: 11.8 us -> 9.91 us  [z_move(): return lax.ppermute(value, 'dev', z_pairs(step))]
where the time goes in v6:
time: 142 us; the launch traced here: 141 us
  starting transfers between devices  61.4 us (43%)
  waiting for transfers between devices  58.4 us (41%)
  Pallas kernels  15.6 us (11%)
  local copies, waits for them, and re-layouts  4.32 us (3%)
    all_to_all x1, waiting for transfers between devices, on_device(): lax.all_to_all(grads, 'dev', split_axis=0, concat_axis=0, tiled=True)  34.9 us
    ppermute x10, starting transfers between devices, y_move(): return lax.ppermute(value, ('region', 'dev'), y_pairs(step, regions, shift))  25.9 us
    ppermute x10, waiting for transfers between devices, y_move(): return lax.ppermute(value, ('region', 'dev'), y_pairs(step, regions, shift))  13.7 us
    ppermute x8, starting transfers between devices, z_move(): return lax.ppermute(value, 'dev', z_pairs(step))  13.1 us
    ppermute x1, starting transfers between devices, on_device(): lax.ppermute(far_sum, 'region', [(r, r + 1) for r in range(regions - 1)])  9.96 us
    ppermute x8, waiting for transfers between devices, z_move(): return lax.ppermute(value, 'dev', z_pairs(step))  9.91 us
    all_to_all x1, starting transfers between devices, on_device(): lax.all_to_all(grads, 'dev', split_axis=0, concat_axis=0, tiled=True)  8.01 us
    pallas_call x1, Pallas kernels, on_device(): pl.pallas_call(pair_kernel, out_shape=[shape((pairs, 1), F32), shape((pee...  7.27 us
  transfers between devices with their start and end apart: 21, of which 10 were waited for; matrix products, arithmetic and copies ran while one was open for 1% of the time, Pallas kernels for 4%

profile of v6, /device:TPU:1, one launch (start us, length us, event | category | flops | bytes accessed | tf_op | source)
XLA Modules:
  0.0 141.4 jit_solution(13048603383980779956)
XLA Ops:
  0.6 4.5 %collective-permute-start = (s32[4,32]{1,0:T(4,128)}, s32[4,32]{1,0:T(4,128)S(1)}, u32[]{:S(2)}, u32[]{:S(2)}) collective-permute-start(s32[4,32]{1,0:T(4,128)} %bitcast.15), channel_id=1, source_target_pairs={{0,32},{32,64},{64,96},{96,128},{128,160},{160,192},{192,224},{1,3... | collective-permute-start | bytes 1544 | tf_op jit(solution)/shard_map/ppermute | solution.py:262
  5.2 0.0 copy-start.5
  5.2 4.4 %shard_map.122._ = bf16[16,6272]{1,0:T(8,128)(2,1)} custom-call(bf16[3,16,4096]{2,1,0:T(8,128)(2,1)} %bitcast.12, bf16[3,16,4096]{2,1,0:T(8,128)(2,1)} %bitcast.13, bf16[4,1024,256]{2,1,0:T(8,128)(2,1)} %constant.10.clone.far_table_ref), custom_call_target="tpu_custom_call" | custom-call | flops 805306368 | bytes 3145728 | tf_op jit(solution)/shard_map/pallas_call | solution.py:264
  9.6 0.0 collective-permute-done.far_ref
  9.6 0.0 copy-start.1
  9.6 0.9 copy-done.1
  10.6 1.7 %collective-permute-start.1 = (bf16[16,6272]{1,0:T(8,128)(2,1)S(1)}, bf16[16,6272]{1,0:T(8,128)(2,1)S(1)}, u32[]{:S(2)}, u32[]{:S(2)}) collective-permute-start(bf16[16,6272]{1,0:T(8,128)(2,1)S(1)} %shard_map.123.refs_0_), channel_id=1, source_target_pairs={{0,4},{1,5},{2,6},{3,7},{4,8},{5,9},{6,10},{7,11},{8,12},{9,13},{1... | collective-permute-start | bytes 602120 | tf_op jit(solution)/shard_map/ppermute | solution.py:257
  12.3 4.0 %collective-permute-start.2 = (bf16[16,6272]{1,0:T(8,128)(2,1)S(1)}, bf16[16,6272]{1,0:T(8,128)(2,1)S(1)}, u32[]{:S(2)}, u32[]{:S(2)}) collective-permute-start(bf16[16,6272]{1,0:T(8,128)(2,1)S(1)} %shard_map.123.refs_0_), channel_id=1, source_target_pairs={{0,28},{1,29},{2,30},{3,31},{4,0},{5,1},{6,2},{7,3},{8,4},{9,5},{1... | collective-permute-start | bytes 602120 | tf_op jit(solution)/shard_map/ppermute | solution.py:257
  16.3 0.7 copy-done.2
  17.0 3.4 %collective-permute-done.1.refs_1_ = bf16[16,6272]{1,0:T(8,128)(2,1)S(1)} collective-permute-done((bf16[16,6272]{1,0:T(8,128)(2,1)S(1)}, bf16[16,6272]{1,0:T(8,128)(2,1)S(1)}, u32[]{:S(2)}, u32[]{:S(2)}) %collective-permute-start.1) | collective-permute-done | bytes 200736 | tf_op jit(solution)/shard_map/ppermute | solution.py:257
  20.4 3.0 %collective-permute-start.4 = (bf16[16,6272]{1,0:T(8,128)(2,1)S(1)}, bf16[16,6272]{1,0:T(8,128)(2,1)S(1)}, u32[]{:S(2)}, u32[]{:S(2)}) collective-permute-start(bf16[16,6272]{1,0:T(8,128)(2,1)S(1)} %collective-permute-done.2.refs_2_), channel_id=1, source_target_pairs={{0,28},{1,29},{2,30},{3,31},{4,0},{5,1},{6,2},{7,3},{8,4},{9,5},{1... | collective-permute-start | bytes 602120 | tf_op jit(solution)/shard_map/ppermute | solution.py:257
  23.4 5.1 %collective-permute-done.3.refs_3_ = bf16[16,6272]{1,0:T(8,128)(2,1)S(1)} collective-permute-done((bf16[16,6272]{1,0:T(8,128)(2,1)S(1)}, bf16[16,6272]{1,0:T(8,128)(2,1)S(1)}, u32[]{:S(2)}, u32[]{:S(2)}) %collective-permute-start.3) | collective-permute-done | bytes 200736 | tf_op jit(solution)/shard_map/ppermute | solution.py:257
  28.6 0.0 collective-permute-start.5
  28.6 2.8 %collective-permute-start.6 = (bf16[16,6272]{1,0:T(8,128)(2,1)S(1)}, bf16[16,6272]{1,0:T(8,128)(2,1)S(1)}, u32[]{:S(2)}, u32[]{:S(2)}) collective-permute-start(bf16[16,6272]{1,0:T(8,128)(2,1)S(1)} %collective-permute-done.4.refs_4_), channel_id=1, source_target_pairs={{0,28},{1,29},{2,30},{3,31},{4,0},{5,1},{6,2},{7,3},{8,4},{9,5},{1... | collective-permute-start | bytes 602120 | tf_op jit(solution)/shard_map/ppermute | solution.py:257
  31.4 0.9 copy-done.3
  32.3 0.5 shard_map.124
  32.9 1.4 collective-permute-start.7
  34.2 1.5 %collective-permute-start.8 = (bf16[2,3,16,1024]{3,2,1,0:T(8,128)(2,1)S(1)}, bf16[2,3,16,1024]{3,2,1,0:T(8,128)(2,1)S(1)}, u32[]{:S(2)}, u32[]{:S(2)}) collective-permute-start(bf16[2,3,16,1024]{3,2,1,0:T(8,128)(2,1)S(1)} %get-tuple-element.32), channel_id=1, source_target_pairs={{0,3},{1,0},{2,1},{3,2},{4,7},{5,4},{6,5},{7,6},{8,11},{9,8},{10,9... | collective-permute-start | bytes 589832 | tf_op jit(solution)/shard_map/ppermute | solution.py:260
  35.8 0.1 collective-permute-done.5.refs_5_
  35.9 3.8 %collective-permute-done.7.refs_2_ = bf16[2,3,16,1024]{3,2,1,0:T(8,128)(2,1)S(1)} collective-permute-done((bf16[2,3,16,1024]{3,2,1,0:T(8,128)(2,1)S(1)}, bf16[2,3,16,1024]{3,2,1,0:T(8,128)(2,1)S(1)}, u32[]{:S(2)}, u32[]{:S(2)}) %collective-permute-start.7) | collective-permute-done | bytes 196640 | tf_op jit(solution)/shard_map/ppermute | solution.py:260
  39.7 0.3 collective-permute-start.10
  40.0 1.2 collective-permute-start.9
  41.2 2.3 %collective-permute-start.14 = (bf16[2,3,16,1024]{3,2,1,0:T(8,128)(2,1)S(1)}, bf16[2,3,16,1024]{3,2,1,0:T(8,128)(2,1)S(1)}, u32[]{:S(2)}, u32[]{:S(2)}) collective-permute-start(bf16[2,3,16,1024]{3,2,1,0:T(8,128)(2,1)S(1)} %get-tuple-element.39), channel_id=1, source_target_pairs={{0,2},{1,3},{2,0},{3,1},{4,6},{5,7},{6,4},{7,5},{8,10},{9,11},{10,... | collective-permute-start | bytes 589832 | tf_op jit(solution)/shard_map/ppermute | solution.py:260
  43.5 1.2 collective-permute-done.9
  44.7 1.2 shard_map.125
  45.9 1.0 collective-permute-start.11
  46.9 2.8 %collective-permute-start.12 = (bf16[2,3,16,1024]{3,2,1,0:T(8,128)(2,1)S(1)}, bf16[2,3,16,1024]{3,2,1,0:T(8,128)(2,1)S(1)}, u32[]{:S(2)}, u32[]{:S(2)}) collective-permute-start(bf16[2,3,16,1024]{3,2,1,0:T(8,128)(2,1)S(1)} %get-tuple-element.37), channel_id=1, source_target_pairs={{0,2},{1,3},{2,0},{3,1},{4,6},{5,7},{6,4},{7,5},{8,10},{9,11},{10,... | collective-permute-start | bytes 589832 | tf_op jit(solution)/shard_map/ppermute | solution.py:260
  49.7 0.6 collective-permute-start.13
  50.3 6.6 %collective-permute-start.16 = (bf16[2,3,32,1024]{3,2,1,0:T(8,128)(2,1)S(1)}, bf16[2,3,32,1024]{3,2,1,0:T(8,128)(2,1)S(1)}, u32[]{:S(2)}, u32[]{:S(2)}) collective-permute-start(bf16[2,3,32,1024]{3,2,1,0:T(8,128)(2,1)S(1)} %get-tuple-element.49), channel_id=1, source_target_pairs={{32,1},{33,2},{34,3},{35,0},{36,5},{37,6},{38,7},{39,4},{40,9},{41... | collective-permute-start | bytes 1179656 | tf_op jit(solution)/shard_map/ppermute | solution.py:260
  57.0 1.9 %collective-permute-start.17 = (bf16[2,3,32,1024]{3,2,1,0:T(8,128)(2,1)S(1)}, bf16[2,3,32,1024]{3,2,1,0:T(8,128)(2,1)S(1)}, u32[]{:S(2)}, u32[]{:S(2)}) collective-permute-start(bf16[2,3,32,1024]{3,2,1,0:T(8,128)(2,1)S(1)} %get-tuple-element.50), channel_id=1, source_target_pairs={{32,2},{33,3},{34,0},{35,1},{36,6},{37,7},{38,4},{39,5},{40,10},{4... | collective-permute-start | bytes 1179656 | tf_op jit(solution)/shard_map/ppermute | solution.py:260
  58.9 1.9 %collective-permute-start.18 = (bf16[2,3,32,1024]{3,2,1,0:T(8,128)(2,1)S(1)}, bf16[2,3,32,1024]{3,2,1,0:T(8,128)(2,1)S(1)}, u32[]{:S(2)}, u32[]{:S(2)}) collective-permute-start(bf16[2,3,32,1024]{3,2,1,0:T(8,128)(2,1)S(1)} %get-tuple-element.51), channel_id=1, source_target_pairs={{32,3},{33,0},{34,1},{35,2},{36,7},{37,4},{38,5},{39,6},{40,11},{4... | collective-permute-start | bytes 1179656 | tf_op jit(solution)/shard_map/ppermute | solution.py:260
  60.9 5.8 %collective-permute-start.15 = (bf16[2,3,32,1024]{3,2,1,0:T(8,128)(2,1)S(1)}, bf16[2,3,32,1024]{3,2,1,0:T(8,128)(2,1)S(1)}, u32[]{:S(2)}, u32[]{:S(2)}) collective-permute-start(bf16[2,3,32,1024]{3,2,1,0:T(8,128)(2,1)S(1)} %get-tuple-element.48), channel_id=1, source_target_pairs={{32,0},{33,1},{34,2},{35,3},{36,4},{37,5},{38,6},{39,7},{40,8},{41... | collective-permute-start | bytes 1179656 | tf_op jit(solution)/shard_map/ppermute | solution.py:260
  66.7 3.6 %collective-permute-done.16.refs_9_ = bf16[2,3,32,1024]{3,2,1,0:T(8,128)(2,1)S(1)} collective-permute-done((bf16[2,3,32,1024]{3,2,1,0:T(8,128)(2,1)S(1)}, bf16[2,3,32,1024]{3,2,1,0:T(8,128)(2,1)S(1)}, u32[]{:S(2)}, u32[]{:S(2)}) %collective-permute-start.16) | collective-permute-done | bytes 393248 | tf_op jit(solution)/shard_map/ppermute | solution.py:260
  70.3 4.2 %collective-permute-done.17.refs_10_ = bf16[2,3,32,1024]{3,2,1,0:T(8,128)(2,1)S(1)} collective-permute-done((bf16[2,3,32,1024]{3,2,1,0:T(8,128)(2,1)S(1)}, bf16[2,3,32,1024]{3,2,1,0:T(8,128)(2,1)S(1)}, u32[]{:S(2)}, u32[]{:S(2)}) %collective-permute-start.17) | collective-permute-done | bytes 393248 | tf_op jit(solution)/shard_map/ppermute | solution.py:260
  74.6 0.8 collective-permute-done.18.refs_11_
  75.4 1.2 collective-permute-done.15.refs_8_
  76.6 7.3 %shard_map.126 = (f32[256,1]{1,0:T(8,128)S(1)}, bf16[32,48,512]{2,1,0:T(8,128)(2,1)}) custom-call(s32[4,256]{1,0:T(4,128)S(1)} %pad_add_fusion.1.slots_ref, bf16[1024,512]{1,0:T(8,128)(2,1)S(1)} %copy-done.5, bf16[2,3,16,1024]{3,2,1,0:T(8,128)(2,1)S(1)} %get-tuple-element.30.refs_0_, bf16[2,3,16,1024]{3,2,1,0:T(8,128)(2,1)S(1)} %get-tuple-element.41.refs_1_, ...), custom_call_target="tpu_custom_call" | custom-call | flops 9663676416 | bytes 9437184 | tf_op jit(solution)/shard_map/pallas_call | solution.py:317
  83.9 8.0 %all-to-all-start = ((bf16[32,48,512]{2,1,0:T(8,128)(2,1)}), bf16[32,48,512]{2,1,0:T(8,128)(2,1)S(1)}, u32[]{:S(2)}, u32[]{:S(2)}) async-start(bf16[32,48,512]{2,1,0:T(8,128)(2,1)} %get-tuple-element.52), calls=%async_computation | async-start | bytes 3145728 | tf_op jit(solution)/shard_map/all_to_all | solution.py:325
  91.9 0.1 copy.15
  92.0 0.1 reshape.13.held_ref
  92.1 0.7 reduce
  92.8 34.9 %all-to-all-done.grad_ref = bf16[32,48,512]{2,1,0:T(8,128)(2,1)S(1)} async-done(((bf16[32,48,512]{2,1,0:T(8,128)(2,1)}), bf16[32,48,512]{2,1,0:T(8,128)(2,1)S(1)}, u32[]{:S(2)}, u32[]{:S(2)}) %all-to-all-start) | async-done | bytes 1572896 | tf_op jit(solution)/shard_map/all_to_all | solution.py:325
  127.6 0.8 shard_map.127
  128.4 10.0 %collective-permute-start.19 = (bf16[48,1024]{1,0:T(8,128)(2,1)S(1)}, bf16[48,1024]{1,0:T(8,128)(2,1)S(1)}, u32[]{:S(2)}, u32[]{:S(2)}) collective-permute-start(bf16[48,1024]{1,0:T(8,128)(2,1)S(1)} %get-tuple-element.56), channel_id=1, source_target_pairs={{0,32},{32,64},{64,96},{96,128},{128,160},{160,192},{192,224},{1,3... | collective-permute-start | bytes 294920 | tf_op jit(solution)/shard_map/ppermute | solution.py:341
  138.4 0.0 copy-start
  138.4 1.6 %copy-done = bf16[4,256,1024]{2,1,0:T(8,128)(2,1)S(1)} copy-done((bf16[4,256,1024]{2,1,0:T(8,128)(2,1)S(1)}, bf16[4,256,1024]{2,1,0:T(8,128)(2,1)}, u32[]{:S(2)}) %copy-start) | copy-done | bytes 2097176
  140.0 0.1 shard_map.128.table_ref
  140.1 1.2 shard_map.129
  (34 shorter events, 0.1 us)
Async XLA Ops:
  0.6 9.0 %copy-start.4 = (s32[32,4]{0,1:T(4,128)S(1)}, s32[32,4]{0,1:T(4,128)}, u32[]{:S(2)}) copy-start(s32[32,4]{0,1:T(4,128)} %param.13) | copy-start | bytes 1540
  0.6 9.0 %collective-permute-start = (s32[4,32]{1,0:T(4,128)}, s32[4,32]{1,0:T(4,128)S(1)}, u32[]{:S(2)}, u32[]{:S(2)}) collective-permute-start(s32[4,32]{1,0:T(4,128)} %bitcast.15), channel_id=1, source_target_pairs={{0,32},{32,64},{64,96},{96,128},{128,160},{160,192},{192,224},{1,3... | collective-permute-start | bytes 1544 | tf_op jit(solution)/shard_map/ppermute | solution.py:262
  5.2 71.4 %copy-start.5 = (bf16[1024,512]{1,0:T(8,128)(2,1)S(1)}, bf16[1024,512]{1,0:T(8,128)(2,1)}, u32[]{:S(2)}) copy-start(bf16[1024,512]{1,0:T(8,128)(2,1)} %constant.12.clone.lag_ref) | copy-start | bytes 3145732
  9.6 0.9 copy-start.1
  10.5 56.1 %copy-start.7 = (s32[256]{0:T(256)S(1)}, s32[256]{0:T(256)}, u32[]{:S(2)}) copy-start(s32[256]{0:T(256)} %param.18) | copy-start | bytes 3076
  10.5 56.1 %copy-start.8 = (s32[256]{0:T(256)S(1)}, s32[256]{0:T(256)}, u32[]{:S(2)}) copy-start(s32[256]{0:T(256)} %param.17) | copy-start | bytes 3076
  10.6 56.2 %copy-start.9 = (s32[256]{0:T(256)S(1)}, s32[256]{0:T(256)}, u32[]{:S(2)}) copy-start(s32[256]{0:T(256)} %param.16) | copy-start | bytes 3076
  10.6 56.2 %copy-start.10 = (s32[256]{0:T(256)S(1)}, s32[256]{0:T(256)}, u32[]{:S(2)}) copy-start(s32[256]{0:T(256)} %param.15) | copy-start | bytes 3076
  10.6 9.8 %collective-permute-start.1 = (bf16[16,6272]{1,0:T(8,128)(2,1)S(1)}, bf16[16,6272]{1,0:T(8,128)(2,1)S(1)}, u32[]{:S(2)}, u32[]{:S(2)}) collective-permute-start(bf16[16,6272]{1,0:T(8,128)(2,1)S(1)} %shard_map.123.refs_0_), channel_id=1, source_target_pairs={{0,4},{1,5},{2,6},{3,7},{4,8},{5,9},{6,10},{7,11},{8,12},{9,13},{1... | collective-permute-start | bytes 602120 | tf_op jit(solution)/shard_map/ppermute | solution.py:257
  12.3 8.1 %collective-permute-start.2 = (bf16[16,6272]{1,0:T(8,128)(2,1)S(1)}, bf16[16,6272]{1,0:T(8,128)(2,1)S(1)}, u32[]{:S(2)}, u32[]{:S(2)}) collective-permute-start(bf16[16,6272]{1,0:T(8,128)(2,1)S(1)} %shard_map.123.refs_0_), channel_id=1, source_target_pairs={{0,28},{1,29},{2,30},{3,31},{4,0},{5,1},{6,2},{7,3},{8,4},{9,5},{1... | collective-permute-start | bytes 602120 | tf_op jit(solution)/shard_map/ppermute | solution.py:257
  16.3 0.7 copy-start.2
  20.4 8.2 %collective-permute-start.3 = (bf16[16,6272]{1,0:T(8,128)(2,1)S(1)}, bf16[16,6272]{1,0:T(8,128)(2,1)S(1)}, u32[]{:S(2)}, u32[]{:S(2)}) collective-permute-start(bf16[16,6272]{1,0:T(8,128)(2,1)S(1)} %collective-permute-done.1.refs_1_), channel_id=1, source_target_pairs={{0,4},{1,5},{2,6},{3,7},{4,8},{5,9},{6,10},{7,11},{8,12},{9,13},{1... | collective-permute-start | bytes 602120 | tf_op jit(solution)/shard_map/ppermute | solution.py:257
  20.4 8.2 %collective-permute-start.4 = (bf16[16,6272]{1,0:T(8,128)(2,1)S(1)}, bf16[16,6272]{1,0:T(8,128)(2,1)S(1)}, u32[]{:S(2)}, u32[]{:S(2)}) collective-permute-start(bf16[16,6272]{1,0:T(8,128)(2,1)S(1)} %collective-permute-done.2.refs_2_), channel_id=1, source_target_pairs={{0,28},{1,29},{2,30},{3,31},{4,0},{5,1},{6,2},{7,3},{8,4},{9,5},{1... | collective-permute-start | bytes 602120 | tf_op jit(solution)/shard_map/ppermute | solution.py:257
  28.6 7.3 %collective-permute-start.5 = (bf16[16,6272]{1,0:T(8,128)(2,1)S(1)}, bf16[16,6272]{1,0:T(8,128)(2,1)S(1)}, u32[]{:S(2)}, u32[]{:S(2)}) collective-permute-start(bf16[16,6272]{1,0:T(8,128)(2,1)S(1)} %collective-permute-done.3.refs_3_), channel_id=1, source_target_pairs={{0,4},{1,5},{2,6},{3,7},{4,8},{5,9},{6,10},{7,11},{8,12},{9,13},{1... | collective-permute-start | bytes 602120 | tf_op jit(solution)/shard_map/ppermute | solution.py:257
  28.6 7.3 %collective-permute-start.6 = (bf16[16,6272]{1,0:T(8,128)(2,1)S(1)}, bf16[16,6272]{1,0:T(8,128)(2,1)S(1)}, u32[]{:S(2)}, u32[]{:S(2)}) collective-permute-start(bf16[16,6272]{1,0:T(8,128)(2,1)S(1)} %collective-permute-done.4.refs_4_), channel_id=1, source_target_pairs={{0,28},{1,29},{2,30},{3,31},{4,0},{5,1},{6,2},{7,3},{8,4},{9,5},{1... | collective-permute-start | bytes 602120 | tf_op jit(solution)/shard_map/ppermute | solution.py:257
  31.4 0.9 copy-start.3
  32.9 6.9 %collective-permute-start.7 = (bf16[2,3,16,1024]{3,2,1,0:T(8,128)(2,1)S(1)}, bf16[2,3,16,1024]{3,2,1,0:T(8,128)(2,1)S(1)}, u32[]{:S(2)}, u32[]{:S(2)}) collective-permute-start(bf16[2,3,16,1024]{3,2,1,0:T(8,128)(2,1)S(1)} %get-tuple-element.31), channel_id=1, source_target_pairs={{0,1},{1,2},{2,3},{3,0},{4,5},{5,6},{6,7},{7,4},{8,9},{9,10},{10,1... | collective-permute-start | bytes 589832 | tf_op jit(solution)/shard_map/ppermute | solution.py:260
  34.2 5.5 %collective-permute-start.8 = (bf16[2,3,16,1024]{3,2,1,0:T(8,128)(2,1)S(1)}, bf16[2,3,16,1024]{3,2,1,0:T(8,128)(2,1)S(1)}, u32[]{:S(2)}, u32[]{:S(2)}) collective-permute-start(bf16[2,3,16,1024]{3,2,1,0:T(8,128)(2,1)S(1)} %get-tuple-element.32), channel_id=1, source_target_pairs={{0,3},{1,0},{2,1},{3,2},{4,7},{5,4},{6,5},{7,6},{8,11},{9,8},{10,9... | collective-permute-start | bytes 589832 | tf_op jit(solution)/shard_map/ppermute | solution.py:260
  39.7 5.0 %collective-permute-start.10 = (bf16[16,3200]{1,0:T(8,128)(2,1)S(1)}, bf16[16,3200]{1,0:T(8,128)(2,1)S(1)}, u32[]{:S(2)}, u32[]{:S(2)}) collective-permute-start(bf16[16,3200]{1,0:T(8,128)(2,1)S(1)} %slice.9), channel_id=1, source_target_pairs={{0,28},{1,29},{2,30},{3,31},{4,0},{5,1},{6,2},{7,3},{8,4},{9,5},{1... | collective-permute-start | bytes 307208 | tf_op jit(solution)/shard_map/ppermute | solution.py:257
  40.0 4.7 %collective-permute-start.9 = (bf16[16,3072]{1,0:T(8,128)(2,1)S(1)}, bf16[16,3072]{1,0:T(8,128)(2,1)S(1)}, u32[]{:S(2)}, u32[]{:S(2)}) collective-permute-start(bf16[16,3072]{1,0:T(8,128)(2,1)S(1)} %slice.8), channel_id=1, source_target_pairs={{0,4},{1,5},{2,6},{3,7},{4,8},{5,9},{6,10},{7,11},{8,12},{9,13},{1... | collective-permute-start | bytes 294920 | tf_op jit(solution)/shard_map/ppermute | solution.py:257
  41.2 15.8 %collective-permute-start.14 = (bf16[2,3,16,1024]{3,2,1,0:T(8,128)(2,1)S(1)}, bf16[2,3,16,1024]{3,2,1,0:T(8,128)(2,1)S(1)}, u32[]{:S(2)}, u32[]{:S(2)}) collective-permute-start(bf16[2,3,16,1024]{3,2,1,0:T(8,128)(2,1)S(1)} %get-tuple-element.39), channel_id=1, source_target_pairs={{0,2},{1,3},{2,0},{3,1},{4,6},{5,7},{6,4},{7,5},{8,10},{9,11},{10,... | collective-permute-start | bytes 589832 | tf_op jit(solution)/shard_map/ppermute | solution.py:260
  45.9 13.0 %collective-permute-start.11 = (bf16[2,3,16,1024]{3,2,1,0:T(8,128)(2,1)S(1)}, bf16[2,3,16,1024]{3,2,1,0:T(8,128)(2,1)S(1)}, u32[]{:S(2)}, u32[]{:S(2)}) collective-permute-start(bf16[2,3,16,1024]{3,2,1,0:T(8,128)(2,1)S(1)} %get-tuple-element.36), channel_id=1, source_target_pairs={{0,1},{1,2},{2,3},{3,0},{4,5},{5,6},{6,7},{7,4},{8,9},{9,10},{10,1... | collective-permute-start | bytes 589832 | tf_op jit(solution)/shard_map/ppermute | solution.py:260
  46.9 13.9 %collective-permute-start.12 = (bf16[2,3,16,1024]{3,2,1,0:T(8,128)(2,1)S(1)}, bf16[2,3,16,1024]{3,2,1,0:T(8,128)(2,1)S(1)}, u32[]{:S(2)}, u32[]{:S(2)}) collective-permute-start(bf16[2,3,16,1024]{3,2,1,0:T(8,128)(2,1)S(1)} %get-tuple-element.37), channel_id=1, source_target_pairs={{0,2},{1,3},{2,0},{3,1},{4,6},{5,7},{6,4},{7,5},{8,10},{9,11},{10,... | collective-permute-start | bytes 589832 | tf_op jit(solution)/shard_map/ppermute | solution.py:260
  49.7 11.2 %collective-permute-start.13 = (bf16[2,3,16,1024]{3,2,1,0:T(8,128)(2,1)S(1)}, bf16[2,3,16,1024]{3,2,1,0:T(8,128)(2,1)S(1)}, u32[]{:S(2)}, u32[]{:S(2)}) collective-permute-start(bf16[2,3,16,1024]{3,2,1,0:T(8,128)(2,1)S(1)} %get-tuple-element.38), channel_id=1, source_target_pairs={{0,3},{1,0},{2,1},{3,2},{4,7},{5,4},{6,5},{7,6},{8,11},{9,8},{10,9... | collective-permute-start | bytes 589832 | tf_op jit(solution)/shard_map/ppermute | solution.py:260
  50.3 20.0 %collective-permute-start.16 = (bf16[2,3,32,1024]{3,2,1,0:T(8,128)(2,1)S(1)}, bf16[2,3,32,1024]{3,2,1,0:T(8,128)(2,1)S(1)}, u32[]{:S(2)}, u32[]{:S(2)}) collective-permute-start(bf16[2,3,32,1024]{3,2,1,0:T(8,128)(2,1)S(1)} %get-tuple-element.49), channel_id=1, source_target_pairs={{32,1},{33,2},{34,3},{35,0},{36,5},{37,6},{38,7},{39,4},{40,9},{41... | collective-permute-start | bytes 1179656 | tf_op jit(solution)/shard_map/ppermute | solution.py:260
  57.0 17.6 %collective-permute-start.17 = (bf16[2,3,32,1024]{3,2,1,0:T(8,128)(2,1)S(1)}, bf16[2,3,32,1024]{3,2,1,0:T(8,128)(2,1)S(1)}, u32[]{:S(2)}, u32[]{:S(2)}) collective-permute-start(bf16[2,3,32,1024]{3,2,1,0:T(8,128)(2,1)S(1)} %get-tuple-element.50), channel_id=1, source_target_pairs={{32,2},{33,3},{34,0},{35,1},{36,6},{37,7},{38,4},{39,5},{40,10},{4... | collective-permute-start | bytes 1179656 | tf_op jit(solution)/shard_map/ppermute | solution.py:260
  58.9 16.4 %collective-permute-start.18 = (bf16[2,3,32,1024]{3,2,1,0:T(8,128)(2,1)S(1)}, bf16[2,3,32,1024]{3,2,1,0:T(8,128)(2,1)S(1)}, u32[]{:S(2)}, u32[]{:S(2)}) collective-permute-start(bf16[2,3,32,1024]{3,2,1,0:T(8,128)(2,1)S(1)} %get-tuple-element.51), channel_id=1, source_target_pairs={{32,3},{33,0},{34,1},{35,2},{36,7},{37,4},{38,5},{39,6},{40,11},{4... | collective-permute-start | bytes 1179656 | tf_op jit(solution)/shard_map/ppermute | solution.py:260
  60.9 15.7 %collective-permute-start.15 = (bf16[2,3,32,1024]{3,2,1,0:T(8,128)(2,1)S(1)}, bf16[2,3,32,1024]{3,2,1,0:T(8,128)(2,1)S(1)}, u32[]{:S(2)}, u32[]{:S(2)}) collective-permute-start(bf16[2,3,32,1024]{3,2,1,0:T(8,128)(2,1)S(1)} %get-tuple-element.48), channel_id=1, source_target_pairs={{32,0},{33,1},{34,2},{35,3},{36,4},{37,5},{38,6},{39,7},{40,8},{41... | collective-permute-start | bytes 1179656 | tf_op jit(solution)/shard_map/ppermute | solution.py:260
  83.9 8.0 %copy-start.6 = (s32[32,4]{0,1:T(4,128)S(1)}, s32[32,4]{0,1:T(4,128)}, u32[]{:S(2)}) copy-start(s32[32,4]{0,1:T(4,128)} %param.14) | copy-start | bytes 1540
  83.9 43.8 %all-to-all-start = ((bf16[32,48,512]{2,1,0:T(8,128)(2,1)}), bf16[32,48,512]{2,1,0:T(8,128)(2,1)S(1)}, u32[]{:S(2)}, u32[]{:S(2)}) async-start(bf16[32,48,512]{2,1,0:T(8,128)(2,1)} %get-tuple-element.52), calls=%async_computation | async-start | bytes 3145728 | tf_op jit(solution)/shard_map/all_to_all | solution.py:325
  128.4 11.7 %collective-permute-start.19 = (bf16[48,1024]{1,0:T(8,128)(2,1)S(1)}, bf16[48,1024]{1,0:T(8,128)(2,1)S(1)}, u32[]{:S(2)}, u32[]{:S(2)}) collective-permute-start(bf16[48,1024]{1,0:T(8,128)(2,1)S(1)} %get-tuple-element.56), channel_id=1, source_target_pairs={{0,32},{32,64},{64,96},{96,128},{128,160},{160,192},{192,224},{1,3... | collective-permute-start | bytes 294920 | tf_op jit(solution)/shard_map/ppermute | solution.py:341
  138.4 1.6 %copy-start = (bf16[4,256,1024]{2,1,0:T(8,128)(2,1)S(1)}, bf16[4,256,1024]{2,1,0:T(8,128)(2,1)}, u32[]{:S(2)}) copy-start(bf16[4,256,1024]{2,1,0:T(8,128)(2,1)} %constant.11.clone.source_ref) | copy-start | bytes 6291460
